TPU v7x, 32 devices: a whole 2x2x4 slice. The times are simulated.
32 devices in a mesh: groups: 2 (over x), tp: 8 (over z, y), sub: 2 (over core).
Axes of the slice: x: 2, y: 2, z: 4, core: 2. Of those that a mesh axis runs over, the one named last changes fastest.
Arguments:
- tokens: bfloat16 [2, 32, 16384], P(None, 'groups', ('tp', 'sub')), parts along dimension 1, may hold values from -6 to 6
- query_weight: bfloat16 [16384, 8192], P(None, ('tp', 'sub')), may hold values from -0.125 to 0.125
- key_value_weight: bfloat16 [16384, 1024], P(('tp', 'sub')), may hold values from -0.046875 to 0.046875
- output_weight: bfloat16 [8192, 16384], P(('tp', 'sub')), may hold values from -0.09375 to 0.09375
- cached_rotated_keys: bfloat16 [32, 512, 512], P(('groups', 'tp', 'sub')), parts along dimension 0, may hold values from -800 to 800, as said below
- cached_values: bfloat16 [32, 512, 512], P(('groups', 'tp', 'sub')), parts along dimension 0, may hold values from -6 to 6
- lengths: int32 [32], P(('groups', 'tp', 'sub')), parts along dimension 0, may hold values from 128 to 512, as said below
- request_adapter: int32 [32], P('groups'), parts along dimension 0, may hold values from 0 to 15
- adapter_pool_slot: int32 [16], replicated, may hold values from 0 to 15, each once
- adapter_down_maps: bfloat16 [16, 48, 16384], P(('tp', 'sub')), may hold values from -0.046875 to 0.046875
- query_up_maps: bfloat16 [16, 16, 8192], P(('tp', 'sub')), may hold values from -1.5 to 1.5
- key_up_maps: bfloat16 [16, 16, 512], P(('tp', 'sub')), may hold values from -1.5 to 1.5
- value_up_maps: bfloat16 [16, 16, 512], P(('tp', 'sub')), may hold values from -1.5 to 1.5
- result_lowering_factors: bfloat16 [16, 16, 8192], P(('tp', 'sub')), may hold values from -0.0625 to 0.0625
- output_up_maps: bfloat16 [16, 16, 16384], P(('tp', 'sub')), may hold values from -1.5 to 1.5
Outputs:
- attended: bfloat16 [2, 32, 16384], P(None, 'groups', ('tp', 'sub')), parts along dimension 1
- entries: bfloat16 [2, 32, 1024], P(None, ('groups', 'tp', 'sub')), parts along dimension 1
There are 2 independent parts, one for each index of `groups`. A program takes and returns all parts, laid end to end along the dimension named above; an argument that names none is the same for every part. Nothing has to cross between parts.
Inputs may be any that keep to these rules, and one draw needn't show every extreme that they name: `cached_rotated_keys`: the first 64 slots of every row are filled. `lengths`: some request's cache holds exactly 512. `adapter_pool_slot`: a permutation; slot s lives on the device of index s // 1 along tp+sub.
All inputs are finite; a program needn't handle non-finite values.
Results may differ from a plain program's by a relative error of at most 0.006.
The roundings to bfloat16 on the way count: a program that leaves them out, or rounds other values in their place, can miss the bound.
Values may be sent and summed in bfloat16 or wider, within the bound.
No kernel may reach another device: no remote copies, remote signals or barrier semaphores. Data moves between devices by JAX's collectives and lax.ppermute only.
A program may use at most 128 MiB of HBM per device.

v0:
```python
import math

import jax
import jax.numpy as jnp
from jax import lax
from jax.sharding import PartitionSpec as P

ASKER_GROUPS = 64
KEY_HEADS = 4
HEAD_WIDTH = 128
STEPS = 2


adapter_scale = 0.5
rope_base = 500000.0
masked_score = -1e30


def rotate(vectors, positions):
    half_width = vectors.shape[-1] // 2
    frequency = rope_base ** (-2.0 * jnp.arange(half_width, dtype=jnp.float32) / vectors.shape[-1])
    angles = positions.astype(jnp.float32)[..., None, None] * frequency
    cosine = jnp.cos(angles)
    sine_part = jnp.sin(angles)
    first_half = vectors[..., :half_width]
    second_half = vectors[..., half_width:]
    return jnp.concatenate(
        [
            first_half * cosine - second_half * sine_part,
            second_half * cosine + first_half * sine_part,
        ],
        axis=-1,
    )


def attend(
    query_rot, cached_rotated_keys, cached_values, lengths, fresh_keys, fresh_values, first_step
):
    decode_iterations, row_count = (query_rot.shape[0], query_rot.shape[1])
    memory_length = cached_rotated_keys.shape[1]
    fresh_count = fresh_keys.shape[0]
    grouped = query_rot.reshape(
        decode_iterations, row_count, KEY_HEADS, ASKER_GROUPS // KEY_HEADS, HEAD_WIDTH
    )
    old_keys = cached_rotated_keys.reshape(row_count, memory_length, KEY_HEADS, HEAD_WIDTH)
    old_values = cached_values.reshape(row_count, memory_length, KEY_HEADS, HEAD_WIDTH)
    score_scale = 1.0 / math.sqrt(HEAD_WIDTH)
    scores_old = (
        jnp.einsum("brkgd,rlkd->brkgl", grouped, old_keys, preferred_element_type=jnp.float32)
        * score_scale
    )
    valid_cache = jnp.arange(memory_length, dtype=jnp.int32)[None, :] < lengths[:, None]
    scores_old = jnp.where(valid_cache[None, :, None, None, :], scores_old, masked_score)
    scores_new = (
        jnp.einsum("brkgd,trkd->brkgt", grouped, fresh_keys, preferred_element_type=jnp.float32)
        * score_scale
    )
    causal = (
        jnp.arange(fresh_count, dtype=jnp.int32)[None, :]
        <= first_step + jnp.arange(decode_iterations, dtype=jnp.int32)[:, None]
    )
    scores_new = jnp.where(causal[:, None, None, None, :], scores_new, masked_score)
    highest = jnp.maximum(jnp.max(scores_old, axis=-1), jnp.max(scores_new, axis=-1))
    earlier_probabilities = jnp.exp(scores_old - highest[..., None])
    weights_new = jnp.exp(scores_new - highest[..., None])
    totals = jnp.sum(earlier_probabilities, axis=-1) + jnp.sum(weights_new, axis=-1)
    probs_old = (earlier_probabilities / totals[..., None]).astype(jnp.bfloat16)
    probs_new = (weights_new / totals[..., None]).astype(jnp.bfloat16)
    attended_result_matrix = jnp.einsum(
        "brkgl,rlkd->brkgd", probs_old, old_values, preferred_element_type=jnp.float32
    )
    attended_result_matrix = attended_result_matrix + jnp.einsum(
        "brkgt,trkd->brkgd", probs_new, fresh_values, preferred_element_type=jnp.float32
    )
    return attended_result_matrix.reshape(
        decode_iterations, row_count, ASKER_GROUPS * HEAD_WIDTH
    ).astype(jnp.bfloat16)


def body(
    tokens,
    query_weight,
    key_value_weight,
    output_weight,
    cached_rotated_keys,
    cached_values,
    lengths,
    request_adapter,
    adapter_pool_slot,
    adapter_down_maps,
    query_up_maps,
    key_up_maps,
    value_up_maps,
    result_lowering_factors,
    output_up_maps,
):
    devices = lax.axis_size(("tp", "sub"))
    position = lax.axis_index(("tp", "sub"))
    total_rows = tokens.shape[1]
    resident_pool = adapter_down_maps.shape[0]
    pool_size = resident_pool * devices
    head_cols = query_weight.shape[1]
    kv_cols = key_value_weight.shape[1] // 2
    rank_columns = key_up_maps.shape[1]
    pool_index = jnp.arange(pool_size, dtype=jnp.int32)
    lender_index_entry = jnp.sum(
        jnp.where(request_adapter[:, None] == pool_index[None, :], adapter_pool_slot[None, :], 0),
        axis=1,
    )
    owner_mask = (
        lender_index_entry[:, None]
        == position * resident_pool + jnp.arange(resident_pool, dtype=jnp.int32)[None, :]
    ).astype(jnp.float32)
    step_groups = [(step, 1) for step in range(STEPS)]
    fresh_keys = []
    fresh_values = []
    outputs = []
    new_entries = []
    for first_step, decode_iterations in step_groups:
        step_tokens = tokens[first_step : first_step + decode_iterations]
        flat_rows = decode_iterations * total_rows
        local_flat = step_tokens.reshape(flat_rows, step_tokens.shape[2])
        collected_rows = lax.all_gather(step_tokens, ("tp", "sub"), axis=2, tiled=True).reshape(
            flat_rows, -1
        )
        owner_rows = jnp.tile(owner_mask, (decode_iterations, 1))
        down_all = jnp.einsum(
            "bu,yfu->byf", collected_rows, adapter_down_maps, preferred_element_type=jnp.float32
        )
        rank_in = jnp.sum(down_all * owner_rows[:, :, None], axis=1).astype(jnp.bfloat16)
        owner_rank = (owner_rows[:, :, None] * rank_in[:, None, :].astype(jnp.float32)).astype(
            jnp.bfloat16
        )
        key_correction = jnp.einsum(
            "mjc,jcn->mn",
            owner_rank[:, :, rank_columns : 2 * rank_columns],
            key_up_maps,
            preferred_element_type=jnp.float32,
        )
        value_correction = jnp.einsum(
            "mjc,jcn->mn",
            owner_rank[:, :, 2 * rank_columns :],
            value_up_maps,
            preferred_element_type=jnp.float32,
        )
        key_value_parts = jnp.dot(local_flat, key_value_weight, preferred_element_type=jnp.float32)
        key_value_parts = key_value_parts + adapter_scale * jnp.concatenate(
            [key_correction, value_correction], axis=1
        )
        kv_rows = lax.psum_scatter(
            key_value_parts.reshape(decode_iterations, total_rows, 2 * kv_cols),
            ("tp", "sub"),
            scatter_dimension=1,
            tiled=True,
        )
        row_count = kv_rows.shape[1]
        positions = (
            lengths[None, :] + first_step + jnp.arange(decode_iterations, dtype=jnp.int32)[:, None]
        )
        keys_now = rotate(
            kv_rows[..., :kv_cols].reshape(decode_iterations, row_count, KEY_HEADS, HEAD_WIDTH),
            positions,
        ).astype(jnp.bfloat16)
        current_values = kv_rows[..., kv_cols:].astype(jnp.bfloat16)
        fresh_keys.append(keys_now)
        fresh_values.append(
            current_values.reshape(decode_iterations, row_count, KEY_HEADS, HEAD_WIDTH)
        )
        new_entries.append(
            jnp.concatenate(
                [keys_now.reshape(decode_iterations, row_count, kv_cols), current_values], axis=-1
            )
        )
        query_plain = jnp.dot(collected_rows, query_weight, preferred_element_type=jnp.float32)
        full_delta = jnp.einsum(
            "mjc,jcn->mn",
            owner_rank[:, :, :rank_columns],
            query_up_maps,
            preferred_element_type=jnp.float32,
        )
        query_correction = lax.psum_scatter(
            full_delta, ("tp", "sub"), scatter_dimension=1, tiled=True
        )
        query_head_rows = (query_plain + adapter_scale * query_correction).astype(jnp.bfloat16)
        query_rows = lax.all_to_all(
            query_head_rows.reshape(decode_iterations, total_rows, head_cols),
            ("tp", "sub"),
            split_axis=1,
            concat_axis=2,
            tiled=True,
        )
        query_rot = rotate(
            query_rows.astype(jnp.float32).reshape(
                decode_iterations, row_count, ASKER_GROUPS, HEAD_WIDTH
            ),
            positions,
        ).astype(jnp.bfloat16)
        attended_result_matrix = attend(
            query_rot,
            cached_rotated_keys,
            cached_values,
            lengths,
            jnp.concatenate(fresh_keys, axis=0),
            jnp.concatenate(fresh_values, axis=0),
            first_step,
        )
        context_heads = lax.all_to_all(
            attended_result_matrix, ("tp", "sub"), split_axis=2, concat_axis=1, tiled=True
        )
        output_parts = jnp.dot(
            context_heads.reshape(flat_rows, head_cols),
            output_weight,
            preferred_element_type=jnp.float32,
        )
        context_gathered = lax.all_gather(context_heads, ("tp", "sub"), axis=2, tiled=True).reshape(
            flat_rows, -1
        )
        rank_all = jnp.einsum(
            "zs,abs->zab",
            context_gathered,
            result_lowering_factors,
            preferred_element_type=jnp.float32,
        )
        result_lowered_entries = jnp.sum(rank_all * owner_rows[:, :, None], axis=1).astype(
            jnp.bfloat16
        )
        owned_output = (
            owner_rows[:, :, None] * result_lowered_entries[:, None, :].astype(jnp.float32)
        ).astype(jnp.bfloat16)
        output_correction = jnp.einsum(
            "yna,nau->yu", owned_output, output_up_maps, preferred_element_type=jnp.float32
        )
        output_parts = output_parts + adapter_scale * output_correction
        summed = lax.psum_scatter(
            output_parts.reshape(decode_iterations, total_rows, -1),
            ("tp", "sub"),
            scatter_dimension=2,
            tiled=True,
        )
        outputs.append(summed.astype(jnp.bfloat16))
    return (jnp.concatenate(outputs, axis=0), jnp.concatenate(new_entries, axis=0))


def solution(mesh):
    placed = (
        P(None, "groups", ("tp", "sub")),
        P(None, ("tp", "sub")),
        P(("tp", "sub"), None),
        P(("tp", "sub"), None),
        P(("groups", "tp", "sub"), None, None),
        P(("groups", "tp", "sub"), None, None),
        P(("groups", "tp", "sub")),
        P("groups"),
        P(),
        P(("tp", "sub"), None, None),
        P(("tp", "sub"), None, None),
        P(("tp", "sub"), None, None),
        P(("tp", "sub"), None, None),
        P(("tp", "sub"), None, None),
        P(("tp", "sub"), None, None),
    )
    return jax.shard_map(
        body,
        mesh=mesh,
        in_specs=placed,
        out_specs=(P(None, "groups", ("tp", "sub")), P(None, ("groups", "tp", "sub"), None)),
        check_vma=False,
    )
```

profile of v0, /device:TPU:0, one launch (start us, length us, event | category | flops | bytes accessed | tf_op | source)
XLA Modules:
  0.0 706.1 jit_solution(18028298264520086186)
XLA Ops:
  7.3 0.9 fusion.136
  8.2 24.6 %all_gather.12 = bf16[1,16,16384]{2,1,0:T(8,128)(2,1)S(1)} all-gather(bf16[1,16,1024]{2,1,0:T(8,128)(2,1)S(1)} %get-tuple-element.20), channel_id=1, replica_groups=mesh['groups'=2,'tp'=8,'sub'=2] {'tp','sub'}, dimensions={2}, use_global_device_ids=true | all-gather | bytes 557056 | tf_op jit(solution)/shard_map/all_gather | solution.py:123
  32.7 0.9 select_reduce_fusion
  33.6 1.9 fusion.63
  35.5 1.0 fusion.104
  36.5 0.9 fusion.108
  37.4 18.9 %all_gather.14 = bf16[1,16,16384]{2,1,0:T(8,128)(2,1)S(1)} all-gather(bf16[1,16,1024]{2,1,0:T(8,128)(2,1)S(1)} %get-tuple-element.21), channel_id=1, replica_groups=mesh['groups'=2,'tp'=8,'sub'=2] {'tp','sub'}, dimensions={2}, use_global_device_ids=true | all-gather | bytes 557056 | tf_op jit(solution)/shard_map/all_gather | solution.py:123
  56.3 1.9 fusion.66
  58.2 0.2 fusion.102
  58.6 1.0 fusion.15
  59.6 1.0 fusion.14
  60.7 1.0 fusion.92
  61.8 1.0 fusion.90
  63.6 2.0 reshape.598
  65.6 2.0 reshape.607
  67.6 0.6 dynamic-slice
  68.1 78.2 %all-reduce.5.cloned.1.call-done = (f32[1,16,1024]{2,1,0:T(8,128)}, f32[1,16,1024]{2,1,0:T(8,128)}) async-done(((f32[1,16,1024]{2,1,0:T(8,128)}, f32[1,16,1024]{2,1,0:T(8,128)}), (f32[1,16,1024]{2,1,0:T(8,128)}, f32[1,16,1024]{2,1,0:T(8,128)})) %all-reduce.5.cloned.1.call-update) | async-done | bytes 131088
  146.4 1.4 constant_dynamic-slice_fusion
  147.8 1.5 fusion.135
  149.6 57.8 %reduce-scatter.7.cloned.1.call-done = f32[16,512]{1,0:T(8,128)} async-done(((f32[16,8192]{1,0:T(8,128)}), f32[16,512]{1,0:T(8,128)}) %reduce-scatter.7.cloned.1.call-update) | async-done | bytes 32784 | tf_op jit(solution)/shard_map/reduce_scatter | solution.py:181
  207.4 8.0 %fusion.23 = bf16[1,16,512]{2,1,0:T(8,128)(2,1)S(1)} fusion(bf16[16384,512]{1,0:T(8,128)(2,1)} %param.16, bf16[1,16,16384]{2,1,0:T(8,128)(2,1)S(1)} %all_gather.12, f32[16,512]{1,0:T(8,128)} %reduce-scatter.7.cloned.1.call-done), kind=kOutput, calls=%fused_computation.34 | convolution fusion | flops 268460032 | bytes 17350656 | tf_op jit(solution)/shard_map/dot_general | solution.py:174
  215.5 0.5 broadcast.194
  216.0 0.7 reduce.14
  216.7 0.6 reshape.650
  217.3 3.7 all-to-all-start
  221.1 45.1 %reduce-scatter.11.cloned.1.call-done = f32[16,512]{1,0:T(8,128)} async-done(((f32[16,8192]{1,0:T(8,128)}), f32[16,512]{1,0:T(8,128)}) %reduce-scatter.11.cloned.1.call-update) | async-done | bytes 32784 | tf_op jit(solution)/shard_map/reduce_scatter | solution.py:181
  266.2 8.0 %fusion.22 = bf16[1,16,512]{2,1,0:T(8,128)(2,1)S(1)} fusion(bf16[16384,512]{1,0:T(8,128)(2,1)} %param.16, bf16[1,16,16384]{2,1,0:T(8,128)(2,1)S(1)} %all_gather.14, f32[16,512]{1,0:T(8,128)} %reduce-scatter.11.cloned.1.call-done), kind=kOutput, calls=%fused_computation.33 | convolution fusion | flops 268460032 | bytes 17350656 | tf_op jit(solution)/shard_map/dot_general | solution.py:174
  274.3 0.7 reduce.12
  275.0 0.6 reshape.646
  275.7 4.3 all-to-all-start.2
  280.1 6.3 all-to-all-done.2
  286.6 0.2 fusion.112
  286.8 0.4 fusion.139
  287.1 0.2 fusion.94
  287.3 0.4 fusion.137
  287.7 0.2 fusion.138
  288.2 1.3 convolution_bitcast_fusion
  289.5 0.2 fusion.21
  289.7 5.9 convert_element_type.287
  295.6 62.6 %reduce.13 = bf16[8192]{0:T(1024)(128)(2,1)S(1)} reduce(bf16[8192,1,1]{2,1,0:T(2,128)(2,1)} %bitcast.237, bf16[]{:T(256)} %broadcast.194), dimensions={1,2}, to_apply=%bitcast.213.reduce_sub_computation | reduce | bytes 32770
  358.2 0.6 reshape.648
  358.9 3.7 all-to-all-start.3
  362.5 0.2 fusion.24
  362.8 5.9 convert_element_type.286
  368.7 62.6 %reduce.15 = bf16[8192]{0:T(1024)(128)(2,1)S(1)} reduce(bf16[8192,1,1]{2,1,0:T(2,128)(2,1)} %bitcast.236, bf16[]{:T(256)} %broadcast.194), dimensions={1,2}, to_apply=%bitcast.217.reduce_sub_computation | reduce | bytes 32770
  431.3 0.6 reshape.652
  432.0 6.1 all-to-all-start.1
  438.0 0.3 reduce-scatter.13.cloned.1.call-start
  438.3 8.4 %reshape.649 = bf16[8192,1,1]{2,1,0:T(2,128)(2,1)} reshape(bf16[16,2,256]{2,1,0:T(2,128)(2,1)S(1)} %all-to-all-done.3) | data formatting | bytes 32768
  446.7 62.0 %bitcast_reduce_fusion.1 = bf16[8192]{0:T(1024)(128)(2,1)S(1)} fusion(bf16[8192,1,1]{2,1,0:T(2,128)(2,1)} %reshape.649), kind=kLoop, calls=%fused_computation.173 | loop fusion | bytes 32768 | tf_op jit(solution)/shard_map/all_to_all | solution.py:207
  508.7 22.4 %all_gather.15 = bf16[1,16,8192]{2,1,0:T(8,128)(2,1)S(1)} all-gather(bf16[1,16,512]{2,1,0:T(8,128)(2,1)S(1)} %all_to_all.17), channel_id=1, replica_groups=mesh['groups'=2,'tp'=8,'sub'=2] {'tp','sub'}, dimensions={2}, use_global_device_ids=true | all-gather | bytes 278528 | tf_op jit(solution)/shard_map/all_gather | solution.py:215
  531.2 8.1 %fusion.141 = f32[16,16384]{1,0:T(8,128)S(1)} fusion(bf16[16,512]{1,0:T(8,128)(2,1)S(1)} %reshape.628, bf16[512,16384]{1,0:T(8,128)(2,1)} %param.18), kind=kOutput, calls=%fused_computation.179 | convolution fusion | flops 268435456 | bytes 17842176 | tf_op jit(solution)/shard_map/dot_general | solution.py:210
  539.2 2.8 fusion.1
  542.0 0.3 reduce-scatter.9.cloned.1.call-start
  542.3 8.4 %reshape.653 = bf16[8192,1,1]{2,1,0:T(2,128)(2,1)} reshape(bf16[16,2,256]{2,1,0:T(2,128)(2,1)S(1)} %all-to-all-done.1) | data formatting | bytes 32768
  550.7 62.0 %bitcast_reduce_fusion = bf16[8192]{0:T(1024)(128)(2,1)S(1)} fusion(bf16[8192,1,1]{2,1,0:T(2,128)(2,1)} %reshape.653), kind=kLoop, calls=%fused_computation.172 | loop fusion | bytes 32768 | tf_op jit(solution)/shard_map/all_to_all | solution.py:207
  612.8 18.2 %all_gather.13 = bf16[1,16,8192]{2,1,0:T(8,128)(2,1)S(1)} all-gather(bf16[1,16,512]{2,1,0:T(8,128)(2,1)S(1)} %all_to_all.14), channel_id=1, replica_groups=mesh['groups'=2,'tp'=8,'sub'=2] {'tp','sub'}, dimensions={2}, use_global_device_ids=true | all-gather | bytes 278528 | tf_op jit(solution)/shard_map/all_gather | solution.py:215
  630.9 8.1 %fusion.140 = f32[16,16384]{1,0:T(8,128)S(1)} fusion(bf16[16,512]{1,0:T(8,128)(2,1)S(1)} %reshape.609, bf16[512,16384]{1,0:T(8,128)(2,1)} %param.18), kind=kOutput, calls=%fused_computation.178 | convolution fusion | flops 268435456 | bytes 17842176 | tf_op jit(solution)/shard_map/dot_general | solution.py:210
  639.0 2.8 fusion.3
  641.9 0.6 copy.101
  642.5 0.8 convert_element_type.281
  643.3 54.5 %reduce-scatter.9.cloned.1.call-done = f32[1,16,1024]{2,1,0:T(8,128)} async-done(((f32[1,16,16384]{2,1,0:T(8,128)}), f32[1,16,1024]{2,1,0:T(8,128)}) %reduce-scatter.9.cloned.1.call-update) | async-done | bytes 65552 | tf_op jit(solution)/shard_map/reduce_scatter | solution.py:234
  697.8 0.8 convert_element_type.261
  698.6 0.6 pad_maximum_fusion
  (61 shorter events, 1.7 us)
Async XLA Ops:
  7.2 51.4 %copy-start = (bf16[1024,1024]{1,0:T(8,128)(2,1)S(1)}, bf16[1024,1024]{1,0:T(8,128)(2,1)}, u32[]{:S(2)}) copy-start(bf16[1024,1024]{1,0:T(8,128)(2,1)} %param.17) | copy-start | bytes 6291460
  7.2 51.4 %copy-start.4 = (bf16[2,16,1024]{2,1,0:T(8,128)(2,1)S(1)}, bf16[2,16,1024]{2,1,0:T(8,128)(2,1)}, u32[]{:S(2)}) copy-start(bf16[2,16,1024]{2,1,0:T(8,128)(2,1)} %param.15) | copy-start | bytes 196612
  7.2 51.0 %copy-start.5 = (bf16[1,16,512]{2,1,0:T(8,128)(2,1)S(1)}, bf16[1,16,512]{2,1,0:T(8,128)(2,1)}, u32[]{:S(2)}) copy-start(bf16[1,16,512]{2,1,0:T(8,128)(2,1)} %param.27) | copy-start | bytes 49156
  7.2 51.2 %copy-start.6 = (bf16[1,16,512]{2,1,0:T(8,128)(2,1)S(1)}, bf16[1,16,512]{2,1,0:T(8,128)(2,1)}, u32[]{:S(2)}) copy-start(bf16[1,16,512]{2,1,0:T(8,128)(2,1)} %param.26) | copy-start | bytes 49156
  7.2 139.2 %all-reduce.5.cloned.1.call-start = ((), (), s32[]{:S(2)}) async-start(), calls=%async_computation.12 | async-start | bytes 262144
  35.5 25.2 %copy-start.2 = (bf16[1,16,8192]{2,1,0:T(8,128)(2,1)S(1)}, bf16[1,16,8192]{2,1,0:T(8,128)(2,1)}, u32[]{:S(2)}) copy-start(bf16[1,16,8192]{2,1,0:T(8,128)(2,1)} %param.25) | copy-start | bytes 786436
  58.6 9.0 %copy-start.7 = (u32[32]{0:T(128)S(1)}, u32[32]{0:T(128)}, u32[]{:S(2)}) copy-start(u32[32]{0:T(128)} %constant.54) | copy-start | bytes 388
  60.6 146.8 %reduce-scatter.7.cloned.1.call-start = ((), (), s32[]{:S(2)}) async-start(), calls=%async_computation.8 | async-start | bytes 557056 | tf_op jit(solution)/shard_map/reduce_scatter | solution.py:181
  61.7 204.5 %reduce-scatter.11.cloned.1.call-start = ((), (), s32[]{:S(2)}) async-start(), calls=%async_computation.10 | async-start | bytes 557056 | tf_op jit(solution)/shard_map/reduce_scatter | solution.py:181
  217.3 58.3 %all-to-all-start = ((bf16[16,2,256]{2,1,0:T(2,128)(2,1)}), bf16[16,2,256]{2,1,0:T(2,128)(2,1)S(1)}, u32[]{:S(2)}, u32[]{:S(2)}) async-start(bf16[16,2,256]{2,1,0:T(2,128)(2,1)} %reshape.650), calls=%async_computation.1 | async-start | bytes 32768 | tf_op jit(solution)/shard_map/all_to_all | solution.py:185
  221.1 65.7 %copy-start.1 = (bf16[512,4,128]{2,1,0:T(4,128)(2,1)S(1)}, bf16[512,4,128]{2,1,0:T(4,128)(2,1)}, u32[]{:S(2)}) copy-start(bf16[512,4,128]{2,1,0:T(4,128)(2,1)} %reshape.598) | copy-start | bytes 1572868
  275.7 10.8 %all-to-all-start.2 = ((bf16[16,2,256]{2,1,0:T(2,128)(2,1)}), bf16[16,2,256]{2,1,0:T(2,128)(2,1)S(1)}, u32[]{:S(2)}, u32[]{:S(2)}) async-start(bf16[16,2,256]{2,1,0:T(2,128)(2,1)} %reshape.646), calls=%async_computation.5 | async-start | bytes 32768 | tf_op jit(solution)/shard_map/all_to_all | solution.py:185
  289.7 72.9 %copy-start.3 = (bf16[512,4,128]{2,1,0:T(4,128)(2,1)S(1)}, bf16[512,4,128]{2,1,0:T(4,128)(2,1)}, u32[]{:S(2)}) copy-start(bf16[512,4,128]{2,1,0:T(4,128)(2,1)} %reshape.607) | copy-start | bytes 1572868
  358.9 73.1 %all-to-all-start.3 = ((bf16[16,2,256]{2,1,0:T(2,128)(2,1)}), bf16[16,2,256]{2,1,0:T(2,128)(2,1)S(1)}, u32[]{:S(2)}, u32[]{:S(2)}) async-start(bf16[16,2,256]{2,1,0:T(2,128)(2,1)} %reshape.648), calls=%async_computation.6 | async-start | bytes 32768 | tf_op jit(solution)/shard_map/all_to_all | solution.py:207
  432.0 110.4 %all-to-all-start.1 = ((bf16[16,2,256]{2,1,0:T(2,128)(2,1)}), bf16[16,2,256]{2,1,0:T(2,128)(2,1)S(1)}, u32[]{:S(2)}, u32[]{:S(2)}) async-start(bf16[16,2,256]{2,1,0:T(2,128)(2,1)} %reshape.652), calls=%async_computation.2 | async-start | bytes 32768 | tf_op jit(solution)/shard_map/all_to_all | solution.py:207
  438.0 204.4 %reduce-scatter.13.cloned.1.call-start = ((), (), s32[]{:S(2)}) async-start(), calls=%async_computation.11 | async-start | bytes 1114112 | tf_op jit(solution)/shard_map/reduce_scatter | solution.py:234
  542.0 155.8 %reduce-scatter.9.cloned.1.call-start = ((), (), s32[]{:S(2)}) async-start(), calls=%async_computation.9 | async-start | bytes 1114112 | tf_op jit(solution)/shard_map/reduce_scatter | solution.py:234
Sparse Core Ops, SparseCore 0:
  60.8 85.5 all-reduce.4
  149.9 57.4 reduce-scatter.6
  211.4 54.7 reduce-scatter.10
  542.1 54.6 reduce-scatter.12
  641.9 55.8 reduce-scatter.8
where the time goes:
time: 712 us; the launch traced here: 706 us
  waiting for transfers between devices  242 us (34%)
  local copies, waits for them, and re-layouts  163 us (23%)
  other arithmetic  133 us (19%)
  blocking collectives  84 us (12%)
  matrix products  50.8 us (7%)
  starting transfers between devices  18.4 us (3%)
  between operations  15 us (2%)
    unnamed x4, other arithmetic  127 us
    all_to_all x4, local copies, waits for them, and re-layouts, body(): lax.all_to_all(attended_result_matrix, ('tp', 'sub'), split_axis=2, conca...  124 us
    reduce_scatter x2, waiting for transfers between devices, body(): lax.psum_scatter(full_delta, ('tp', 'sub'), scatter_dimension=1, tiled=True)  103 us
    unnamed x6, waiting for transfers between devices  78.3 us
    reduce_scatter x2, waiting for transfers between devices, body(): lax.psum_scatter(output_parts.reshape(decode_iterations, total_rows, -1),...  54.5 us
    all_gather x2, blocking collectives, body(): lax.all_gather(step_tokens, ('tp', 'sub'), axis=2, tiled=True)  43.4 us
    all_gather x2, blocking collectives, body(): lax.all_gather(context_heads, ('tp', 'sub'), axis=2, tiled=True)  40.6 us
    unnamed x27, local copies, waits for them, and re-layouts  21.1 us
  transfers between devices with their start and end apart: 9, of which 5 were waited for; matrix products, arithmetic and copies ran while one was open for 37% of the time, Pallas kernels for 0%

commit v1 on v0

v1 whole, which is shorter than its diff:
```python
import functools
import math

import jax
import jax.numpy as jnp
from jax import lax
from jax.experimental import pallas as pl
from jax.experimental.pallas import tpu as pltpu
from jax.sharding import PartitionSpec as P

HEAD_WIDTH = 128
ROPE_BASE = 500000.0
MASKED = -1e30
SCALE = 0.5
F32 = jnp.float32
BF16 = jnp.bfloat16

PARAMS = pltpu.CompilerParams(vmem_limit_bytes=48 * 1024 * 1024)


def nn(a, b):
    return lax.dot_general(a, b, (((1,), (0,)), ((), ())), preferred_element_type=F32)


def nt(a, b):
    return lax.dot_general(a, b, (((1,), (1,)), ((), ())), preferred_element_type=F32)


def tn(a, b):
    return lax.dot_general(a, b, (((0,), (0,)), ((), ())), preferred_element_type=F32)


def query_half_kernel(which, x_ref, w_ref, q_ref):
    @pl.when(pl.program_id(0) == 0)
    def _():
        q_ref[...] = jnp.zeros_like(q_ref)

    total = nn(x_ref[0], w_ref[0, 0])
    for j in range(1, x_ref.shape[0]):
        total = total + nn(x_ref[j], w_ref[j, 0])
    q_ref[...] += total


def query_half(which, x, weight):
    chips, rows, width = x.shape
    cols = weight.shape[-1]
    per = 2
    return pl.pallas_call(
        query_half_kernel,
        out_shape=jax.ShapeDtypeStruct((rows, cols), F32),
        grid_spec=pltpu.PrefetchScalarGridSpec(
            num_scalar_prefetch=1,
            grid=(chips // per,),
            in_specs=[
                pl.BlockSpec((per, rows, width), lambda i, s: (i, 0, 0)),
                pl.BlockSpec((per, 1, width, cols), lambda i, s: (i, s[0], 0, 0)),
            ],
            out_specs=pl.BlockSpec((rows, cols), lambda i, s: (0, 0)),
        ),
        compiler_params=PARAMS,
    )(which, x, weight)


def rank_half_kernel(which, x_ref, d_ref, r_ref):
    chips, rows, width = x_ref.shape
    total = None
    for c in range(chips):
        start = pl.multiple_of((2 * c + which[0]) * width, width)
        part = nt(d_ref[:, pl.ds(start, width)], x_ref[c])
        total = part if total is None else total + part
    r_ref[...] = total


def rank_half(which, x, down):
    return pl.pallas_call(
        rank_half_kernel,
        out_shape=jax.ShapeDtypeStruct((down.shape[0], x.shape[1]), F32),
        in_specs=[
            pl.BlockSpec(memory_space=pltpu.SMEM),
            pl.BlockSpec(memory_space=pltpu.VMEM),
            pl.BlockSpec(memory_space=pltpu.VMEM),
        ],
        compiler_params=PARAMS,
    )(which, x, down)


def dense_kernel(x_ref, w_ref, o_ref):
    o_ref[...] = nn(x_ref[...], w_ref[...])


def dense(x, weight):
    return pl.pallas_call(
        dense_kernel,
        out_shape=jax.ShapeDtypeStruct((x.shape[0], weight.shape[1]), F32),
        compiler_params=PARAMS,
    )(x, weight)


def finish_kernel(qa_ref, qb_ref, ranks_ref, mask_ref, up_ref, kv_ref, own_ref, kup_ref, vup_ref, o_ref):
    owners, rank, rows = ranks_ref.shape
    devices, steps, _ = o_ref.shape
    cols = qa_ref.shape[1]
    half = kup_ref.shape[1]
    u = ranks_ref[0].astype(F32)
    for o in range(1, owners):
        u = u + ranks_ref[o].astype(F32)
    spread = jnp.concatenate([u] * owners, axis=0) * mask_ref[...]
    query = qa_ref[...] + qb_ref[...] + SCALE * tn(spread.astype(BF16), up_ref[...])
    own = own_ref[...].astype(BF16)
    keys = kv_ref[:, :half] + SCALE * tn(own[:rank], kup_ref[...])
    values = kv_ref[:, half:] + SCALE * tn(own[rank:], vup_ref[...])
    for r in range(devices):
        for t in range(steps):
            m = t * devices + r
            o_ref[r, t : t + 1, :cols] = query[m : m + 1]
            o_ref[r, t : t + 1, cols : cols + half] = keys[m : m + 1]
            o_ref[r, t : t + 1, cols + half :] = values[m : m + 1]


def rope(v, cosine, sine):
    return v * cosine + pltpu.roll(v, HEAD_WIDTH // 2, 1) * sine


def attend_kernel(len_ref, recv_ref, cos_ref, sin_ref, k_ref, v_ref, ctx_ref, ent_ref, q_s, kn_s, vn_s):
    devices, steps, cols = ctx_ref.shape
    slots, kv_cols = k_ref.shape
    kv_heads = kv_cols // HEAD_WIDTH
    per_device = cols // HEAD_WIDTH
    group = devices * per_device // kv_heads
    rows = group * steps
    score_scale = 1.0 / math.sqrt(HEAD_WIDTH)
    length = len_ref[0]
    kv = recv_ref[0, :, cols:]
    for d in range(1, devices):
        kv = kv + recv_ref[d, :, cols:]
    cosine = cos_ref[...]
    sine = sin_ref[...]
    kn_s[...] = jnp.zeros_like(kn_s)
    vn_s[...] = jnp.zeros_like(vn_s)
    fresh = kn_s.shape[0]
    col_old = lax.broadcasted_iota(jnp.int32, (rows, slots), 1)
    col_new = lax.broadcasted_iota(jnp.int32, (rows, fresh), 1)
    step_new = lax.rem(lax.broadcasted_iota(jnp.int32, (rows, fresh), 0), steps)
    for k in range(kv_heads):
        lanes = slice(k * HEAD_WIDTH, (k + 1) * HEAD_WIDTH)
        for i in range(group):
            h = k * group + i
            d, hh = h // per_device, h % per_device
            q_s[i * steps : (i + 1) * steps, :] = recv_ref[d, :, hh * HEAD_WIDTH : (hh + 1) * HEAD_WIDTH]
        query = q_s[...].astype(BF16).astype(F32)
        query = rope(query, cosine, sine).astype(BF16)
        key_now = rope(kv[:, lanes], cosine[:steps], sine[:steps]).astype(BF16).astype(F32)
        value_now = kv[:, kv_cols + k * HEAD_WIDTH : kv_cols + (k + 1) * HEAD_WIDTH].astype(BF16).astype(F32)
        ent_ref[:, lanes] = key_now
        ent_ref[:, kv_cols + k * HEAD_WIDTH : kv_cols + (k + 1) * HEAD_WIDTH] = value_now
        kn_s[:steps, :] = key_now
        vn_s[:steps, :] = value_now
        old = nt(query, k_ref[:, lanes]) * score_scale
        old = jnp.where(col_old < length, old, MASKED)
        new = nt(query, kn_s[...].astype(BF16)) * score_scale
        new = jnp.where((col_new < steps) & (col_new <= step_new), new, MASKED)
        top = jnp.maximum(jnp.max(old, axis=1, keepdims=True), jnp.max(new, axis=1, keepdims=True))
        e_old = jnp.exp(old - top)
        e_new = jnp.exp(new - top)
        total = jnp.sum(e_old, axis=1, keepdims=True) + jnp.sum(e_new, axis=1, keepdims=True)
        p_old = (e_old / total).astype(BF16)
        p_new = (e_new / total).astype(BF16)
        out = nn(p_old, v_ref[:, lanes]) + nn(p_new, vn_s[...].astype(BF16))
        out = out.astype(BF16).astype(F32)
        for i in range(group):
            h = k * group + i
            d, hh = h // per_device, h % per_device
            ctx_ref[d, :, hh * HEAD_WIDTH : (hh + 1) * HEAD_WIDTH] = out[i * steps : (i + 1) * steps, :]


def lower_kernel(ctx_ref, mask_ref, low_ref, x_ref, part_ref, x_s):
    devices, steps, cols = ctx_ref.shape
    rank = part_ref.shape[0]
    for r in range(devices):
        for t in range(steps):
            x_s[t * devices + r : t * devices + r + 1, :] = ctx_ref[r, t : t + 1, :]
    x = x_s[...].astype(BF16)
    x_ref[...] = x
    every = nt(low_ref[...], x) * mask_ref[...]
    part = every[:rank]
    for s in range(1, every.shape[0] // rank):
        part = part + every[s * rank : (s + 1) * rank]
    part_ref[...] = part


def out_half_kernel(which, x_ref, w_ref, o_ref):
    o_ref[0] = nn(x_ref[...], w_ref[...])


def out_half(which, x, weight, chips):
    rows, cols = x.shape
    width = weight.shape[1] // (2 * chips)
    return pl.pallas_call(
        out_half_kernel,
        out_shape=jax.ShapeDtypeStruct((chips, rows, width), F32),
        grid_spec=pltpu.PrefetchScalarGridSpec(
            num_scalar_prefetch=1,
            grid=(chips,),
            in_specs=[
                pl.BlockSpec((rows, cols), lambda i, s: (0, 0)),
                pl.BlockSpec((cols, width), lambda i, s: (0, 2 * i + s[0])),
            ],
            out_specs=pl.BlockSpec((1, rows, width), lambda i, s: (i, 0, 0)),
        ),
        compiler_params=PARAMS,
    )(which, x, weight)


def pair_kernel(a_ref, b_ref, parts_ref, mask_ref, up_ref, o_ref):
    u = parts_ref[0]
    for d in range(1, parts_ref.shape[0]):
        u = u + parts_ref[d]
    u = u.astype(BF16).astype(F32)
    spread = jnp.concatenate([u * mask_ref[0:1, :], u * mask_ref[1:2, :]], axis=0).astype(BF16)
    for c in range(a_ref.shape[0]):
        o_ref[c] = (a_ref[c] + b_ref[c] + SCALE * tn(spread, up_ref[c])).astype(BF16)


def total_kernel(x_ref, o_ref):
    total = x_ref[0].astype(F32)
    for c in range(1, x_ref.shape[0]):
        total = total + x_ref[c].astype(F32)
    o_ref[...] = total.astype(BF16)


def body(
    tokens,
    query_weight,
    key_value_weight,
    output_weight,
    cached_rotated_keys,
    cached_values,
    lengths,
    request_adapter,
    adapter_pool_slot,
    adapter_down_maps,
    query_up_maps,
    key_up_maps,
    value_up_maps,
    result_lowering_factors,
    output_up_maps,
):
    both = ("tp", "sub")
    chips = lax.axis_size("tp")
    devices = lax.axis_size(both)
    me = lax.axis_index(both)
    core = lax.axis_index("sub")
    steps, requests, width = tokens.shape
    rows = steps * requests
    cols = query_weight.shape[1]
    rank = key_up_maps.shape[1]
    pool = devices
    assert adapter_down_maps.shape[0] == 1 and requests == devices and cached_values.shape[0] == 1
    swap = [(0, 1), (1, 0)]
    here = core.astype(jnp.int32).reshape(1)
    there = 1 - here

    x = tokens.reshape(rows, width)
    copies = jnp.broadcast_to(x[None], (chips, rows, width))
    mine = lax.all_to_all(copies, "tp", 0, 0, tiled=True)
    other = lax.ppermute(mine, "sub", swap)

    kv = dense(x, key_value_weight)

    index = jnp.arange(pool, dtype=jnp.int32)
    slot = jnp.sum(
        jnp.where(request_adapter[:, None] == index[None, :], adapter_pool_slot[None, :], 0), axis=1
    )
    row_slot = jnp.tile(slot, steps)[None, :]
    spread_mask = (jnp.repeat(index, rank)[:, None] == row_slot).astype(F32)
    own_mask = (row_slot == me).astype(F32)
    pair_mask = (jnp.stack([me, me + 1 - 2 * core])[:, None] == row_slot).astype(F32)

    def by_heads(maps, after):
        pieces = maps.reshape(rank, devices, cols).transpose(1, 0, 2)
        pieces, _ = lax.optimization_barrier((pieces, after))
        return lax.all_to_all(pieces, both, 0, 0, tiled=True).reshape(pool * rank, cols)

    up_by_heads = by_heads(query_up_maps, mine)

    out_up = output_up_maps.reshape(rank, chips, 2, width).transpose(2, 1, 0, 3)
    up_here = lax.dynamic_index_in_dim(out_up, core, 0, keepdims=False)
    up_there = lax.dynamic_index_in_dim(out_up, 1 - core, 0, keepdims=False)
    up_pair = jnp.concatenate([up_here, lax.ppermute(up_there, "sub", swap)], axis=1)

    down = adapter_down_maps.reshape(adapter_down_maps.shape[1], -1)
    weight = query_weight.reshape(chips, 2, width, cols)
    q_mine = query_half(here, mine, weight)
    rank_mine = rank_half(here, mine, down)
    rank_all = (rank_mine + rank_half(there, other, down)).astype(BF16).astype(F32) * own_mask
    rank_query = rank_all[:rank].astype(BF16)
    ranks = lax.all_to_all(
        jnp.broadcast_to(rank_query[None], (devices, rank, rows)), both, 0, 0, tiled=True
    )
    q_other = query_half(there, other, weight)
    to_rows = pl.pallas_call(
        finish_kernel,
        out_shape=jax.ShapeDtypeStruct((devices, steps, cols + kv.shape[1]), F32),
        compiler_params=PARAMS,
    )(
        q_mine,
        q_other,
        ranks,
        spread_mask,
        up_by_heads,
        kv,
        rank_all[rank:],
        key_up_maps[0],
        value_up_maps[0],
    )
    arrived = lax.all_to_all(to_rows, both, 0, 0, tiled=True)

    low_by_heads = by_heads(result_lowering_factors, arrived)

    kv_cols = key_value_weight.shape[1] // 2
    half_width = HEAD_WIDTH // 2
    frequency = ROPE_BASE ** (-2.0 * jnp.arange(half_width, dtype=F32) / HEAD_WIDTH)
    positions = lengths[0] + jnp.arange(steps, dtype=jnp.int32)
    angles = positions.astype(F32)[:, None] * frequency
    cosine, sine = jnp.cos(angles), jnp.sin(angles)
    group = devices * cols // kv_cols
    cosine = jnp.tile(jnp.concatenate([cosine, cosine], axis=1), (group, 1))
    sine = jnp.tile(jnp.concatenate([-sine, sine], axis=1), (group, 1))
    vmem = pl.BlockSpec(memory_space=pltpu.VMEM)
    context, fresh = pl.pallas_call(
        attend_kernel,
        out_shape=(
            jax.ShapeDtypeStruct((devices, steps, cols), F32),
            jax.ShapeDtypeStruct((steps, 2 * kv_cols), F32),
        ),
        in_specs=[pl.BlockSpec(memory_space=pltpu.SMEM)] + [vmem] * 5,
        scratch_shapes=[
            pltpu.VMEM((group * steps, HEAD_WIDTH), F32),
            pltpu.VMEM((16, HEAD_WIDTH), F32),
            pltpu.VMEM((16, HEAD_WIDTH), F32),
        ],
        compiler_params=PARAMS,
    )(lengths, arrived, cosine, sine, cached_rotated_keys[0], cached_values[0])
    entries = fresh.astype(BF16)[:, None, :]

    by_head = lax.all_to_all(context, both, 0, 0, tiled=True)
    lhs, part = pl.pallas_call(
        lower_kernel,
        out_shape=(
            jax.ShapeDtypeStruct((rows, cols), BF16),
            jax.ShapeDtypeStruct((rank, rows), F32),
        ),
        scratch_shapes=[pltpu.VMEM((rows, cols), F32)],
        compiler_params=PARAMS,
    )(by_head, spread_mask, low_by_heads)
    parts = lax.all_to_all(
        jnp.broadcast_to(part[None], (devices, rank, rows)), both, 0, 0, tiled=True
    )
    out_there = out_half(there, lhs, output_weight, chips)
    received = lax.ppermute(out_there, "sub", swap)
    out_here = out_half(here, lhs, output_weight, chips)
    chip_total = pl.pallas_call(
        pair_kernel,
        out_shape=jax.ShapeDtypeStruct((chips, rows, width), BF16),
        compiler_params=PARAMS,
    )(out_here, received, parts, pair_mask, up_pair)
    pieces = lax.all_to_all(chip_total, "tp", 0, 0, tiled=True)
    attended = pl.pallas_call(
        total_kernel,
        out_shape=jax.ShapeDtypeStruct((rows, width), BF16),
        compiler_params=PARAMS,
    )(pieces)
    return attended.reshape(steps, requests, width), entries


def solution(mesh):
    placed = (
        P(None, "groups", ("tp", "sub")),
        P(None, ("tp", "sub")),
        P(("tp", "sub"), None),
        P(("tp", "sub"), None),
        P(("groups", "tp", "sub"), None, None),
        P(("groups", "tp", "sub"), None, None),
        P(("groups", "tp", "sub")),
        P("groups"),
        P(),
        P(("tp", "sub"), None, None),
        P(("tp", "sub"), None, None),
        P(("tp", "sub"), None, None),
        P(("tp", "sub"), None, None),
        P(("tp", "sub"), None, None),
        P(("tp", "sub"), None, None),
    )
    return jax.shard_map(
        body,
        mesh=mesh,
        in_specs=placed,
        out_specs=(P(None, "groups", ("tp", "sub")), P(None, ("groups", "tp", "sub"), None)),
        check_vma=False,
    )
```

time: 712 us -> 143 us (0.20)
  waiting for transfers between devices: 242 us -> 34.2 us
  local copies, waits for them, and re-layouts: 163 us -> 11.4 us
  other arithmetic: 133 us -> 2.68 us
  matrix products: 50.8 us -> 0 us
  blocking collectives: 84 us -> 34.2 us
  Pallas kernels: 0 us -> 30.8 us
  between operations: 15 us -> 1.65 us
  starting transfers between devices: 18.4 us -> 26.8 us
    reduce_scatter x4 -> x0, waiting for transfers between devices: 157 us -> none  [the longest x2 103 us: body(): lax.psum_scatter(full_delta, ('tp', 'sub'), scatter_dimension=1, tiled=True)]
    unnamed x4 -> x0, other arithmetic: 127 us -> none
    all_to_all x4 -> x1, local copies, waits for them, and re-layouts: 124 us -> 0.52 us  [body(): lax.all_to_all(jnp.broadcast_to(part[None], (devices, rank, rows)), both,...]
    all_gather x4 -> x0, blocking collectives: 84 us -> none  [the longest x2 43.4 us: body(): lax.all_gather(step_tokens, ('tp', 'sub'), axis=2, tiled=True)]
    unnamed x6 -> x0, waiting for transfers between devices: 78.3 us -> none
    dot_general x23 -> x0, matrix products: 50.8 us -> none  [the longest x2 16.1 us: body(): jnp.dot(context_heads.reshape(flat_rows, head_cols), output_weight, prefe...]
    all_to_all x0 -> x2, blocking collectives: none -> 34.2 us  [the longest x1 21.6 us: body(): mine = lax.all_to_all(copies, 'tp', 0, 0, tiled=True)]
    pallas_call x0 -> x12, Pallas kernels: none -> 30.8 us  [the longest x2 13.2 us: out_half(): pl.pallas_call(out_half_kernel, out_shape=jax.ShapeDtypeStruct((chips, ro...]
  transfers between devices with their start and end apart: 9 -> 9, of which waited for: 5 -> 4; matrix products, arithmetic and copies ran while one was open for 37% -> 6% of each run, Pallas kernels for 0% -> 12%
where the time goes in v1:
time: 143 us; the launch traced here: 142 us
  blocking collectives  34.2 us (24%)
  waiting for transfers between devices  34.2 us (24%)
  Pallas kernels  30.8 us (22%)
  starting transfers between devices  26.8 us (19%)
  local copies, waits for them, and re-layouts  11.4 us (8%)
  other arithmetic  2.68 us (2%)
  between operations  1.65 us (1%)
    all_to_all x1, blocking collectives, body(): mine = lax.all_to_all(copies, 'tp', 0, 0, tiled=True)  21.6 us
    all_to_all x1, waiting for transfers between devices, body(): pieces = lax.all_to_all(chip_total, 'tp', 0, 0, tiled=True)  14.2 us
    pallas_call x2, Pallas kernels, out_half(): pl.pallas_call(out_half_kernel, out_shape=jax.ShapeDtypeStruct((chips, ro...  13.2 us
    all_to_all x1, blocking collectives, by_heads(): lax.all_to_all(pieces, both, 0, 0, tiled=True).reshape(pool * rank, cols)  12.6 us
    pallas_call x2, Pallas kernels, query_half(): pl.pallas_call(query_half_kernel, out_shape=jax.ShapeDtypeStruct((rows, c...  9.94 us
    all_to_all x1, waiting for transfers between devices, body(): arrived = lax.all_to_all(to_rows, both, 0, 0, tiled=True)  8.79 us
    unnamed x26, local copies, waits for them, and re-layouts  7.22 us
    all_to_all x1, waiting for transfers between devices, body(): by_head = lax.all_to_all(context, both, 0, 0, tiled=True)  6.6 us
  transfers between devices with their start and end apart: 9, of which 4 were waited for; matrix products, arithmetic and copies ran while one was open for 6% of the time, Pallas kernels for 12%

profile of v1, /device:TPU:0, one launch (start us, length us, event | category | flops | bytes accessed | tf_op | source)
XLA Modules:
  0.0 141.7 jit_solution(15490499311428471090)
XLA Ops:
  0.6 0.9 broadcast_in_dim.25
  1.5 21.6 %all_to_all.40.x_ref = bf16[8,32,1024]{2,1,0:T(8,128)(2,1)S(1)} all-to-all(bf16[8,32,1024]{2,1,0:T(8,128)(2,1)S(1)} %broadcast_in_dim.25), channel_id=1, replica_groups=mesh['groups'=2,'tp'=8,'sub'=2] {'tp'}, dimensions={0} | all-to-all | bytes 1048576 | tf_op jit(solution)/shard_map/all_to_all | solution.py:265
  23.1 0.0 collective-permute-start
  23.1 0.9 select_reduce_fusion
  24.0 0.1 broadcast_in_dim_tile.3
  24.1 1.4 copy-done
  25.5 0.3 shard_map.160
  25.9 0.0 collective-permute-done.x_ref
  25.9 0.3 shard_map.161
  26.3 0.7 reshape.77
  27.0 3.8 %all-to-all-start.1 = ((bf16[16,2,256]{2,1,0:T(2,128)(2,1)}), bf16[16,2,256]{2,1,0:T(2,128)(2,1)S(1)}, u32[]{:S(2)}, u32[]{:S(2)}) async-start(bf16[16,2,256]{2,1,0:T(2,128)(2,1)} %reshape.77), calls=%async_computation.1 | async-start | bytes 32768 | tf_op jit(solution)/shard_map/all_to_all | solution.py:297
  30.8 1.0 copy.29
  31.8 0.8 copy.38
  32.7 4.6 %all-to-all-done.1 = bf16[16,2,256]{2,1,0:T(2,128)(2,1)S(1)} async-done(((bf16[16,2,256]{2,1,0:T(2,128)(2,1)}), bf16[16,2,256]{2,1,0:T(2,128)(2,1)S(1)}, u32[]{:S(2)}, u32[]{:S(2)}) %all-to-all-start.1) | async-done | bytes 16416 | tf_op jit(solution)/shard_map/all_to_all | solution.py:297
  37.3 3.5 %all-to-all-start.2 = ((bf16[16,16,512]{2,1,0:T(8,128)(2,1)}), bf16[16,16,512]{2,1,0:T(8,128)(2,1)S(1)}, u32[]{:S(2)}, u32[]{:S(2)}) async-start(bf16[16,16,512]{2,1,0:T(8,128)(2,1)} %bitcast.39), calls=%async_computation.2 | async-start | bytes 524288 | tf_op jit(solution)/shard_map/all_to_all | solution.py:282
  41.5 0.1 eq.57
  41.6 1.6 %copy-done.1 = bf16[1024,1024]{1,0:T(8,128)(2,1)S(1)} copy-done((bf16[1024,1024]{1,0:T(8,128)(2,1)S(1)}, bf16[1024,1024]{1,0:T(8,128)(2,1)}, u32[]{:S(2)}) %copy-start.1) | copy-done | bytes 2097176
  43.2 0.8 copy-done.4
  44.0 0.5 shard_map.162.kv_ref
  44.5 0.1 compare_convert_fusion.mask_ref
  44.6 0.0 copy-start.5
  44.6 0.0 copy-start.6
  44.6 0.0 copy-start.2
  44.6 0.0 copy-start.3
  44.6 0.0 copy-start.8
  44.6 5.0 %shard_map.158.qa_ref = f32[32,512]{1,0:T(8,128)S(1)} custom-call(s32[1]{0:T(128)} %bitcast.which, bf16[8,32,1024]{2,1,0:T(8,128)(2,1)S(1)} %all_to_all.40.x_ref, bf16[8,2,1024,512]{3,2,1,0:T(8,128)(2,1)} %bitcast.53), custom_call_target="tpu_custom_call" | custom-call | tf_op jit(solution)/shard_map/pallas_call | solution.py:48
  49.7 0.0 copy-start.7
  49.7 5.0 %shard_map.159.qb_ref = f32[32,512]{1,0:T(8,128)S(1)} custom-call(s32[1]{0:T(128)S(6)} %sub.9.which, bf16[8,32,1024]{2,1,0:T(8,128)(2,1)S(1)} %collective-permute-done.x_ref, bf16[8,2,1024,512]{3,2,1,0:T(8,128)(2,1)} %bitcast.54), custom_call_target="tpu_custom_call" | custom-call | tf_op jit(solution)/shard_map/pallas_call | solution.py:48
  54.6 0.1 reshape.78.ranks_ref
  54.7 0.0 all-to-all-done.2
  54.8 0.9 shard_map.163
  55.7 6.0 %all-to-all-start.3 = ((f32[16,2,1536]{2,1,0:T(2,128)}), f32[16,2,1536]{2,1,0:T(2,128)S(1)}, u32[]{:S(2)}, u32[]{:S(2)}) async-start(f32[16,2,1536]{2,1,0:T(2,128)} %shard_map.163), calls=%async_computation.3 | async-start | bytes 393216 | tf_op jit(solution)/shard_map/all_to_all | solution.py:316
  61.7 0.1 fusion
  61.8 0.1 pad_maximum_fusion.1
  61.9 8.8 %all-to-all-done.3.recv_ref = f32[16,2,1536]{2,1,0:T(2,128)S(1)} async-done(((f32[16,2,1536]{2,1,0:T(2,128)}), f32[16,2,1536]{2,1,0:T(2,128)S(1)}, u32[]{:S(2)}, u32[]{:S(2)}) %all-to-all-start.3) | async-done | bytes 196640 | tf_op jit(solution)/shard_map/all_to_all | solution.py:316
  70.7 2.2 %shard_map.164 = (f32[16,2,512]{2,1,0:T(2,128)}, f32[2,1024]{1,0:T(2,128)S(1)}) custom-call(s32[1]{0:T(128)} %copy.39.len_ref, f32[16,2,1536]{2,1,0:T(2,128)S(1)} %all-to-all-done.3.recv_ref, f32[32,128]{1,0:T(8,128)S(1)} %bitcast.49, f32[32,128]{1,0:T(8,128)S(1)} %bitcast.50, bf16[512,512]{1,0:T(8,128)(2,1)S(1)} %bitcast.45, bf16[512,512]{1,0:T(8,128)(2,1)S(1)} %bitcast.46), custom_call_target="tpu_custom_call" | custom-call | tf_op jit(solution)/shard_map/pallas_call | solution.py:330
  72.9 3.5 %all-to-all-start.4 = ((f32[16,2,512]{2,1,0:T(2,128)}), f32[16,2,512]{2,1,0:T(2,128)S(1)}, u32[]{:S(2)}, u32[]{:S(2)}) async-start(f32[16,2,512]{2,1,0:T(2,128)} %get-tuple-element.9), calls=%async_computation.4 | async-start | bytes 131072 | tf_op jit(solution)/shard_map/all_to_all | solution.py:346
  76.5 0.1 copy.30
  76.6 0.2 copy.37
  76.7 6.6 %all-to-all-done.4.ctx_ref = f32[16,2,512]{2,1,0:T(2,128)S(1)} async-done(((f32[16,2,512]{2,1,0:T(2,128)}), f32[16,2,512]{2,1,0:T(2,128)S(1)}, u32[]{:S(2)}, u32[]{:S(2)}) %all-to-all-start.4) | async-done | bytes 65568 | tf_op jit(solution)/shard_map/all_to_all | solution.py:346
  83.3 12.6 %all_to_all.41 = bf16[16,16,512]{2,1,0:T(8,128)(2,1)S(1)} all-to-all(bf16[16,16,512]{2,1,0:T(8,128)(2,1)S(1)} %bitcast.56), channel_id=1, replica_groups=mesh['groups'=2,'tp'=8,'sub'=2] {'tp','sub'}, dimensions={0} | all-to-all | bytes 524288 | tf_op jit(solution)/shard_map/all_to_all | solution.py:282
  95.9 0.2 shard_map.165
  96.2 6.6 %shard_map.167 = f32[8,32,1024]{2,1,0:T(8,128)S(1)} custom-call(s32[1]{0:T(128)S(6)} %sub.9.which, bf16[32,512]{1,0:T(8,128)(2,1)S(1)} %get-tuple-element.11.x_ref, bf16[512,16384]{1,0:T(8,128)(2,1)} %w_ref.5), custom_call_target="tpu_custom_call" | custom-call | tf_op jit(solution)/shard_map/pallas_call | solution.py:198
  102.8 0.0 collective-permute-start.1
  102.8 0.4 reshape.75
  103.2 1.1 constant_dynamic-slice_fusion.1
  104.4 0.3 copy.35
  104.7 0.6 collective-permute-start.2
  105.2 0.1 pad_add_fusion
  105.3 0.3 copy.36
  105.6 0.1 compare_convert_fusion.1.mask_ref
  105.7 0.7 reshape.79
  106.4 3.5 %all-to-all-start.6 = ((f32[16,1,512]{2,1,0:T(1,128)}), f32[16,1,512]{2,1,0:T(1,128)S(1)}, u32[]{:S(2)}, u32[]{:S(2)}) async-start(f32[16,1,512]{2,1,0:T(1,128)} %reshape.79), calls=%async_computation.6 | async-start | bytes 65536 | tf_op jit(solution)/shard_map/all_to_all | solution.py:356
  109.9 0.0 collective-permute-done.2
  110.0 6.6 %shard_map.166.a_ref = f32[8,32,1024]{2,1,0:T(8,128)S(1)} custom-call(s32[1]{0:T(128)} %bitcast.which, bf16[32,512]{1,0:T(8,128)(2,1)S(1)} %get-tuple-element.11.x_ref, bf16[512,16384]{1,0:T(8,128)(2,1)} %w_ref.5), custom_call_target="tpu_custom_call" | custom-call | tf_op jit(solution)/shard_map/pallas_call | solution.py:198
  116.6 0.0 all-to-all-done.6
  116.6 0.5 broadcast.32
  117.1 0.7 reduce
  117.8 0.1 reshape.80.parts_ref
  117.9 2.4 %shard_map.168 = bf16[8,32,1024]{2,1,0:T(8,128)(2,1)} custom-call(f32[8,32,1024]{2,1,0:T(8,128)S(1)} %shard_map.166.a_ref, f32[8,32,1024]{2,1,0:T(8,128)} %collective-permute-done.1.b_ref, f32[16,16,32]{2,1,0:T(8,128)S(1)} %reshape.80.parts_ref, f32[2,32]{1,0:T(2,128)S(1)} %compare_convert_fusion.1.mask_ref, bf16[8,32,1024]{2,1,0:T(8,128)(2,1)S(1)} %pad_maximum_fusion.up_ref), custom_call_target="tpu_custom_call" | custom-call | tf_op jit(solution)/shard_map/pallas_call | solution.py:362
  120.3 5.9 %all-to-all-start.7 = ((bf16[8,32,1024]{2,1,0:T(8,128)(2,1)}), bf16[8,32,1024]{2,1,0:T(8,128)(2,1)S(1)}, u32[]{:S(2)}, u32[]{:S(2)}) async-start(bf16[8,32,1024]{2,1,0:T(8,128)(2,1)} %shard_map.168), calls=%async_computation.7 | async-start | bytes 1048576 | tf_op jit(solution)/shard_map/all_to_all | solution.py:367
  126.2 0.6 convert_bitcast_fusion
  126.8 14.2 %all-to-all-done.7.x_ref = bf16[8,32,1024]{2,1,0:T(8,128)(2,1)S(1)} async-done(((bf16[8,32,1024]{2,1,0:T(8,128)(2,1)}), bf16[8,32,1024]{2,1,0:T(8,128)(2,1)S(1)}, u32[]{:S(2)}, u32[]{:S(2)}) %all-to-all-start.7) | async-done | bytes 524320 | tf_op jit(solution)/shard_map/all_to_all | solution.py:367
  141.0 0.7 shard_map.169
  (23 shorter events, 0.2 us)
Async XLA Ops:
  23.1 2.7 %collective-permute-start = (bf16[8,32,1024]{2,1,0:T(8,128)(2,1)S(1)}, bf16[8,32,1024]{2,1,0:T(8,128)(2,1)S(1)}, u32[]{:S(2)}, u32[]{:S(2)}) collective-permute-start(bf16[8,32,1024]{2,1,0:T(8,128)(2,1)S(1)} %all_to_all.40.x_ref), channel_id=1, source_target_pairs={{0,1},{1,0},{2,3},{3,2},{4,5},{5,4},{6,7},{7,6},{8,9},{9,8},{10,11... | collective-permute-start | bytes 1572872 | tf_op jit(solution)/shard_map/ppermute | solution.py:266
  24.1 1.4 copy-start
  27.0 10.3 %all-to-all-start.1 = ((bf16[16,2,256]{2,1,0:T(2,128)(2,1)}), bf16[16,2,256]{2,1,0:T(2,128)(2,1)S(1)}, u32[]{:S(2)}, u32[]{:S(2)}) async-start(bf16[16,2,256]{2,1,0:T(2,128)(2,1)} %reshape.77), calls=%async_computation.1 | async-start | bytes 32768 | tf_op jit(solution)/shard_map/all_to_all | solution.py:297
  37.3 17.5 %all-to-all-start.2 = ((bf16[16,16,512]{2,1,0:T(8,128)(2,1)}), bf16[16,16,512]{2,1,0:T(8,128)(2,1)S(1)}, u32[]{:S(2)}, u32[]{:S(2)}) async-start(bf16[16,16,512]{2,1,0:T(8,128)(2,1)} %bitcast.39), calls=%async_computation.2 | async-start | bytes 524288 | tf_op jit(solution)/shard_map/all_to_all | solution.py:282
  41.6 1.6 %copy-start.1 = (bf16[1024,1024]{1,0:T(8,128)(2,1)S(1)}, bf16[1024,1024]{1,0:T(8,128)(2,1)}, u32[]{:S(2)}) copy-start(bf16[1024,1024]{1,0:T(8,128)(2,1)} %w_ref.3) | copy-start | bytes 6291460
  43.2 0.8 copy-start.4
  44.6 10.2 %copy-start.5 = (bf16[1,16,512]{2,1,0:T(8,128)(2,1)S(1)}, bf16[1,16,512]{2,1,0:T(8,128)(2,1)}, u32[]{:S(2)}) copy-start(bf16[1,16,512]{2,1,0:T(8,128)(2,1)} %param.26) | copy-start | bytes 49156
  44.6 10.2 %copy-start.6 = (bf16[1,16,512]{2,1,0:T(8,128)(2,1)S(1)}, bf16[1,16,512]{2,1,0:T(8,128)(2,1)}, u32[]{:S(2)}) copy-start(bf16[1,16,512]{2,1,0:T(8,128)(2,1)} %param.27) | copy-start | bytes 49156
  44.6 26.1 %copy-start.2 = (bf16[1,512,512]{2,1,0:T(8,128)(2,1)S(1)}, bf16[1,512,512]{2,1,0:T(8,128)(2,1)}, u32[]{:S(2)}) copy-start(bf16[1,512,512]{2,1,0:T(8,128)(2,1)} %param.19) | copy-start | bytes 1572868
  44.6 26.1 %copy-start.3 = (bf16[1,512,512]{2,1,0:T(8,128)(2,1)S(1)}, bf16[1,512,512]{2,1,0:T(8,128)(2,1)}, u32[]{:S(2)}) copy-start(bf16[1,512,512]{2,1,0:T(8,128)(2,1)} %param.20) | copy-start | bytes 1572868
  44.6 31.8 %copy-start.8 = (bf16[1,16,8192]{2,1,0:T(8,128)(2,1)S(1)}, bf16[1,16,8192]{2,1,0:T(8,128)(2,1)}, u32[]{:S(2)}) copy-start(bf16[1,16,8192]{2,1,0:T(8,128)(2,1)} %param.28) | copy-start | bytes 786436
  49.7 53.2 %copy-start.7 = (bf16[1,16,16384]{2,1,0:T(8,128)(2,1)S(1)}, bf16[1,16,16384]{2,1,0:T(8,128)(2,1)}, u32[]{:S(2)}) copy-start(bf16[1,16,16384]{2,1,0:T(8,128)(2,1)} %param.29) | copy-start | bytes 1572868
  55.7 15.0 %all-to-all-start.3 = ((f32[16,2,1536]{2,1,0:T(2,128)}), f32[16,2,1536]{2,1,0:T(2,128)S(1)}, u32[]{:S(2)}, u32[]{:S(2)}) async-start(f32[16,2,1536]{2,1,0:T(2,128)} %shard_map.163), calls=%async_computation.3 | async-start | bytes 393216 | tf_op jit(solution)/shard_map/all_to_all | solution.py:316
  72.9 10.4 %all-to-all-start.4 = ((f32[16,2,512]{2,1,0:T(2,128)}), f32[16,2,512]{2,1,0:T(2,128)S(1)}, u32[]{:S(2)}, u32[]{:S(2)}) async-start(f32[16,2,512]{2,1,0:T(2,128)} %get-tuple-element.9), calls=%async_computation.4 | async-start | bytes 131072 | tf_op jit(solution)/shard_map/all_to_all | solution.py:346
  102.8 15.1 %collective-permute-start.1 = (f32[8,32,1024]{2,1,0:T(8,128)S(1)}, f32[8,32,1024]{2,1,0:T(8,128)}, u32[]{:S(2)}, u32[]{:S(2)}) collective-permute-start(f32[8,32,1024]{2,1,0:T(8,128)S(1)} %shard_map.167), channel_id=1, source_target_pairs={{0,1},{1,0},{2,3},{3,2},{4,5},{5,4},{6,7},{7,6},{8,9},{9,8},{10,11... | collective-permute-start | bytes 3145736 | tf_op jit(solution)/shard_map/ppermute | solution.py:360
  104.7 5.2 %collective-permute-start.2 = (bf16[8,16,1024]{2,1,0:T(8,128)(2,1)S(1)}, bf16[8,16,1024]{2,1,0:T(8,128)(2,1)S(1)}, u32[]{:S(2)}, u32[]{:S(2)}) collective-permute-start(bf16[8,16,1024]{2,1,0:T(8,128)(2,1)S(1)} %bitcast.59), channel_id=1, source_target_pairs={{0,1},{1,0},{2,3},{3,2},{4,5},{5,4},{6,7},{7,6},{8,9},{9,8},{10,11... | collective-permute-start | bytes 786440 | tf_op jit(solution)/shard_map/ppermute | solution.py:289
  106.4 10.2 %all-to-all-start.6 = ((f32[16,1,512]{2,1,0:T(1,128)}), f32[16,1,512]{2,1,0:T(1,128)S(1)}, u32[]{:S(2)}, u32[]{:S(2)}) async-start(f32[16,1,512]{2,1,0:T(1,128)} %reshape.79), calls=%async_computation.6 | async-start | bytes 65536 | tf_op jit(solution)/shard_map/all_to_all | solution.py:356
  120.3 20.7 %all-to-all-start.7 = ((bf16[8,32,1024]{2,1,0:T(8,128)(2,1)}), bf16[8,32,1024]{2,1,0:T(8,128)(2,1)S(1)}, u32[]{:S(2)}, u32[]{:S(2)}) async-start(bf16[8,32,1024]{2,1,0:T(8,128)(2,1)} %shard_map.168), calls=%async_computation.7 | async-start | bytes 1048576 | tf_op jit(solution)/shard_map/all_to_all | solution.py:367

commit v2 on v1

v2 whole, which is shorter than its diff:
```python
import functools
import math

import jax
import jax.numpy as jnp
from jax import lax
from jax.experimental import pallas as pl
from jax.experimental.pallas import tpu as pltpu
from jax.sharding import PartitionSpec as P

HEAD_WIDTH = 128
ROPE_BASE = 500000.0
MASKED = -1e30
SCALE = 0.5
F32 = jnp.float32
BF16 = jnp.bfloat16

PARAMS = pltpu.CompilerParams(vmem_limit_bytes=16 * 1024 * 1024)


def nn(a, b):
    return lax.dot_general(a, b, (((1,), (0,)), ((), ())), preferred_element_type=F32)


def nt(a, b):
    return lax.dot_general(a, b, (((1,), (1,)), ((), ())), preferred_element_type=F32)


def tn(a, b):
    return lax.dot_general(a, b, (((0,), (0,)), ((), ())), preferred_element_type=F32)


VMEM = pl.BlockSpec(memory_space=pltpu.VMEM)
SMEM = pl.BlockSpec(memory_space=pltpu.SMEM)
ANY = pl.BlockSpec(memory_space=pl.ANY)


def device_at(at_ref, chips, k, sign):
    dt, ds = k // 2, k % 2
    tp = lax.rem(at_ref[0] + chips + sign * dt, chips)
    core = at_ref[1] if ds == 0 else 1 - at_ref[1]
    return 2 * tp + core


def chip_at(at_ref, chips, k, flip):
    lines = chips // 2
    z = lax.rem(at_ref[0] // 2 + lines - k, lines)
    y = lax.rem(at_ref[0], 2)
    return 2 * z + (1 - y if flip else y)


def piece_at(at_ref, chips, k, flip, cross):
    core = 1 - at_ref[1] if cross else at_ref[1]
    return 2 * chip_at(at_ref, chips, k, flip) + core


def query_kernel(flip, cross, chips, *refs):
    at_ref, w_ref = refs[0], refs[1]
    pieces = refs[2:-3]
    q_ref, w_s, sems = refs[-3:]
    width = pieces[0].shape[1]
    copies = []
    for k in range(len(pieces)):
        start = pl.multiple_of(piece_at(at_ref, chips, k, flip, cross) * width, width)
        copy = pltpu.make_async_copy(w_ref.at[pl.ds(start, width)], w_s.at[k], sems.at[k])
        copy.start()
        copies.append(copy)
    total = None
    for k, piece in enumerate(pieces):
        copies[k].wait()
        part = nn(piece[...], w_s[k])
        total = part if total is None else total + part
    q_ref[...] = total


def query_pieces(at, weight, pieces, chips, flip, cross):
    rows, width = pieces[0].shape
    cols = weight.shape[1]
    return pl.pallas_call(
        functools.partial(query_kernel, flip, cross, chips),
        out_shape=jax.ShapeDtypeStruct((rows, cols), F32),
        in_specs=[SMEM, ANY] + [VMEM] * len(pieces),
        scratch_shapes=[
            pltpu.VMEM((len(pieces), width, cols), BF16),
            pltpu.SemaphoreType.DMA((len(pieces),)),
        ],
        compiler_params=PARAMS,
    )(at, weight, *pieces)


def rank_kernel(kinds, chips, *refs):
    at_ref, d_ref = refs[0], refs[1]
    pieces, r_ref = refs[2:-1], refs[-1]
    width = pieces[0].shape[1]
    total = None
    for (k, flip, cross), piece in zip(kinds, pieces):
        start = pl.multiple_of(piece_at(at_ref, chips, k, flip, cross) * width, width)
        part = nt(d_ref[:, pl.ds(start, width)], piece[...])
        total = part if total is None else total + part
    r_ref[...] = total


def rank_pieces(at, down, pieces, kinds, chips):
    return pl.pallas_call(
        functools.partial(rank_kernel, kinds, chips),
        out_shape=jax.ShapeDtypeStruct((down.shape[0], pieces[0].shape[0]), F32),
        in_specs=[SMEM] + [VMEM] * (1 + len(pieces)),
        compiler_params=PARAMS,
    )(at, down, *pieces)


def dense_kernel(x_ref, w_ref, o_ref):
    o_ref[...] = nn(x_ref[...], w_ref[...])


def dense(x, weight):
    return pl.pallas_call(
        dense_kernel,
        out_shape=jax.ShapeDtypeStruct((x.shape[0], weight.shape[1]), F32),
        compiler_params=PARAMS,
    )(x, weight)


def split_kernel(chips, at_ref, m_ref, dep_ref, *outs):
    cols = outs[0].shape[1]
    for k, out in enumerate(outs):
        start = pl.multiple_of(device_at(at_ref, chips, k, 1) * cols, cols)
        out[...] = m_ref[:, pl.ds(start, cols)]


def split_map(at, maps, dep, chips):
    rank, width = maps.shape
    devices = 2 * chips
    return pl.pallas_call(
        functools.partial(split_kernel, chips),
        out_shape=[jax.ShapeDtypeStruct((rank, width // devices), BF16)] * devices,
        in_specs=[SMEM, VMEM, ANY],
        compiler_params=PARAMS,
    )(at, maps, dep)


def other_half_kernel(at_ref, m_ref, o_ref):
    width = o_ref.shape[2]
    for c in range(o_ref.shape[0]):
        start = pl.multiple_of((2 * c + 1 - at_ref[1]) * width, width)
        o_ref[c] = m_ref[:, pl.ds(start, width)]


def finish_kernel(chips, *refs):
    devices = 2 * chips
    at_ref, mask_ref, own_ref, kv_ref, kup_ref, vup_ref = refs[:6]
    rest = refs[6:]
    ups, rest = rest[:devices], rest[devices:]
    ranks, rest = rest[:devices], rest[devices:]
    queries, rest = rest[: -devices - 1], rest[-devices - 1 :]
    outs, y_s = rest[:devices], rest[devices]
    rank = ranks[0].shape[0]
    cols = queries[0].shape[1]
    half = kup_ref.shape[1]
    steps = outs[0].shape[0]
    u = ranks[0][...].astype(F32)
    for r in ranks[1:]:
        u = u + r[...].astype(F32)
    query = queries[0][...]
    for q in queries[1:]:
        query = query + q[...]
    spread = []
    for k in range(devices):
        start = pl.multiple_of(device_at(at_ref, chips, k, -1) * rank, rank)
        spread.append(u * mask_ref[pl.ds(start, rank), :])
    spread = jnp.concatenate(spread, axis=0).astype(BF16)
    up = jnp.concatenate([m[...] for m in ups], axis=0)
    y_s[:, :cols] = query + SCALE * tn(spread, up)
    own = own_ref[...].astype(BF16)
    y_s[:, cols : cols + half] = kv_ref[:, :half] + SCALE * tn(own[:rank], kup_ref[...])
    y_s[:, cols + half :] = kv_ref[:, half:] + SCALE * tn(own[rank:], vup_ref[...])
    for k, out in enumerate(outs):
        dest = device_at(at_ref, chips, k, 1)
        for t in range(steps):
            out[t : t + 1, :] = y_s[pl.ds(t * devices + dest, 1), :]


def rope(v, cosine, sine):
    return v * cosine + pltpu.roll(v, HEAD_WIDTH // 2, 1) * sine


def attend_kernel(chips, *refs):
    devices = 2 * chips
    at_ref, len_ref, cos_ref, sin_ref, k_ref, v_ref = refs[:6]
    rest = refs[6:]
    arrived, rest = rest[:devices], rest[devices:]
    outs, rest = rest[:devices], rest[devices:]
    ent_ref, q_s, c_s, kn_s, vn_s = rest
    steps, cols = outs[0].shape
    slots, kv_cols = k_ref.shape
    kv_heads = kv_cols // HEAD_WIDTH
    per_device = cols // HEAD_WIDTH
    group = devices * per_device // kv_heads
    rows = group * steps
    score_scale = 1.0 / math.sqrt(HEAD_WIDTH)
    length = len_ref[0]
    kv = arrived[0][:, cols:]
    for a in arrived[1:]:
        kv = kv + a[:, cols:]
    for k, a in enumerate(arrived):
        first = device_at(at_ref, chips, k, -1) * (per_device * steps)
        for hh in range(per_device):
            for t in range(steps):
                q_s[pl.ds(first + hh * steps + t, 1), :] = a[t : t + 1, hh * HEAD_WIDTH : (hh + 1) * HEAD_WIDTH]
    cosine = cos_ref[...]
    sine = sin_ref[...]
    kn_s[...] = jnp.zeros_like(kn_s)
    vn_s[...] = jnp.zeros_like(vn_s)
    fresh = kn_s.shape[0]
    col_old = lax.broadcasted_iota(jnp.int32, (rows, slots), 1)
    col_new = lax.broadcasted_iota(jnp.int32, (rows, fresh), 1)
    step_new = lax.rem(lax.broadcasted_iota(jnp.int32, (rows, fresh), 0), steps)
    for k in range(kv_heads):
        lanes = slice(k * HEAD_WIDTH, (k + 1) * HEAD_WIDTH)
        value_lanes = slice(kv_cols + k * HEAD_WIDTH, kv_cols + (k + 1) * HEAD_WIDTH)
        query = q_s[k * rows : (k + 1) * rows, :].astype(BF16).astype(F32)
        query = rope(query, cosine, sine).astype(BF16)
        key_now = rope(kv[:, lanes], cosine[:steps], sine[:steps]).astype(BF16).astype(F32)
        value_now = kv[:, value_lanes].astype(BF16).astype(F32)
        ent_ref[:, lanes] = key_now
        ent_ref[:, value_lanes] = value_now
        kn_s[:steps, :] = key_now
        vn_s[:steps, :] = value_now
        old = nt(query, k_ref[:, lanes]) * score_scale
        old = jnp.where(col_old < length, old, MASKED)
        new = nt(query, kn_s[...].astype(BF16)) * score_scale
        new = jnp.where((col_new < steps) & (col_new <= step_new), new, MASKED)
        top = jnp.maximum(jnp.max(old, axis=1, keepdims=True), jnp.max(new, axis=1, keepdims=True))
        e_old = jnp.exp(old - top)
        e_new = jnp.exp(new - top)
        total = jnp.sum(e_old, axis=1, keepdims=True) + jnp.sum(e_new, axis=1, keepdims=True)
        p_old = (e_old / total).astype(BF16)
        p_new = (e_new / total).astype(BF16)
        out = nn(p_old, v_ref[:, lanes]) + nn(p_new, vn_s[...].astype(BF16))
        c_s[k * rows : (k + 1) * rows, :] = out.astype(BF16).astype(F32)
    for k, out in enumerate(outs):
        first = device_at(at_ref, chips, k, 1) * (per_device * steps)
        for hh in range(per_device):
            for t in range(steps):
                out[t : t + 1, hh * HEAD_WIDTH : (hh + 1) * HEAD_WIDTH] = c_s[pl.ds(first + hh * steps + t, 1), :]


def lower_kernel(chips, *refs):
    devices = 2 * chips
    at_ref, mask_ref = refs[:2]
    rest = refs[2:]
    lows, rest = rest[:devices], rest[devices:]
    arrived, rest = rest[:devices], rest[devices:]
    x_ref, part_ref, x_s = rest
    steps = arrived[0].shape[0]
    rank = part_ref.shape[0]
    for k, a in enumerate(arrived):
        source = device_at(at_ref, chips, k, -1)
        for t in range(steps):
            x_s[pl.ds(t * devices + source, 1), :] = a[t : t + 1, :]
    x = x_s[...].astype(BF16)
    x_ref[...] = x
    every = nt(jnp.concatenate([m[...] for m in lows], axis=0), x)
    part = None
    for k in range(devices):
        start = pl.multiple_of(device_at(at_ref, chips, k, -1) * rank, rank)
        one = every[k * rank : (k + 1) * rank] * mask_ref[pl.ds(start, rank), :]
        part = one if part is None else part + one
    part_ref[...] = part


def out_half_kernel(cross, at_ref, x_ref, w_ref, o_ref):
    width = o_ref.shape[2]
    core = 1 - at_ref[1] if cross else at_ref[1]
    x = x_ref[...]
    for c in range(o_ref.shape[0]):
        start = pl.multiple_of((2 * c + core) * width, width)
        o_ref[c] = nn(x, w_ref[:, pl.ds(start, width)])


def out_half(at, x, weight, chips, cross):
    width = weight.shape[1] // (2 * chips)
    return pl.pallas_call(
        functools.partial(out_half_kernel, cross),
        out_shape=jax.ShapeDtypeStruct((chips, x.shape[0], width), F32),
        in_specs=[SMEM, VMEM, VMEM],
        compiler_params=PARAMS,
    )(at, x, weight)


def pair_kernel(chips, *refs):
    devices = 2 * chips
    at_ref, a_ref, b_ref, mask_ref, up_ref, other_ref = refs[:6]
    parts, outs = refs[6 : 6 + devices], refs[6 + devices :]
    width = outs[0].shape[1]
    u = parts[0][...]
    for p in parts[1:]:
        u = u + p[...]
    u = u.astype(BF16).astype(F32)
    spread = jnp.concatenate([u * mask_ref[0:1, :], u * mask_ref[1:2, :]], axis=0).astype(BF16)
    for k, out in enumerate(outs):
        dest = lax.rem(at_ref[0] + k, chips)
        start = pl.multiple_of((2 * dest + at_ref[1]) * width, width)
        up = jnp.concatenate([up_ref[:, pl.ds(start, width)], other_ref[dest]], axis=0)
        out[...] = (a_ref[dest] + b_ref[dest] + SCALE * tn(spread, up)).astype(BF16)


def total_kernel(*refs):
    total = refs[0][...].astype(F32)
    for r in refs[1:-1]:
        total = total + r[...].astype(F32)
    refs[-1][...] = total.astype(BF16)


def body(
    tokens,
    query_weight,
    key_value_weight,
    output_weight,
    cached_rotated_keys,
    cached_values,
    lengths,
    request_adapter,
    adapter_pool_slot,
    adapter_down_maps,
    query_up_maps,
    key_up_maps,
    value_up_maps,
    result_lowering_factors,
    output_up_maps,
):
    both = ("tp", "sub")
    chips = lax.axis_size("tp")
    devices = lax.axis_size(both)
    lines = chips // 2
    me = lax.axis_index(both)
    core = lax.axis_index("sub")
    steps, requests, width = tokens.shape
    rows = steps * requests
    cols = query_weight.shape[1]
    rank = key_up_maps.shape[1]
    assert devices == 2 * chips and chips % 2 == 0
    assert adapter_down_maps.shape[0] == 1 and requests == devices and cached_values.shape[0] == 1
    at = jnp.stack([lax.axis_index("tp"), core]).astype(jnp.int32)

    def swap_core(v):
        return lax.ppermute(v, "sub", [(0, 1), (1, 0)])

    def swap_y(v):
        return lax.ppermute(v, "tp", [(i, i ^ 1) for i in range(chips)])

    def shift_z(v, k):
        return lax.ppermute(v, "tp", [(i, (i + 2 * k) % chips) for i in range(chips)])

    def shift(v, k):
        if k == 0:
            return v
        return lax.ppermute(
            v, both, [(i, (i // 2 + k // 2) % chips * 2 + (i % 2 ^ k % 2)) for i in range(devices)]
        )

    few = devices <= 16
    places = jnp.arange(devices, dtype=jnp.int32)

    def place(sign):
        return (at[0] + sign * (places // 2)) % chips * 2 + (core ^ places % 2)

    def exchange(pieces):
        if few:
            return [shift(v, k) for k, v in enumerate(pieces)]
        stacked = jnp.stack(pieces)
        sent = jnp.zeros_like(stacked).at[place(1)].set(stacked)
        return list(lax.all_to_all(sent, both, 0, 0, tiled=True)[place(-1)])

    def spread_all(v):
        if few:
            return [shift(v, k) for k in range(devices)]
        return list(lax.all_gather(v, both)[place(-1)])

    x = tokens.reshape(rows, width)
    line = [x] + [shift_z(x, k) for k in range(1, lines)]
    across = [swap_y(v) for v in line]
    line_cross = [swap_core(v) for v in line]
    across_cross = [swap_core(v) for v in across]

    kv = dense(x, key_value_weight)

    index = jnp.arange(devices, dtype=jnp.int32)
    slot = jnp.sum(
        jnp.where(request_adapter[:, None] == index[None, :], adapter_pool_slot[None, :], 0), axis=1
    )
    row_slot = jnp.tile(slot, steps)[None, :]
    spread_mask = (jnp.repeat(index, rank)[:, None] == row_slot).astype(F32)
    own_mask = (row_slot == me).astype(F32)
    pair_mask = (jnp.stack([me, me + 1 - 2 * core])[:, None] == row_slot).astype(F32)

    ups = exchange(split_map(at, query_up_maps[0], line[-1], chips))

    up_other = swap_core(
        pl.pallas_call(
            other_half_kernel,
            out_shape=jax.ShapeDtypeStruct((chips, rank, width), BF16),
            in_specs=[SMEM, VMEM],
            compiler_params=PARAMS,
        )(at, output_up_maps[0])
    )

    down = adapter_down_maps[0]
    order = range(lines)
    early = rank_pieces(
        at,
        down,
        line + across + line_cross,
        [(k, False, False) for k in order] + [(k, True, False) for k in order] + [(k, False, True) for k in order],
        chips,
    )
    late = rank_pieces(at, down, across_cross, [(k, True, True) for k in order], chips)
    rank_all = (early + late).astype(BF16).astype(F32) * own_mask
    ranks = spread_all(rank_all[:rank].astype(BF16))
    queries = [
        query_pieces(at, query_weight, line, chips, False, False),
        query_pieces(at, query_weight, across, chips, True, False),
        query_pieces(at, query_weight, line_cross, chips, False, True),
        query_pieces(at, query_weight, across_cross, chips, True, True),
    ]
    to_rows = pl.pallas_call(
        functools.partial(finish_kernel, chips),
        out_shape=[jax.ShapeDtypeStruct((steps, cols + kv.shape[1]), F32)] * devices,
        in_specs=[SMEM] + [VMEM] * (5 + 2 * devices + len(queries)),
        scratch_shapes=[pltpu.VMEM((rows, cols + kv.shape[1]), F32)],
        compiler_params=PARAMS,
    )(at, spread_mask, rank_all[rank:], kv, key_up_maps[0], value_up_maps[0], *ups, *ranks, *queries)
    arrived = exchange(to_rows)

    lows = exchange(split_map(at, result_lowering_factors[0], ranks[-1], chips))

    kv_cols = key_value_weight.shape[1] // 2
    half_width = HEAD_WIDTH // 2
    frequency = ROPE_BASE ** (-2.0 * jnp.arange(half_width, dtype=F32) / HEAD_WIDTH)
    positions = lengths[0] + jnp.arange(steps, dtype=jnp.int32)
    angles = positions.astype(F32)[:, None] * frequency
    cosine, sine = jnp.cos(angles), jnp.sin(angles)
    heads = devices * cols // HEAD_WIDTH
    group = devices * cols // kv_cols
    cosine = jnp.tile(jnp.concatenate([cosine, cosine], axis=1), (group, 1))
    sine = jnp.tile(jnp.concatenate([-sine, sine], axis=1), (group, 1))
    results = pl.pallas_call(
        functools.partial(attend_kernel, chips),
        out_shape=[jax.ShapeDtypeStruct((steps, cols), F32)] * devices
        + [jax.ShapeDtypeStruct((steps, 2 * kv_cols), F32)],
        in_specs=[SMEM, SMEM] + [VMEM] * (4 + devices),
        scratch_shapes=[
            pltpu.VMEM((heads * steps, HEAD_WIDTH), F32),
            pltpu.VMEM((heads * steps, HEAD_WIDTH), F32),
            pltpu.VMEM((16, HEAD_WIDTH), F32),
            pltpu.VMEM((16, HEAD_WIDTH), F32),
        ],
        compiler_params=PARAMS,
    )(at, lengths, cosine, sine, cached_rotated_keys[0], cached_values[0], *arrived)
    entries = results[-1].astype(BF16)[:, None, :]

    by_head = exchange(results[:-1])
    lhs, part = pl.pallas_call(
        functools.partial(lower_kernel, chips),
        out_shape=(
            jax.ShapeDtypeStruct((rows, cols), BF16),
            jax.ShapeDtypeStruct((rank, rows), F32),
        ),
        in_specs=[SMEM] + [VMEM] * (1 + 2 * devices),
        scratch_shapes=[pltpu.VMEM((rows, cols), F32)],
        compiler_params=PARAMS,
    )(at, spread_mask, *lows, *by_head)
    parts = spread_all(part)
    out_there = out_half(at, lhs, output_weight, chips, True)
    received = swap_core(out_there)
    out_here = out_half(at, lhs, output_weight, chips, False)
    chip_totals = pl.pallas_call(
        functools.partial(pair_kernel, chips),
        out_shape=[jax.ShapeDtypeStruct((rows, width), BF16)] * chips,
        in_specs=[SMEM] + [VMEM] * (5 + devices),
        compiler_params=PARAMS,
    )(at, out_here, received, pair_mask, output_up_maps[0], up_other, *parts)
    pieces = [shift(v, 2 * k) for k, v in enumerate(chip_totals)]
    attended = pl.pallas_call(
        total_kernel,
        out_shape=jax.ShapeDtypeStruct((rows, width), BF16),
        compiler_params=PARAMS,
    )(*pieces)
    return attended.reshape(steps, requests, width), entries


def solution(mesh):
    placed = (
        P(None, "groups", ("tp", "sub")),
        P(None, ("tp", "sub")),
        P(("tp", "sub"), None),
        P(("tp", "sub"), None),
        P(("groups", "tp", "sub"), None, None),
        P(("groups", "tp", "sub"), None, None),
        P(("groups", "tp", "sub")),
        P("groups"),
        P(),
        P(("tp", "sub"), None, None),
        P(("tp", "sub"), None, None),
        P(("tp", "sub"), None, None),
        P(("tp", "sub"), None, None),
        P(("tp", "sub"), None, None),
        P(("tp", "sub"), None, None),
    )
    return jax.shard_map(
        body,
        mesh=mesh,
        in_specs=placed,
        out_specs=(P(None, "groups", ("tp", "sub")), P(None, ("groups", "tp", "sub"), None)),
        check_vma=False,
    )
```

time: 143 us -> 203 us (1.42)
  starting transfers between devices: 26.8 us -> 139 us
  blocking collectives: 34.2 us -> 0 us
  waiting for transfers between devices: 34.2 us -> 19 us
  Pallas kernels: 30.8 us -> 21.2 us
  local copies, waits for them, and re-layouts: 11.4 us -> 18.3 us
    ppermute x3 -> x114, starting transfers between devices: 0.59 us -> 139 us  [the longest x97 128 us: shift(): lax.ppermute(v, both, [(i, (i // 2 + k // 2) % chips * 2 + (i % 2 ^ k % 2...]
    all_to_all x2 -> x0, blocking collectives: 34.2 us -> none  [the longest x1 21.6 us: body(): mine = lax.all_to_all(copies, 'tp', 0, 0, tiled=True)]
    all_to_all x6 -> x0, waiting for transfers between devices: 34.2 us -> none  [the longest x1 14.2 us: body(): pieces = lax.all_to_all(chip_total, 'tp', 0, 0, tiled=True)]
    all_to_all x6 -> x0, starting transfers between devices: 26.2 us -> none  [the longest x1 5.98 us: body(): arrived = lax.all_to_all(to_rows, both, 0, 0, tiled=True)]
    ppermute x3 -> x114, waiting for transfers between devices: 0.01 us -> 19 us  [the longest x97 14.7 us: shift(): lax.ppermute(v, both, [(i, (i // 2 + k // 2) % chips * 2 + (i % 2 ^ k % 2...]
    unnamed x26 -> x36, local copies, waits for them, and re-layouts: 7.22 us -> 18.1 us
    pallas_call x10 -> x15, Pallas kernels: 29.6 us -> 20 us  [the longest x4 7.32 us: query_pieces(): pl.pallas_call(functools.partial(query_kernel, flip, cross, chips), out_s...]
  transfers between devices with their start and end apart: 9 -> 114, of which waited for: 4 -> 24; matrix products, arithmetic and copies ran while one was open for 6% -> 1% of each run, Pallas kernels for 12% -> 7%
where the time goes in v2:
time: 203 us; the launch traced here: 202 us
  starting transfers between devices  139 us (68%)
  Pallas kernels  21.2 us (10%)
  waiting for transfers between devices  19 us (9%)
  local copies, waits for them, and re-layouts  18.3 us (9%)
    ppermute x97, starting transfers between devices, shift(): lax.ppermute(v, both, [(i, (i // 2 + k // 2) % chips * 2 + (i % 2 ^ k % 2...  128 us
    unnamed x36, local copies, waits for them, and re-layouts  18.1 us
    ppermute x97, waiting for transfers between devices, shift(): lax.ppermute(v, both, [(i, (i // 2 + k // 2) % chips * 2 + (i % 2 ^ k % 2...  14.7 us
    pallas_call x4, Pallas kernels, query_pieces(): pl.pallas_call(functools.partial(query_kernel, flip, cross, chips), out_s...  7.32 us
    ppermute x3, starting transfers between devices, shift_z(): lax.ppermute(v, 'tp', [(i, (i + 2 * k) % chips) for i in range(chips)])  6.11 us
    ppermute x4, starting transfers between devices, swap_y(): return lax.ppermute(v, 'tp', [(i, i ^ 1) for i in range(chips)])  4.2 us
    pallas_call x2, Pallas kernels, out_half(): pl.pallas_call(functools.partial(out_half_kernel, cross), out_shape=jax.S...  4.2 us
  transfers between devices with their start and end apart: 114, of which 24 were waited for; matrix products, arithmetic and copies ran while one was open for 1% of the time, Pallas kernels for 7%

profile of v2, /device:TPU:0, one launch (start us, length us, event | category | flops | bytes accessed | tf_op | source)
XLA Modules:
  0.0 201.6 jit_solution(4796000890960055503)
XLA Ops:
  0.6 5.1 %collective-permute-start.2 = (bf16[32,1024]{1,0:T(8,128)(2,1)}, bf16[32,1024]{1,0:T(8,128)(2,1)S(1)}, u32[]{:S(2)}, u32[]{:S(2)}) collective-permute-start(bf16[32,1024]{1,0:T(8,128)(2,1)} %bitcast.26), channel_id=1, source_target_pairs={{0,12},{2,14},{4,0},{6,2},{8,4},{10,6},{12,8},{14,10},{1,13},{3,15... | collective-permute-start | bytes 196616 | tf_op jit(solution)/shard_map/ppermute | solution.py:353
  6.7 1.5 collective-permute-start.3
  10.5 1.6 collective-permute-done.refs_3_
  12.1 1.5 collective-permute-start.32
  14.7 1.7 collective-permute-start.35
  16.5 1.5 collective-permute-start.6
  22.1 1.7 collective-permute-done.4.refs_7_.refs_3_
  26.1 1.4 collective-permute-start.36
  28.3 1.8 collective-permute-start.38
  30.0 1.3 collective-permute-start.39
  31.3 2.4 %collective-permute-start.40 = (bf16[16,512]{1,0:T(8,128)(2,1)S(1)}, bf16[16,512]{1,0:T(8,128)(2,1)S(1)}, u32[]{:S(2)}, u32[]{:S(2)}) collective-permute-start(bf16[16,512]{1,0:T(8,128)(2,1)S(1)} %get-tuple-element.103), channel_id=1, source_target_pairs={{0,10},{1,11},{2,12},{3,13},{4,14},{5,15},{6,0},{7,1},{8,2},{9,3},... | collective-permute-start | bytes 49160 | tf_op jit(solution)/shard_map/ppermute | solution.py:358
  33.7 1.4 copy-done.2
  38.7 2.2 %collective-permute-start.42 = (bf16[16,512]{1,0:T(8,128)(2,1)S(1)}, bf16[16,512]{1,0:T(8,128)(2,1)S(1)}, u32[]{:S(2)}, u32[]{:S(2)}) collective-permute-start(bf16[16,512]{1,0:T(8,128)(2,1)S(1)} %get-tuple-element.105), channel_id=1, source_target_pairs={{0,12},{1,13},{2,14},{3,15},{4,0},{5,1},{6,2},{7,3},{8,4},{9,5},{1... | collective-permute-start | bytes 49160 | tf_op jit(solution)/shard_map/ppermute | solution.py:358
  40.9 2.8 %collective-permute-start.43 = (bf16[16,512]{1,0:T(8,128)(2,1)S(1)}, bf16[16,512]{1,0:T(8,128)(2,1)S(1)}, u32[]{:S(2)}, u32[]{:S(2)}) collective-permute-start(bf16[16,512]{1,0:T(8,128)(2,1)S(1)} %get-tuple-element.106), channel_id=1, source_target_pairs={{0,13},{1,12},{2,15},{3,14},{4,1},{5,0},{6,3},{7,2},{8,5},{9,4},{1... | collective-permute-start | bytes 49160 | tf_op jit(solution)/shard_map/ppermute | solution.py:358
  44.9 2.5 %collective-permute-start.15 = (bf16[16,32]{1,0:T(8,128)(2,1)S(1)}, bf16[16,32]{1,0:T(8,128)(2,1)S(1)}, u32[]{:S(2)}, u32[]{:S(2)}) collective-permute-start(bf16[16,32]{1,0:T(8,128)(2,1)S(1)} %slice.12.refs_22_), channel_id=1, source_target_pairs={{0,15},{1,14},{2,1},{3,0},{4,3},{5,2},{6,5},{7,4},{8,7},{9,6},{10,... | collective-permute-start | bytes 3080 | tf_op jit(solution)/shard_map/ppermute | solution.py:358
  49.2 1.4 collective-permute-start.50
  50.7 2.3 %collective-permute-start.51 = (bf16[16,32]{1,0:T(8,128)(2,1)S(1)}, bf16[16,32]{1,0:T(8,128)(2,1)S(1)}, u32[]{:S(2)}, u32[]{:S(2)}) collective-permute-start(bf16[16,32]{1,0:T(8,128)(2,1)S(1)} %slice.12.refs_22_), channel_id=1, source_target_pairs={{0,6},{1,7},{2,8},{3,9},{4,10},{5,11},{6,12},{7,13},{8,14},{9,15},... | collective-permute-start | bytes 3080 | tf_op jit(solution)/shard_map/ppermute | solution.py:358
  54.0 3.0 %collective-permute-start.53 = (bf16[16,32]{1,0:T(8,128)(2,1)S(1)}, bf16[16,32]{1,0:T(8,128)(2,1)S(1)}, u32[]{:S(2)}, u32[]{:S(2)}) collective-permute-start(bf16[16,32]{1,0:T(8,128)(2,1)S(1)} %slice.12.refs_22_), channel_id=1, source_target_pairs={{0,8},{1,9},{2,10},{3,11},{4,12},{5,13},{6,14},{7,15},{8,0},{9,1},... | collective-permute-start | bytes 3080 | tf_op jit(solution)/shard_map/ppermute | solution.py:358
  57.2 2.9 %collective-permute-start.55 = (bf16[16,32]{1,0:T(8,128)(2,1)S(1)}, bf16[16,32]{1,0:T(8,128)(2,1)S(1)}, u32[]{:S(2)}, u32[]{:S(2)}) collective-permute-start(bf16[16,32]{1,0:T(8,128)(2,1)S(1)} %slice.12.refs_22_), channel_id=1, source_target_pairs={{0,10},{1,11},{2,12},{3,13},{4,14},{5,15},{6,0},{7,1},{8,2},{9,3},... | collective-permute-start | bytes 3080 | tf_op jit(solution)/shard_map/ppermute | solution.py:358
  60.3 1.7 collective-permute-start.57
  62.0 3.3 %collective-permute-start.58 = (bf16[16,32]{1,0:T(8,128)(2,1)S(1)}, bf16[16,32]{1,0:T(8,128)(2,1)S(1)}, u32[]{:S(2)}, u32[]{:S(2)}) collective-permute-start(bf16[16,32]{1,0:T(8,128)(2,1)S(1)} %slice.12.refs_22_), channel_id=1, source_target_pairs={{0,13},{1,12},{2,15},{3,14},{4,1},{5,0},{6,3},{7,2},{8,5},{9,4},{1... | collective-permute-start | bytes 3080 | tf_op jit(solution)/shard_map/ppermute | solution.py:358
  65.4 1.6 copy-done.3
  69.0 5.8 %copy-done = bf16[16384,512]{1,0:T(8,128)(2,1)S(1)} copy-done((bf16[16384,512]{1,0:T(8,128)(2,1)S(1)}, bf16[16384,512]{1,0:T(8,128)(2,1)}, u32[]{:S(2)}) %copy-start) | copy-done | bytes 16777240
  75.6 1.8 shard_map.163.refs_38_
  77.4 1.8 shard_map.164.refs_39_
  79.4 1.8 shard_map.165.refs_40_
  81.2 1.8 shard_map.166.refs_41_
  84.2 2.0 collective-permute-start.61
  87.1 4.3 %collective-permute-start.65 = (f32[2,1536]{1,0:T(2,128)S(1)}, f32[2,1536]{1,0:T(2,128)S(1)}, u32[]{:S(2)}, u32[]{:S(2)}) collective-permute-start(f32[2,1536]{1,0:T(2,128)S(1)} %get-tuple-element.115), channel_id=1, source_target_pairs={{0,6},{1,7},{2,8},{3,9},{4,10},{5,11},{6,12},{7,13},{8,14},{9,15},... | collective-permute-start | bytes 36872 | tf_op jit(solution)/shard_map/ppermute | solution.py:358
  92.0 1.7 collective-permute-start.67
  94.4 3.2 %collective-permute-start.69 = (f32[2,1536]{1,0:T(2,128)S(1)}, f32[2,1536]{1,0:T(2,128)S(1)}, u32[]{:S(2)}, u32[]{:S(2)}) collective-permute-start(f32[2,1536]{1,0:T(2,128)S(1)} %get-tuple-element.119), channel_id=1, source_target_pairs={{0,10},{1,11},{2,12},{3,13},{4,14},{5,15},{6,0},{7,1},{8,2},{9,3},... | collective-permute-start | bytes 36872 | tf_op jit(solution)/shard_map/ppermute | solution.py:358
  97.9 1.9 collective-permute-start.71
  99.8 2.6 %collective-permute-start.72 = (f32[2,1536]{1,0:T(2,128)S(1)}, f32[2,1536]{1,0:T(2,128)S(1)}, u32[]{:S(2)}, u32[]{:S(2)}) collective-permute-start(f32[2,1536]{1,0:T(2,128)S(1)} %get-tuple-element.122), channel_id=1, source_target_pairs={{0,13},{1,12},{2,15},{3,14},{4,1},{5,0},{6,3},{7,2},{8,5},{9,4},{1... | collective-permute-start | bytes 36872 | tf_op jit(solution)/shard_map/ppermute | solution.py:358
  103.8 2.3 %collective-permute-done.73.refs_20_ = f32[2,1536]{1,0:T(2,128)S(1)} collective-permute-done((f32[2,1536]{1,0:T(2,128)S(1)}, f32[2,1536]{1,0:T(2,128)S(1)}, u32[]{:S(2)}, u32[]{:S(2)}) %collective-permute-start.73) | collective-permute-done | bytes 12320 | tf_op jit(solution)/shard_map/ppermute | solution.py:358
  106.3 2.3 %shard_map.168 = (f32[2,512]{1,0:T(2,128)S(1)}, f32[2,512]{1,0:T(2,128)S(1)}, f32[2,512]{1,0:T(2,128)S(1)}, f32[2,512]{1,0:T(2,128)S(1)}, f32[2,512]{1,0:T(2,128...) custom-call(s32[2]{0:T(128)S(1)} %pad_add_fusion.refs_0_.at_ref, ...), custom_call_target="tpu_custom_call" | custom-call | tf_op jit(solution)/shard_map/pallas_call | solution.py:447
  108.8 2.1 %collective-permute-start.76 = (f32[2,512]{1,0:T(2,128)S(1)}, f32[2,512]{1,0:T(2,128)S(1)}, u32[]{:S(2)}, u32[]{:S(2)}) collective-permute-start(f32[2,512]{1,0:T(2,128)S(1)} %get-tuple-element.127), channel_id=1, source_target_pairs={{0,2},{1,3},{2,4},{3,5},{4,6},{5,7},{6,8},{7,9},{8,10},{9,11},{10,... | collective-permute-start | bytes 12296 | tf_op jit(solution)/shard_map/ppermute | solution.py:358
  112.2 4.2 %collective-permute-start.80 = (f32[2,512]{1,0:T(2,128)S(1)}, f32[2,512]{1,0:T(2,128)S(1)}, u32[]{:S(2)}, u32[]{:S(2)}) collective-permute-start(f32[2,512]{1,0:T(2,128)S(1)} %get-tuple-element.131), channel_id=1, source_target_pairs={{0,6},{1,7},{2,8},{3,9},{4,10},{5,11},{6,12},{7,13},{8,14},{9,15},... | collective-permute-start | bytes 12296 | tf_op jit(solution)/shard_map/ppermute | solution.py:358
  116.7 1.4 collective-permute-start.82
  119.1 3.4 %collective-permute-start.84 = (f32[2,512]{1,0:T(2,128)S(1)}, f32[2,512]{1,0:T(2,128)S(1)}, u32[]{:S(2)}, u32[]{:S(2)}) collective-permute-start(f32[2,512]{1,0:T(2,128)S(1)} %get-tuple-element.135), channel_id=1, source_target_pairs={{0,10},{1,11},{2,12},{3,13},{4,14},{5,15},{6,0},{7,1},{8,2},{9,3},... | collective-permute-start | bytes 12296 | tf_op jit(solution)/shard_map/ppermute | solution.py:358
  122.6 2.3 %collective-permute-start.86 = (f32[2,512]{1,0:T(2,128)S(1)}, f32[2,512]{1,0:T(2,128)S(1)}, u32[]{:S(2)}, u32[]{:S(2)}) collective-permute-start(f32[2,512]{1,0:T(2,128)S(1)} %get-tuple-element.137), channel_id=1, source_target_pairs={{0,12},{1,13},{2,14},{3,15},{4,0},{5,1},{6,2},{7,3},{8,4},{9,5},{1... | collective-permute-start | bytes 12296 | tf_op jit(solution)/shard_map/ppermute | solution.py:358
  124.8 1.9 collective-permute-start.87
  130.6 1.5 collective-permute-start.18
  133.2 2.8 %collective-permute-start.21 = (bf16[16,512]{1,0:T(8,128)(2,1)S(1)}, bf16[16,512]{1,0:T(8,128)(2,1)S(1)}, u32[]{:S(2)}, u32[]{:S(2)}) collective-permute-start(bf16[16,512]{1,0:T(8,128)(2,1)S(1)} %get-tuple-element.83), channel_id=1, source_target_pairs={{0,6},{1,7},{2,8},{3,9},{4,10},{5,11},{6,12},{7,13},{8,14},{9,15},... | collective-permute-start | bytes 49160 | tf_op jit(solution)/shard_map/ppermute | solution.py:358
  137.0 1.7 collective-permute-start.23
  138.7 1.3 collective-permute-start.24
  140.0 2.2 %collective-permute-start.25 = (bf16[16,512]{1,0:T(8,128)(2,1)S(1)}, bf16[16,512]{1,0:T(8,128)(2,1)S(1)}, u32[]{:S(2)}, u32[]{:S(2)}) collective-permute-start(bf16[16,512]{1,0:T(8,128)(2,1)S(1)} %get-tuple-element.87), channel_id=1, source_target_pairs={{0,10},{1,11},{2,12},{3,13},{4,14},{5,15},{6,0},{7,1},{8,2},{9,3},... | collective-permute-start | bytes 49160 | tf_op jit(solution)/shard_map/ppermute | solution.py:358
  143.2 1.5 collective-permute-start.27
  144.7 3.5 %collective-permute-start.28 = (bf16[16,512]{1,0:T(8,128)(2,1)S(1)}, bf16[16,512]{1,0:T(8,128)(2,1)S(1)}, u32[]{:S(2)}, u32[]{:S(2)}) collective-permute-start(bf16[16,512]{1,0:T(8,128)(2,1)S(1)} %get-tuple-element.90), channel_id=1, source_target_pairs={{0,13},{1,12},{2,15},{3,14},{4,1},{5,0},{6,3},{7,2},{8,5},{9,4},{1... | collective-permute-start | bytes 49160 | tf_op jit(solution)/shard_map/ppermute | solution.py:358
  148.2 1.2 collective-permute-start.30
  149.6 2.3 %collective-permute-done.29.refs_16_ = bf16[16,512]{1,0:T(8,128)(2,1)S(1)} collective-permute-done((bf16[16,512]{1,0:T(8,128)(2,1)S(1)}, bf16[16,512]{1,0:T(8,128)(2,1)S(1)}, u32[]{:S(2)}, u32[]{:S(2)}) %collective-permute-start.29) | collective-permute-done | bytes 16416 | tf_op jit(solution)/shard_map/ppermute | solution.py:358
  152.8 2.1 %shard_map.171 = f32[8,32,1024]{2,1,0:T(8,128)S(1)} custom-call(s32[2]{0:T(128)S(1)} %pad_add_fusion.refs_0_.at_ref, bf16[32,512]{1,0:T(8,128)(2,1)S(1)} %get-tuple-element.141.x_ref, bf16[512,16384]{1,0:T(8,128)(2,1)S(1)} %bitcast.21), custom_call_target="tpu_custom_call" | custom-call | tf_op jit(solution)/shard_map/pallas_call | solution.py:283
  155.0 4.7 %collective-permute-start.101 = (f32[16,32]{1,0:T(8,128)S(1)}, f32[16,32]{1,0:T(8,128)S(1)}, u32[]{:S(2)}, u32[]{:S(2)}) collective-permute-start(f32[16,32]{1,0:T(8,128)S(1)} %get-tuple-element.142.refs_6_), channel_id=1, source_target_pairs={{0,10},{1,11},{2,12},{3,13},{4,14},{5,15},{6,0},{7,1},{8,2},{9,3},... | collective-permute-start | bytes 6152 | tf_op jit(solution)/shard_map/ppermute | solution.py:358
  159.8 2.3 %collective-permute-start.103 = (f32[16,32]{1,0:T(8,128)S(1)}, f32[16,32]{1,0:T(8,128)S(1)}, u32[]{:S(2)}, u32[]{:S(2)}) collective-permute-start(f32[16,32]{1,0:T(8,128)S(1)} %get-tuple-element.142.refs_6_), channel_id=1, source_target_pairs={{0,12},{1,13},{2,14},{3,15},{4,0},{5,1},{6,2},{7,3},{8,4},{9,5},{1... | collective-permute-start | bytes 6152 | tf_op jit(solution)/shard_map/ppermute | solution.py:358
  163.0 2.1 %collective-permute-start.105 = (f32[16,32]{1,0:T(8,128)S(1)}, f32[16,32]{1,0:T(8,128)S(1)}, u32[]{:S(2)}, u32[]{:S(2)}) collective-permute-start(f32[16,32]{1,0:T(8,128)S(1)} %get-tuple-element.142.refs_6_), channel_id=1, source_target_pairs={{0,14},{1,15},{2,0},{3,1},{4,2},{5,3},{6,4},{7,5},{8,6},{9,7},{10,... | collective-permute-start | bytes 6152 | tf_op jit(solution)/shard_map/ppermute | solution.py:358
  168.9 1.5 collective-permute-start.95
  170.4 2.2 %collective-permute-done.93.refs_8_ = f32[16,32]{1,0:T(8,128)S(1)} collective-permute-done((f32[16,32]{1,0:T(8,128)S(1)}, f32[16,32]{1,0:T(8,128)S(1)}, u32[]{:S(2)}, u32[]{:S(2)}) %collective-permute-start.93) | collective-permute-done | bytes 2080 | tf_op jit(solution)/shard_map/ppermute | solution.py:358
  172.6 1.4 collective-permute-done.94.refs_9_
  174.3 3.0 %collective-permute-start.98 = (f32[16,32]{1,0:T(8,128)S(1)}, f32[16,32]{1,0:T(8,128)S(1)}, u32[]{:S(2)}, u32[]{:S(2)}) collective-permute-start(f32[16,32]{1,0:T(8,128)S(1)} %get-tuple-element.142.refs_6_), channel_id=1, source_target_pairs={{0,7},{1,6},{2,9},{3,8},{4,11},{5,10},{6,13},{7,12},{8,15},{9,14},... | collective-permute-start | bytes 6152 | tf_op jit(solution)/shard_map/ppermute | solution.py:358
  177.5 5.8 %copy-done.1 = bf16[512,16384]{1,0:T(8,128)(2,1)S(1)} copy-done((bf16[512,16384]{1,0:T(8,128)(2,1)S(1)}, bf16[512,16384]{1,0:T(8,128)(2,1)}, u32[]{:S(2)}) %copy-start.1) | copy-done | bytes 16777240
  183.3 2.1 %shard_map.170.refs_1_ = f32[8,32,1024]{2,1,0:T(8,128)S(1)} custom-call(s32[2]{0:T(128)S(1)} %pad_add_fusion.refs_0_.at_ref, bf16[32,512]{1,0:T(8,128)(2,1)S(1)} %get-tuple-element.141.x_ref, bf16[512,16384]{1,0:T(8,128)(2,1)S(1)} %copy-done.1), custom_call_target="tpu_custom_call" | custom-call | tf_op jit(solution)/shard_map/pallas_call | solution.py:283
  187.7 3.7 %collective-permute-start.109 = (bf16[32,1024]{1,0:T(8,128)(2,1)S(1)}, bf16[32,1024]{1,0:T(8,128)(2,1)S(1)}, u32[]{:S(2)}, u32[]{:S(2)}) collective-permute-start(bf16[32,1024]{1,0:T(8,128)(2,1)S(1)} %get-tuple-element.146), channel_id=1, source_target_pairs={{0,6},{1,7},{2,8},{3,9},{4,10},{5,11},{6,12},{7,13},{8,14},{9,15},... | collective-permute-start | bytes 196616 | tf_op jit(solution)/shard_map/ppermute | solution.py:358
  191.4 1.5 collective-permute-start.110
  194.0 2.1 %collective-permute-start.112 = (bf16[32,1024]{1,0:T(8,128)(2,1)S(1)}, bf16[32,1024]{1,0:T(8,128)(2,1)S(1)}, u32[]{:S(2)}, u32[]{:S(2)}) collective-permute-start(bf16[32,1024]{1,0:T(8,128)(2,1)S(1)} %get-tuple-element.149), channel_id=1, source_target_pairs={{0,12},{1,13},{2,14},{3,15},{4,0},{5,1},{6,2},{7,3},{8,4},{9,5},{1... | collective-permute-start | bytes 196616 | tf_op jit(solution)/shard_map/ppermute | solution.py:358
  196.2 2.9 %collective-permute-start.113 = (bf16[32,1024]{1,0:T(8,128)(2,1)S(1)}, bf16[32,1024]{1,0:T(8,128)(2,1)S(1)}, u32[]{:S(2)}, u32[]{:S(2)}) collective-permute-start(bf16[32,1024]{1,0:T(8,128)(2,1)S(1)} %get-tuple-element.150), channel_id=1, source_target_pairs={{0,14},{1,15},{2,0},{3,1},{4,2},{5,3},{6,4},{7,5},{8,6},{9,7},{10,... | collective-permute-start | bytes 196616 | tf_op jit(solution)/shard_map/ppermute | solution.py:358
  (238 shorter events, 49.1 us)
Async XLA Ops:
  0.6 7.9 %collective-permute-start.2 = (bf16[32,1024]{1,0:T(8,128)(2,1)}, bf16[32,1024]{1,0:T(8,128)(2,1)S(1)}, u32[]{:S(2)}, u32[]{:S(2)}) collective-permute-start(bf16[32,1024]{1,0:T(8,128)(2,1)} %bitcast.26), channel_id=1, source_target_pairs={{0,12},{2,14},{4,0},{6,2},{8,4},{10,6},{12,8},{14,10},{1,13},{3,15... | collective-permute-start | bytes 196616 | tf_op jit(solution)/shard_map/ppermute | solution.py:353
  5.7 7.9 %collective-permute-start.1 = (bf16[32,1024]{1,0:T(8,128)(2,1)}, bf16[32,1024]{1,0:T(8,128)(2,1)S(1)}, u32[]{:S(2)}, u32[]{:S(2)}) collective-permute-start(bf16[32,1024]{1,0:T(8,128)(2,1)} %bitcast.28), channel_id=1, source_target_pairs={{0,8},{2,10},{4,12},{6,14},{8,0},{10,2},{12,4},{14,6},{1,9},{3,11}... | collective-permute-start | bytes 196616 | tf_op jit(solution)/shard_map/ppermute | solution.py:353
  6.7 8.0 %collective-permute-start.3 = (bf16[32,1024]{1,0:T(8,128)(2,1)}, bf16[32,1024]{1,0:T(8,128)(2,1)S(1)}, u32[]{:S(2)}, u32[]{:S(2)}) collective-permute-start(bf16[32,1024]{1,0:T(8,128)(2,1)} %bitcast.29), channel_id=1, source_target_pairs={{0,2},{2,0},{4,6},{6,4},{8,10},{10,8},{12,14},{14,12},{1,3},{3,1},... | collective-permute-start | bytes 196616 | tf_op jit(solution)/shard_map/ppermute | solution.py:350
  8.3 6.5 %collective-permute-start.7 = (bf16[32,1024]{1,0:T(8,128)(2,1)}, bf16[32,1024]{1,0:T(8,128)(2,1)S(1)}, u32[]{:S(2)}, u32[]{:S(2)}) collective-permute-start(bf16[32,1024]{1,0:T(8,128)(2,1)} %bitcast.30), channel_id=1, source_target_pairs={{0,1},{1,0},{2,3},{3,2},{4,5},{5,4},{6,7},{7,6},{8,9},{9,8},{10,11... | collective-permute-start | bytes 196616 | tf_op jit(solution)/shard_map/ppermute | solution.py:347
  14.7 6.8 %collective-permute-start.35 = (bf16[16,512]{1,0:T(8,128)(2,1)S(1)}, bf16[16,512]{1,0:T(8,128)(2,1)S(1)}, u32[]{:S(2)}, u32[]{:S(2)}) collective-permute-start(bf16[16,512]{1,0:T(8,128)(2,1)S(1)} %get-tuple-element.98), channel_id=1, source_target_pairs={{0,5},{1,4},{2,7},{3,6},{4,9},{5,8},{6,11},{7,10},{8,13},{9,12},{1... | collective-permute-start | bytes 49160 | tf_op jit(solution)/shard_map/ppermute | solution.py:358
  24.6 6.7 %collective-permute-start.13 = (bf16[32,1024]{1,0:T(8,128)(2,1)S(1)}, bf16[32,1024]{1,0:T(8,128)(2,1)S(1)}, u32[]{:S(2)}, u32[]{:S(2)}) collective-permute-start(bf16[32,1024]{1,0:T(8,128)(2,1)S(1)} %collective-permute-done.5.refs_8_.refs_4_), channel_id=1, source_target_pairs={{0,1},{1,0},{2,3},{3,2},{4,5},{5,4},{6,7},{7,6},{8,9},{9,8},{10,11... | collective-permute-start | bytes 196616 | tf_op jit(solution)/shard_map/ppermute | solution.py:347
  26.1 11.6 %collective-permute-start.36 = (bf16[16,512]{1,0:T(8,128)(2,1)S(1)}, bf16[16,512]{1,0:T(8,128)(2,1)S(1)}, u32[]{:S(2)}, u32[]{:S(2)}) collective-permute-start(bf16[16,512]{1,0:T(8,128)(2,1)S(1)} %get-tuple-element.99), channel_id=1, source_target_pairs={{0,6},{1,7},{2,8},{3,9},{4,10},{5,11},{6,12},{7,13},{8,14},{9,15},... | collective-permute-start | bytes 49160 | tf_op jit(solution)/shard_map/ppermute | solution.py:358
  27.5 11.2 %collective-permute-start.37 = (bf16[16,512]{1,0:T(8,128)(2,1)S(1)}, bf16[16,512]{1,0:T(8,128)(2,1)S(1)}, u32[]{:S(2)}, u32[]{:S(2)}) collective-permute-start(bf16[16,512]{1,0:T(8,128)(2,1)S(1)} %get-tuple-element.100), channel_id=1, source_target_pairs={{0,7},{1,6},{2,9},{3,8},{4,11},{5,10},{6,13},{7,12},{8,15},{9,14},... | collective-permute-start | bytes 49160 | tf_op jit(solution)/shard_map/ppermute | solution.py:358
  28.3 12.6 %collective-permute-start.38 = (bf16[16,512]{1,0:T(8,128)(2,1)S(1)}, bf16[16,512]{1,0:T(8,128)(2,1)S(1)}, u32[]{:S(2)}, u32[]{:S(2)}) collective-permute-start(bf16[16,512]{1,0:T(8,128)(2,1)S(1)} %get-tuple-element.101), channel_id=1, source_target_pairs={{0,8},{1,9},{2,10},{3,11},{4,12},{5,13},{6,14},{7,15},{8,0},{9,1},... | collective-permute-start | bytes 49160 | tf_op jit(solution)/shard_map/ppermute | solution.py:358
  30.0 13.6 %collective-permute-start.39 = (bf16[16,512]{1,0:T(8,128)(2,1)S(1)}, bf16[16,512]{1,0:T(8,128)(2,1)S(1)}, u32[]{:S(2)}, u32[]{:S(2)}) collective-permute-start(bf16[16,512]{1,0:T(8,128)(2,1)S(1)} %get-tuple-element.102), channel_id=1, source_target_pairs={{0,9},{1,8},{2,11},{3,10},{4,13},{5,12},{6,15},{7,14},{8,1},{9,0},... | collective-permute-start | bytes 49160 | tf_op jit(solution)/shard_map/ppermute | solution.py:358
  31.3 12.3 %collective-permute-start.40 = (bf16[16,512]{1,0:T(8,128)(2,1)S(1)}, bf16[16,512]{1,0:T(8,128)(2,1)S(1)}, u32[]{:S(2)}, u32[]{:S(2)}) collective-permute-start(bf16[16,512]{1,0:T(8,128)(2,1)S(1)} %get-tuple-element.103), channel_id=1, source_target_pairs={{0,10},{1,11},{2,12},{3,13},{4,14},{5,15},{6,0},{7,1},{8,2},{9,3},... | collective-permute-start | bytes 49160 | tf_op jit(solution)/shard_map/ppermute | solution.py:358
  37.7 7.2 %collective-permute-start.41 = (bf16[16,512]{1,0:T(8,128)(2,1)S(1)}, bf16[16,512]{1,0:T(8,128)(2,1)S(1)}, u32[]{:S(2)}, u32[]{:S(2)}) collective-permute-start(bf16[16,512]{1,0:T(8,128)(2,1)S(1)} %get-tuple-element.104), channel_id=1, source_target_pairs={{0,11},{1,10},{2,13},{3,12},{4,15},{5,14},{6,1},{7,0},{8,3},{9,2},... | collective-permute-start | bytes 49160 | tf_op jit(solution)/shard_map/ppermute | solution.py:358
  38.7 8.7 %collective-permute-start.42 = (bf16[16,512]{1,0:T(8,128)(2,1)S(1)}, bf16[16,512]{1,0:T(8,128)(2,1)S(1)}, u32[]{:S(2)}, u32[]{:S(2)}) collective-permute-start(bf16[16,512]{1,0:T(8,128)(2,1)S(1)} %get-tuple-element.105), channel_id=1, source_target_pairs={{0,12},{1,13},{2,14},{3,15},{4,0},{5,1},{6,2},{7,3},{8,4},{9,5},{1... | collective-permute-start | bytes 49160 | tf_op jit(solution)/shard_map/ppermute | solution.py:358
  40.9 6.5 %collective-permute-start.43 = (bf16[16,512]{1,0:T(8,128)(2,1)S(1)}, bf16[16,512]{1,0:T(8,128)(2,1)S(1)}, u32[]{:S(2)}, u32[]{:S(2)}) collective-permute-start(bf16[16,512]{1,0:T(8,128)(2,1)S(1)} %get-tuple-element.106), channel_id=1, source_target_pairs={{0,13},{1,12},{2,15},{3,14},{4,1},{5,0},{6,3},{7,2},{8,5},{9,4},{1... | collective-permute-start | bytes 49160 | tf_op jit(solution)/shard_map/ppermute | solution.py:358
  47.5 6.6 %collective-permute-start.48 = (bf16[16,32]{1,0:T(8,128)(2,1)S(1)}, bf16[16,32]{1,0:T(8,128)(2,1)S(1)}, u32[]{:S(2)}, u32[]{:S(2)}) collective-permute-start(bf16[16,32]{1,0:T(8,128)(2,1)S(1)} %slice.12.refs_22_), channel_id=1, source_target_pairs={{0,3},{1,2},{2,5},{3,4},{4,7},{5,6},{6,9},{7,8},{8,11},{9,10},{10,... | collective-permute-start | bytes 3080 | tf_op jit(solution)/shard_map/ppermute | solution.py:358
  48.3 8.8 %collective-permute-start.49 = (bf16[16,32]{1,0:T(8,128)(2,1)S(1)}, bf16[16,32]{1,0:T(8,128)(2,1)S(1)}, u32[]{:S(2)}, u32[]{:S(2)}) collective-permute-start(bf16[16,32]{1,0:T(8,128)(2,1)S(1)} %slice.12.refs_22_), channel_id=1, source_target_pairs={{0,4},{1,5},{2,6},{3,7},{4,8},{5,9},{6,10},{7,11},{8,12},{9,13},{1... | collective-permute-start | bytes 3080 | tf_op jit(solution)/shard_map/ppermute | solution.py:358
  49.2 8.0 %collective-permute-start.50 = (bf16[16,32]{1,0:T(8,128)(2,1)S(1)}, bf16[16,32]{1,0:T(8,128)(2,1)S(1)}, u32[]{:S(2)}, u32[]{:S(2)}) collective-permute-start(bf16[16,32]{1,0:T(8,128)(2,1)S(1)} %slice.12.refs_22_), channel_id=1, source_target_pairs={{0,5},{1,4},{2,7},{3,6},{4,9},{5,8},{6,11},{7,10},{8,13},{9,12},{1... | collective-permute-start | bytes 3080 | tf_op jit(solution)/shard_map/ppermute | solution.py:358
  50.7 9.4 %collective-permute-start.51 = (bf16[16,32]{1,0:T(8,128)(2,1)S(1)}, bf16[16,32]{1,0:T(8,128)(2,1)S(1)}, u32[]{:S(2)}, u32[]{:S(2)}) collective-permute-start(bf16[16,32]{1,0:T(8,128)(2,1)S(1)} %slice.12.refs_22_), channel_id=1, source_target_pairs={{0,6},{1,7},{2,8},{3,9},{4,10},{5,11},{6,12},{7,13},{8,14},{9,15},... | collective-permute-start | bytes 3080 | tf_op jit(solution)/shard_map/ppermute | solution.py:358
  53.7 6.6 %collective-permute-start.52 = (bf16[16,32]{1,0:T(8,128)(2,1)S(1)}, bf16[16,32]{1,0:T(8,128)(2,1)S(1)}, u32[]{:S(2)}, u32[]{:S(2)}) collective-permute-start(bf16[16,32]{1,0:T(8,128)(2,1)S(1)} %slice.12.refs_22_), channel_id=1, source_target_pairs={{0,7},{1,6},{2,9},{3,8},{4,11},{5,10},{6,13},{7,12},{8,15},{9,14},... | collective-permute-start | bytes 3080 | tf_op jit(solution)/shard_map/ppermute | solution.py:358
  54.0 8.0 %collective-permute-start.53 = (bf16[16,32]{1,0:T(8,128)(2,1)S(1)}, bf16[16,32]{1,0:T(8,128)(2,1)S(1)}, u32[]{:S(2)}, u32[]{:S(2)}) collective-permute-start(bf16[16,32]{1,0:T(8,128)(2,1)S(1)} %slice.12.refs_22_), channel_id=1, source_target_pairs={{0,8},{1,9},{2,10},{3,11},{4,12},{5,13},{6,14},{7,15},{8,0},{9,1},... | collective-permute-start | bytes 3080 | tf_op jit(solution)/shard_map/ppermute | solution.py:358
  57.1 8.2 %collective-permute-start.54 = (bf16[16,32]{1,0:T(8,128)(2,1)S(1)}, bf16[16,32]{1,0:T(8,128)(2,1)S(1)}, u32[]{:S(2)}, u32[]{:S(2)}) collective-permute-start(bf16[16,32]{1,0:T(8,128)(2,1)S(1)} %slice.12.refs_22_), channel_id=1, source_target_pairs={{0,9},{1,8},{2,11},{3,10},{4,13},{5,12},{6,15},{7,14},{8,1},{9,0},... | collective-permute-start | bytes 3080 | tf_op jit(solution)/shard_map/ppermute | solution.py:358
  57.2 25.9 %collective-permute-start.55 = (bf16[16,32]{1,0:T(8,128)(2,1)S(1)}, bf16[16,32]{1,0:T(8,128)(2,1)S(1)}, u32[]{:S(2)}, u32[]{:S(2)}) collective-permute-start(bf16[16,32]{1,0:T(8,128)(2,1)S(1)} %slice.12.refs_22_), channel_id=1, source_target_pairs={{0,10},{1,11},{2,12},{3,13},{4,14},{5,15},{6,0},{7,1},{8,2},{9,3},... | collective-permute-start | bytes 3080 | tf_op jit(solution)/shard_map/ppermute | solution.py:358
  60.1 23.0 %collective-permute-start.56 = (bf16[16,32]{1,0:T(8,128)(2,1)S(1)}, bf16[16,32]{1,0:T(8,128)(2,1)S(1)}, u32[]{:S(2)}, u32[]{:S(2)}) collective-permute-start(bf16[16,32]{1,0:T(8,128)(2,1)S(1)} %slice.12.refs_22_), channel_id=1, source_target_pairs={{0,11},{1,10},{2,13},{3,12},{4,15},{5,14},{6,1},{7,0},{8,3},{9,2},... | collective-permute-start | bytes 3080 | tf_op jit(solution)/shard_map/ppermute | solution.py:358
  60.3 22.8 %collective-permute-start.57 = (bf16[16,32]{1,0:T(8,128)(2,1)S(1)}, bf16[16,32]{1,0:T(8,128)(2,1)S(1)}, u32[]{:S(2)}, u32[]{:S(2)}) collective-permute-start(bf16[16,32]{1,0:T(8,128)(2,1)S(1)} %slice.12.refs_22_), channel_id=1, source_target_pairs={{0,12},{1,13},{2,14},{3,15},{4,0},{5,1},{6,2},{7,3},{8,4},{9,5},{1... | collective-permute-start | bytes 3080 | tf_op jit(solution)/shard_map/ppermute | solution.py:358
  62.0 21.1 %collective-permute-start.58 = (bf16[16,32]{1,0:T(8,128)(2,1)S(1)}, bf16[16,32]{1,0:T(8,128)(2,1)S(1)}, u32[]{:S(2)}, u32[]{:S(2)}) collective-permute-start(bf16[16,32]{1,0:T(8,128)(2,1)S(1)} %slice.12.refs_22_), channel_id=1, source_target_pairs={{0,13},{1,12},{2,15},{3,14},{4,1},{5,0},{6,3},{7,2},{8,5},{9,4},{1... | collective-permute-start | bytes 3080 | tf_op jit(solution)/shard_map/ppermute | solution.py:358
  65.3 17.8 %collective-permute-start.59 = (bf16[16,32]{1,0:T(8,128)(2,1)S(1)}, bf16[16,32]{1,0:T(8,128)(2,1)S(1)}, u32[]{:S(2)}, u32[]{:S(2)}) collective-permute-start(bf16[16,32]{1,0:T(8,128)(2,1)S(1)} %slice.12.refs_22_), channel_id=1, source_target_pairs={{0,14},{1,15},{2,0},{3,1},{4,2},{5,3},{6,4},{7,5},{8,6},{9,7},{10,... | collective-permute-start | bytes 3080 | tf_op jit(solution)/shard_map/ppermute | solution.py:358
  84.2 7.3 %collective-permute-start.61 = (f32[2,1536]{1,0:T(2,128)S(1)}, f32[2,1536]{1,0:T(2,128)S(1)}, u32[]{:S(2)}, u32[]{:S(2)}) collective-permute-start(f32[2,1536]{1,0:T(2,128)S(1)} %get-tuple-element.111), channel_id=1, source_target_pairs={{0,2},{1,3},{2,4},{3,5},{4,6},{5,7},{6,8},{7,9},{8,10},{9,11},{10,... | collective-permute-start | bytes 36872 | tf_op jit(solution)/shard_map/ppermute | solution.py:358
  86.2 7.5 %collective-permute-start.63 = (f32[2,1536]{1,0:T(2,128)S(1)}, f32[2,1536]{1,0:T(2,128)S(1)}, u32[]{:S(2)}, u32[]{:S(2)}) collective-permute-start(f32[2,1536]{1,0:T(2,128)S(1)} %get-tuple-element.113), channel_id=1, source_target_pairs={{0,4},{1,5},{2,6},{3,7},{4,8},{5,9},{6,10},{7,11},{8,12},{9,13},{1... | collective-permute-start | bytes 36872 | tf_op jit(solution)/shard_map/ppermute | solution.py:358
  86.6 7.8 %collective-permute-start.64 = (f32[2,1536]{1,0:T(2,128)S(1)}, f32[2,1536]{1,0:T(2,128)S(1)}, u32[]{:S(2)}, u32[]{:S(2)}) collective-permute-start(f32[2,1536]{1,0:T(2,128)S(1)} %get-tuple-element.114), channel_id=1, source_target_pairs={{0,5},{1,4},{2,7},{3,6},{4,9},{5,8},{6,11},{7,10},{8,13},{9,12},{1... | collective-permute-start | bytes 36872 | tf_op jit(solution)/shard_map/ppermute | solution.py:358
  87.1 10.7 %collective-permute-start.65 = (f32[2,1536]{1,0:T(2,128)S(1)}, f32[2,1536]{1,0:T(2,128)S(1)}, u32[]{:S(2)}, u32[]{:S(2)}) collective-permute-start(f32[2,1536]{1,0:T(2,128)S(1)} %get-tuple-element.115), channel_id=1, source_target_pairs={{0,6},{1,7},{2,8},{3,9},{4,10},{5,11},{6,12},{7,13},{8,14},{9,15},... | collective-permute-start | bytes 36872 | tf_op jit(solution)/shard_map/ppermute | solution.py:358
  91.4 6.4 %collective-permute-start.66 = (f32[2,1536]{1,0:T(2,128)S(1)}, f32[2,1536]{1,0:T(2,128)S(1)}, u32[]{:S(2)}, u32[]{:S(2)}) collective-permute-start(f32[2,1536]{1,0:T(2,128)S(1)} %get-tuple-element.116), channel_id=1, source_target_pairs={{0,7},{1,6},{2,9},{3,8},{4,11},{5,10},{6,13},{7,12},{8,15},{9,14},... | collective-permute-start | bytes 36872 | tf_op jit(solution)/shard_map/ppermute | solution.py:358
  92.0 7.8 %collective-permute-start.67 = (f32[2,1536]{1,0:T(2,128)S(1)}, f32[2,1536]{1,0:T(2,128)S(1)}, u32[]{:S(2)}, u32[]{:S(2)}) collective-permute-start(f32[2,1536]{1,0:T(2,128)S(1)} %get-tuple-element.117), channel_id=1, source_target_pairs={{0,8},{1,9},{2,10},{3,11},{4,12},{5,13},{6,14},{7,15},{8,0},{9,1},... | collective-permute-start | bytes 36872 | tf_op jit(solution)/shard_map/ppermute | solution.py:358
  93.7 8.7 %collective-permute-start.68 = (f32[2,1536]{1,0:T(2,128)S(1)}, f32[2,1536]{1,0:T(2,128)S(1)}, u32[]{:S(2)}, u32[]{:S(2)}) collective-permute-start(f32[2,1536]{1,0:T(2,128)S(1)} %get-tuple-element.118), channel_id=1, source_target_pairs={{0,9},{1,8},{2,11},{3,10},{4,13},{5,12},{6,15},{7,14},{8,1},{9,0},... | collective-permute-start | bytes 36872 | tf_op jit(solution)/shard_map/ppermute | solution.py:358
  94.4 8.7 %collective-permute-start.69 = (f32[2,1536]{1,0:T(2,128)S(1)}, f32[2,1536]{1,0:T(2,128)S(1)}, u32[]{:S(2)}, u32[]{:S(2)}) collective-permute-start(f32[2,1536]{1,0:T(2,128)S(1)} %get-tuple-element.119), channel_id=1, source_target_pairs={{0,10},{1,11},{2,12},{3,13},{4,14},{5,15},{6,0},{7,1},{8,2},{9,3},... | collective-permute-start | bytes 36872 | tf_op jit(solution)/shard_map/ppermute | solution.py:358
  108.8 7.5 %collective-permute-start.76 = (f32[2,512]{1,0:T(2,128)S(1)}, f32[2,512]{1,0:T(2,128)S(1)}, u32[]{:S(2)}, u32[]{:S(2)}) collective-permute-start(f32[2,512]{1,0:T(2,128)S(1)} %get-tuple-element.127), channel_id=1, source_target_pairs={{0,2},{1,3},{2,4},{3,5},{4,6},{5,7},{6,8},{7,9},{8,10},{9,11},{10,... | collective-permute-start | bytes 12296 | tf_op jit(solution)/shard_map/ppermute | solution.py:358
  111.0 7.2 %collective-permute-start.78 = (f32[2,512]{1,0:T(2,128)S(1)}, f32[2,512]{1,0:T(2,128)S(1)}, u32[]{:S(2)}, u32[]{:S(2)}) collective-permute-start(f32[2,512]{1,0:T(2,128)S(1)} %get-tuple-element.129), channel_id=1, source_target_pairs={{0,4},{1,5},{2,6},{3,7},{4,8},{5,9},{6,10},{7,11},{8,12},{9,13},{1... | collective-permute-start | bytes 12296 | tf_op jit(solution)/shard_map/ppermute | solution.py:358
  111.0 8.1 %collective-permute-start.79 = (f32[2,512]{1,0:T(2,128)S(1)}, f32[2,512]{1,0:T(2,128)S(1)}, u32[]{:S(2)}, u32[]{:S(2)}) collective-permute-start(f32[2,512]{1,0:T(2,128)S(1)} %get-tuple-element.130), channel_id=1, source_target_pairs={{0,5},{1,4},{2,7},{3,6},{4,9},{5,8},{6,11},{7,10},{8,13},{9,12},{1... | collective-permute-start | bytes 12296 | tf_op jit(solution)/shard_map/ppermute | solution.py:358
  112.2 10.4 %collective-permute-start.80 = (f32[2,512]{1,0:T(2,128)S(1)}, f32[2,512]{1,0:T(2,128)S(1)}, u32[]{:S(2)}, u32[]{:S(2)}) collective-permute-start(f32[2,512]{1,0:T(2,128)S(1)} %get-tuple-element.131), channel_id=1, source_target_pairs={{0,6},{1,7},{2,8},{3,9},{4,10},{5,11},{6,12},{7,13},{8,14},{9,15},... | collective-permute-start | bytes 12296 | tf_op jit(solution)/shard_map/ppermute | solution.py:358
  116.7 8.1 %collective-permute-start.82 = (f32[2,512]{1,0:T(2,128)S(1)}, f32[2,512]{1,0:T(2,128)S(1)}, u32[]{:S(2)}, u32[]{:S(2)}) collective-permute-start(f32[2,512]{1,0:T(2,128)S(1)} %get-tuple-element.133), channel_id=1, source_target_pairs={{0,8},{1,9},{2,10},{3,11},{4,12},{5,13},{6,14},{7,15},{8,0},{9,1},... | collective-permute-start | bytes 12296 | tf_op jit(solution)/shard_map/ppermute | solution.py:358
  118.2 8.6 %collective-permute-start.83 = (f32[2,512]{1,0:T(2,128)S(1)}, f32[2,512]{1,0:T(2,128)S(1)}, u32[]{:S(2)}, u32[]{:S(2)}) collective-permute-start(f32[2,512]{1,0:T(2,128)S(1)} %get-tuple-element.134), channel_id=1, source_target_pairs={{0,9},{1,8},{2,11},{3,10},{4,13},{5,12},{6,15},{7,14},{8,1},{9,0},... | collective-permute-start | bytes 12296 | tf_op jit(solution)/shard_map/ppermute | solution.py:358
  119.1 8.7 %collective-permute-start.84 = (f32[2,512]{1,0:T(2,128)S(1)}, f32[2,512]{1,0:T(2,128)S(1)}, u32[]{:S(2)}, u32[]{:S(2)}) collective-permute-start(f32[2,512]{1,0:T(2,128)S(1)} %get-tuple-element.135), channel_id=1, source_target_pairs={{0,10},{1,11},{2,12},{3,13},{4,14},{5,15},{6,0},{7,1},{8,2},{9,3},... | collective-permute-start | bytes 12296 | tf_op jit(solution)/shard_map/ppermute | solution.py:358
  122.6 7.0 %collective-permute-start.86 = (f32[2,512]{1,0:T(2,128)S(1)}, f32[2,512]{1,0:T(2,128)S(1)}, u32[]{:S(2)}, u32[]{:S(2)}) collective-permute-start(f32[2,512]{1,0:T(2,128)S(1)} %get-tuple-element.137), channel_id=1, source_target_pairs={{0,12},{1,13},{2,14},{3,15},{4,0},{5,1},{6,2},{7,3},{8,4},{9,5},{1... | collective-permute-start | bytes 12296 | tf_op jit(solution)/shard_map/ppermute | solution.py:358
  129.6 6.4 %collective-permute-start.17 = (bf16[16,512]{1,0:T(8,128)(2,1)S(1)}, bf16[16,512]{1,0:T(8,128)(2,1)S(1)}, u32[]{:S(2)}, u32[]{:S(2)}) collective-permute-start(bf16[16,512]{1,0:T(8,128)(2,1)S(1)} %get-tuple-element.79), channel_id=1, source_target_pairs={{0,2},{1,3},{2,4},{3,5},{4,6},{5,7},{6,8},{7,9},{8,10},{9,11},{10,... | collective-permute-start | bytes 49160 | tf_op jit(solution)/shard_map/ppermute | solution.py:358
  132.2 6.5 %collective-permute-start.19 = (bf16[16,512]{1,0:T(8,128)(2,1)S(1)}, bf16[16,512]{1,0:T(8,128)(2,1)S(1)}, u32[]{:S(2)}, u32[]{:S(2)}) collective-permute-start(bf16[16,512]{1,0:T(8,128)(2,1)S(1)} %get-tuple-element.81), channel_id=1, source_target_pairs={{0,4},{1,5},{2,6},{3,7},{4,8},{5,9},{6,10},{7,11},{8,12},{9,13},{1... | collective-permute-start | bytes 49160 | tf_op jit(solution)/shard_map/ppermute | solution.py:358
  132.2 7.8 %collective-permute-start.20 = (bf16[16,512]{1,0:T(8,128)(2,1)S(1)}, bf16[16,512]{1,0:T(8,128)(2,1)S(1)}, u32[]{:S(2)}, u32[]{:S(2)}) collective-permute-start(bf16[16,512]{1,0:T(8,128)(2,1)S(1)} %get-tuple-element.82), channel_id=1, source_target_pairs={{0,5},{1,4},{2,7},{3,6},{4,9},{5,8},{6,11},{7,10},{8,13},{9,12},{1... | collective-permute-start | bytes 49160 | tf_op jit(solution)/shard_map/ppermute | solution.py:358
  133.2 9.1 %collective-permute-start.21 = (bf16[16,512]{1,0:T(8,128)(2,1)S(1)}, bf16[16,512]{1,0:T(8,128)(2,1)S(1)}, u32[]{:S(2)}, u32[]{:S(2)}) collective-permute-start(bf16[16,512]{1,0:T(8,128)(2,1)S(1)} %get-tuple-element.83), channel_id=1, source_target_pairs={{0,6},{1,7},{2,8},{3,9},{4,10},{5,11},{6,12},{7,13},{8,14},{9,15},... | collective-permute-start | bytes 49160 | tf_op jit(solution)/shard_map/ppermute | solution.py:358
  136.0 7.2 %collective-permute-start.22 = (bf16[16,512]{1,0:T(8,128)(2,1)S(1)}, bf16[16,512]{1,0:T(8,128)(2,1)S(1)}, u32[]{:S(2)}, u32[]{:S(2)}) collective-permute-start(bf16[16,512]{1,0:T(8,128)(2,1)S(1)} %get-tuple-element.84), channel_id=1, source_target_pairs={{0,7},{1,6},{2,9},{3,8},{4,11},{5,10},{6,13},{7,12},{8,15},{9,14},... | collective-permute-start | bytes 49160 | tf_op jit(solution)/shard_map/ppermute | solution.py:358
  137.0 7.7 %collective-permute-start.23 = (bf16[16,512]{1,0:T(8,128)(2,1)S(1)}, bf16[16,512]{1,0:T(8,128)(2,1)S(1)}, u32[]{:S(2)}, u32[]{:S(2)}) collective-permute-start(bf16[16,512]{1,0:T(8,128)(2,1)S(1)} %get-tuple-element.85), channel_id=1, source_target_pairs={{0,8},{1,9},{2,10},{3,11},{4,12},{5,13},{6,14},{7,15},{8,0},{9,1},... | collective-permute-start | bytes 49160 | tf_op jit(solution)/shard_map/ppermute | solution.py:358
  138.7 9.5 %collective-permute-start.24 = (bf16[16,512]{1,0:T(8,128)(2,1)S(1)}, bf16[16,512]{1,0:T(8,128)(2,1)S(1)}, u32[]{:S(2)}, u32[]{:S(2)}) collective-permute-start(bf16[16,512]{1,0:T(8,128)(2,1)S(1)} %get-tuple-element.86), channel_id=1, source_target_pairs={{0,9},{1,8},{2,11},{3,10},{4,13},{5,12},{6,15},{7,14},{8,1},{9,0},... | collective-permute-start | bytes 49160 | tf_op jit(solution)/shard_map/ppermute | solution.py:358
  140.0 8.2 %collective-permute-start.25 = (bf16[16,512]{1,0:T(8,128)(2,1)S(1)}, bf16[16,512]{1,0:T(8,128)(2,1)S(1)}, u32[]{:S(2)}, u32[]{:S(2)}) collective-permute-start(bf16[16,512]{1,0:T(8,128)(2,1)S(1)} %get-tuple-element.87), channel_id=1, source_target_pairs={{0,10},{1,11},{2,12},{3,13},{4,14},{5,15},{6,0},{7,1},{8,2},{9,3},... | collective-permute-start | bytes 49160 | tf_op jit(solution)/shard_map/ppermute | solution.py:358
  142.2 7.2 %collective-permute-start.26 = (bf16[16,512]{1,0:T(8,128)(2,1)S(1)}, bf16[16,512]{1,0:T(8,128)(2,1)S(1)}, u32[]{:S(2)}, u32[]{:S(2)}) collective-permute-start(bf16[16,512]{1,0:T(8,128)(2,1)S(1)} %get-tuple-element.88), channel_id=1, source_target_pairs={{0,11},{1,10},{2,13},{3,12},{4,15},{5,14},{6,1},{7,0},{8,3},{9,2},... | collective-permute-start | bytes 49160 | tf_op jit(solution)/shard_map/ppermute | solution.py:358
  154.9 30.5 %collective-permute-start.90 = (f32[8,32,1024]{2,1,0:T(8,128)S(1)}, f32[8,32,1024]{2,1,0:T(8,128)S(1)}, u32[]{:S(2)}, u32[]{:S(2)}) collective-permute-start(f32[8,32,1024]{2,1,0:T(8,128)S(1)} %shard_map.171), channel_id=1, source_target_pairs={{0,1},{1,0},{2,3},{3,2},{4,5},{5,4},{6,7},{7,6},{8,9},{9,8},{10,11... | collective-permute-start | bytes 3145736 | tf_op jit(solution)/shard_map/ppermute | solution.py:347
  155.0 7.0 %collective-permute-start.100 = (f32[16,32]{1,0:T(8,128)S(1)}, f32[16,32]{1,0:T(8,128)S(1)}, u32[]{:S(2)}, u32[]{:S(2)}) collective-permute-start(f32[16,32]{1,0:T(8,128)S(1)} %get-tuple-element.142.refs_6_), channel_id=1, source_target_pairs={{0,9},{1,8},{2,11},{3,10},{4,13},{5,12},{6,15},{7,14},{8,1},{9,0},... | collective-permute-start | bytes 6152 | tf_op jit(solution)/shard_map/ppermute | solution.py:358
  155.0 8.0 %collective-permute-start.101 = (f32[16,32]{1,0:T(8,128)S(1)}, f32[16,32]{1,0:T(8,128)S(1)}, u32[]{:S(2)}, u32[]{:S(2)}) collective-permute-start(f32[16,32]{1,0:T(8,128)S(1)} %get-tuple-element.142.refs_6_), channel_id=1, source_target_pairs={{0,10},{1,11},{2,12},{3,13},{4,14},{5,15},{6,0},{7,1},{8,2},{9,3},... | collective-permute-start | bytes 6152 | tf_op jit(solution)/shard_map/ppermute | solution.py:358
  167.9 17.5 %collective-permute-start.91 = (bf16[8,16,1024]{2,1,0:T(8,128)(2,1)S(1)}, bf16[8,16,1024]{2,1,0:T(8,128)(2,1)S(1)}, u32[]{:S(2)}, u32[]{:S(2)}) collective-permute-start(bf16[8,16,1024]{2,1,0:T(8,128)(2,1)S(1)} %shard_map.172), channel_id=1, source_target_pairs={{0,1},{1,0},{2,3},{3,2},{4,5},{5,4},{6,7},{7,6},{8,9},{9,8},{10,11... | collective-permute-start | bytes 786440 | tf_op jit(solution)/shard_map/ppermute | solution.py:347
  174.0 11.4 %collective-permute-start.97 = (f32[16,32]{1,0:T(8,128)S(1)}, f32[16,32]{1,0:T(8,128)S(1)}, u32[]{:S(2)}, u32[]{:S(2)}) collective-permute-start(f32[16,32]{1,0:T(8,128)S(1)} %get-tuple-element.142.refs_6_), channel_id=1, source_target_pairs={{0,6},{1,7},{2,8},{3,9},{4,10},{5,11},{6,12},{7,13},{8,14},{9,15},... | collective-permute-start | bytes 6152 | tf_op jit(solution)/shard_map/ppermute | solution.py:358
  174.3 11.1 %collective-permute-start.98 = (f32[16,32]{1,0:T(8,128)S(1)}, f32[16,32]{1,0:T(8,128)S(1)}, u32[]{:S(2)}, u32[]{:S(2)}) collective-permute-start(f32[16,32]{1,0:T(8,128)S(1)} %get-tuple-element.142.refs_6_), channel_id=1, source_target_pairs={{0,7},{1,6},{2,9},{3,8},{4,11},{5,10},{6,13},{7,12},{8,15},{9,14},... | collective-permute-start | bytes 6152 | tf_op jit(solution)/shard_map/ppermute | solution.py:358
  177.4 8.0 %collective-permute-start.99 = (f32[16,32]{1,0:T(8,128)S(1)}, f32[16,32]{1,0:T(8,128)S(1)}, u32[]{:S(2)}, u32[]{:S(2)}) collective-permute-start(f32[16,32]{1,0:T(8,128)S(1)} %get-tuple-element.142.refs_6_), channel_id=1, source_target_pairs={{0,8},{1,9},{2,10},{3,11},{4,12},{5,13},{6,14},{7,15},{8,0},{9,1},... | collective-permute-start | bytes 6152 | tf_op jit(solution)/shard_map/ppermute | solution.py:358
  186.4 7.6 %collective-permute-start.107 = (bf16[32,1024]{1,0:T(8,128)(2,1)S(1)}, bf16[32,1024]{1,0:T(8,128)(2,1)S(1)}, u32[]{:S(2)}, u32[]{:S(2)}) collective-permute-start(bf16[32,1024]{1,0:T(8,128)(2,1)S(1)} %get-tuple-element.144), channel_id=1, source_target_pairs={{0,2},{1,3},{2,4},{3,5},{4,6},{5,7},{6,8},{7,9},{8,10},{9,11},{10,... | collective-permute-start | bytes 196616 | tf_op jit(solution)/shard_map/ppermute | solution.py:358
  187.5 8.7 %collective-permute-start.108 = (bf16[32,1024]{1,0:T(8,128)(2,1)S(1)}, bf16[32,1024]{1,0:T(8,128)(2,1)S(1)}, u32[]{:S(2)}, u32[]{:S(2)}) collective-permute-start(bf16[32,1024]{1,0:T(8,128)(2,1)S(1)} %get-tuple-element.145), channel_id=1, source_target_pairs={{0,4},{1,5},{2,6},{3,7},{4,8},{5,9},{6,10},{7,11},{8,12},{9,13},{1... | collective-permute-start | bytes 196616 | tf_op jit(solution)/shard_map/ppermute | solution.py:358
  187.7 12.0 %collective-permute-start.109 = (bf16[32,1024]{1,0:T(8,128)(2,1)S(1)}, bf16[32,1024]{1,0:T(8,128)(2,1)S(1)}, u32[]{:S(2)}, u32[]{:S(2)}) collective-permute-start(bf16[32,1024]{1,0:T(8,128)(2,1)S(1)} %get-tuple-element.146), channel_id=1, source_target_pairs={{0,6},{1,7},{2,8},{3,9},{4,10},{5,11},{6,12},{7,13},{8,14},{9,15},... | collective-permute-start | bytes 196616 | tf_op jit(solution)/shard_map/ppermute | solution.py:358
  191.4 8.6 %collective-permute-start.110 = (bf16[32,1024]{1,0:T(8,128)(2,1)S(1)}, bf16[32,1024]{1,0:T(8,128)(2,1)S(1)}, u32[]{:S(2)}, u32[]{:S(2)}) collective-permute-start(bf16[32,1024]{1,0:T(8,128)(2,1)S(1)} %get-tuple-element.147), channel_id=1, source_target_pairs={{0,8},{1,9},{2,10},{3,11},{4,12},{5,13},{6,14},{7,15},{8,0},{9,1},... | collective-permute-start | bytes 196616 | tf_op jit(solution)/shard_map/ppermute | solution.py:358
  192.8 8.0 %collective-permute-start.111 = (bf16[32,1024]{1,0:T(8,128)(2,1)S(1)}, bf16[32,1024]{1,0:T(8,128)(2,1)S(1)}, u32[]{:S(2)}, u32[]{:S(2)}) collective-permute-start(bf16[32,1024]{1,0:T(8,128)(2,1)S(1)} %get-tuple-element.148), channel_id=1, source_target_pairs={{0,10},{1,11},{2,12},{3,13},{4,14},{5,15},{6,0},{7,1},{8,2},{9,3},... | collective-permute-start | bytes 196616 | tf_op jit(solution)/shard_map/ppermute | solution.py:358
  194.0 6.8 %collective-permute-start.112 = (bf16[32,1024]{1,0:T(8,128)(2,1)S(1)}, bf16[32,1024]{1,0:T(8,128)(2,1)S(1)}, u32[]{:S(2)}, u32[]{:S(2)}) collective-permute-start(bf16[32,1024]{1,0:T(8,128)(2,1)S(1)} %get-tuple-element.149), channel_id=1, source_target_pairs={{0,12},{1,13},{2,14},{3,15},{4,0},{5,1},{6,2},{7,3},{8,4},{9,5},{1... | collective-permute-start | bytes 196616 | tf_op jit(solution)/shard_map/ppermute | solution.py:358
  (68 other events, 749.7 us)

commit v3 on v1

v3 whole, which is shorter than its diff:
```python
import functools
import math

import jax
import jax.numpy as jnp
from jax import lax
from jax.experimental import pallas as pl
from jax.experimental.pallas import tpu as pltpu
from jax.sharding import PartitionSpec as P

HEAD_WIDTH = 128
ROPE_BASE = 500000.0
MASKED = -1e30
SCALE = 0.5
F32 = jnp.float32
BF16 = jnp.bfloat16

PARAMS = pltpu.CompilerParams(vmem_limit_bytes=16 * 1024 * 1024)


def nn(a, b):
    return lax.dot_general(a, b, (((1,), (0,)), ((), ())), preferred_element_type=F32)


def nt(a, b):
    return lax.dot_general(a, b, (((1,), (1,)), ((), ())), preferred_element_type=F32)


def tn(a, b):
    return lax.dot_general(a, b, (((0,), (0,)), ((), ())), preferred_element_type=F32)


WIDE = pltpu.CompilerParams(vmem_limit_bytes=52 * 1024 * 1024)
VMEM = pl.BlockSpec(memory_space=pltpu.VMEM)
SMEM = pl.BlockSpec(memory_space=pltpu.SMEM)
HBM = pl.BlockSpec(memory_space=pltpu.HBM)
ANY = pl.BlockSpec(memory_space=pl.ANY)


def piece_at(at_ref, chips, k, flip, cross):
    lines = chips // 2
    z = lax.rem(at_ref[0] // 2 + lines - k, lines)
    y = lax.rem(at_ref[0], 2)
    core = 1 - at_ref[1] if cross else at_ref[1]
    return 4 * z + 2 * (1 - y if flip else y) + core


def stack_kernel(*refs):
    for k, r in enumerate(refs[:-1]):
        refs[-1][k] = r[...]


def query_kernel(flip, cross, *refs):
    at_ref, w_ref, x_ref = refs[:3]
    q_ref, w_s, sems = refs[-3:]
    lines, _, width = x_ref.shape
    copies = []
    for k in range(lines):
        start = pl.multiple_of(piece_at(at_ref, 2 * lines, k, flip, cross) * width, width)
        copy = pltpu.make_async_copy(w_ref.at[pl.ds(start, width)], w_s.at[k], sems.at[k])
        copy.start()
        copies.append(copy)
    total = refs[3][...] if len(refs) > 6 else None
    for k in range(lines):
        copies[k].wait()
        part = nn(x_ref[k], w_s[k])
        total = part if total is None else total + part
    q_ref[...] = total


def query_stack(at, weight, x, flip, cross, *before):
    lines, rows, width = x.shape
    cols = weight.shape[1]
    return pl.pallas_call(
        functools.partial(query_kernel, flip, cross),
        out_shape=jax.ShapeDtypeStruct((rows, cols), F32),
        in_specs=[SMEM, HBM] + [VMEM] * (1 + len(before)),
        scratch_shapes=[
            pltpu.VMEM((lines, width, cols), BF16),
            pltpu.SemaphoreType.DMA((lines,)),
        ],
        compiler_params=WIDE,
    )(at, weight, x, *before)


def rank_sum(at_ref, d_ref, stacks, kinds, total):
    for x_ref, (flip, cross) in zip(stacks, kinds):
        lines, _, width = x_ref.shape
        for k in range(lines):
            start = pl.multiple_of(piece_at(at_ref, 2 * lines, k, flip, cross) * width, width)
            part = nt(d_ref[:, pl.ds(start, width)], x_ref[k])
            total = part if total is None else total + part
    return total


def rank_early_kernel(at_ref, d_ref, a_ref, b_ref, c_ref, r_ref):
    kinds = ((False, False), (True, False), (False, True))
    r_ref[...] = rank_sum(at_ref, d_ref, (a_ref, b_ref, c_ref), kinds, None)


def rank_late_kernel(at_ref, d_ref, x_ref, early_ref, own_ref, send_ref, rest_ref):
    devices, rank, _ = send_ref.shape
    rows = early_ref.shape[1]
    total = rank_sum(at_ref, d_ref, (x_ref,), ((True, True),), early_ref[...])
    total = total.astype(BF16).astype(F32) * own_ref[...]
    rest_ref[...] = total[rank:].astype(BF16)
    first = total[:rank].astype(BF16)
    if rows < send_ref.shape[2]:
        send_ref[...] = jnp.zeros_like(send_ref)
    for d in range(devices):
        send_ref[d, :, :rows] = first


def split_kernel(at_ref, q_ref, l_ref, o_ref, dep_ref, heads_ref, half_ref):
    rank, _ = q_ref.shape
    devices, _, cols = heads_ref.shape
    for d in range(devices):
        heads_ref[d, :rank, :] = q_ref[:, d * cols : (d + 1) * cols]
        heads_ref[d, rank:, :] = l_ref[:, d * cols : (d + 1) * cols]
    width = half_ref.shape[2]
    for c in range(half_ref.shape[0]):
        start = pl.multiple_of((2 * c + 1 - at_ref[1]) * width, width)
        half_ref[c] = o_ref[:, pl.ds(start, width)]


def kv_kernel(x_ref, w_ref, own_ref, kup_ref, vup_ref, o_ref):
    devices, steps, _ = o_ref.shape
    rank, half = kup_ref.shape
    own = own_ref[...]
    both = nn(x_ref[...], w_ref[...])
    keys = both[:, :half] + SCALE * tn(own[:rank], kup_ref[...])
    values = both[:, half:] + SCALE * tn(own[rank:], vup_ref[...])
    for r in range(devices):
        for t in range(steps):
            m = t * devices + r
            o_ref[r, t : t + 1, :half] = keys[m : m + 1]
            o_ref[r, t : t + 1, half:] = values[m : m + 1]


def finish_kernel(q_ref, ranks_ref, mask_ref, up_ref, dep_ref, o_ref):
    devices, steps, _ = o_ref.shape
    rank = ranks_ref.shape[1]
    rows, _ = q_ref.shape
    u = ranks_ref[0].astype(F32)
    for d in range(1, devices):
        u = u + ranks_ref[d].astype(F32)
    u = u[:, :rows]
    spread = (jnp.concatenate([u] * devices, axis=0) * mask_ref[...]).astype(BF16)
    up = jnp.concatenate([up_ref[d, :rank] for d in range(devices)], axis=0)
    query = q_ref[...] + SCALE * tn(spread, up)
    for r in range(devices):
        for t in range(steps):
            m = t * devices + r
            o_ref[r, t : t + 1, :] = query[m : m + 1]


def rope(v, cosine, sine):
    return v * cosine + pltpu.roll(v, HEAD_WIDTH // 2, 1) * sine


def attend_kernel(len_ref, recv_ref, kv_ref, cos_ref, sin_ref, k_ref, v_ref, ctx_ref, ent_ref, q_s, kn_s, vn_s):
    devices, steps, cols = ctx_ref.shape
    slots, kv_cols = k_ref.shape
    kv_heads = kv_cols // HEAD_WIDTH
    per_device = cols // HEAD_WIDTH
    group = devices * per_device // kv_heads
    rows = group * steps
    score_scale = 1.0 / math.sqrt(HEAD_WIDTH)
    length = len_ref[0]
    kv = kv_ref[0]
    for d in range(1, devices):
        kv = kv + kv_ref[d]
    cosine = cos_ref[...]
    sine = sin_ref[...]
    kn_s[...] = jnp.zeros_like(kn_s)
    vn_s[...] = jnp.zeros_like(vn_s)
    fresh = kn_s.shape[0]
    col_old = lax.broadcasted_iota(jnp.int32, (rows, slots), 1)
    col_new = lax.broadcasted_iota(jnp.int32, (rows, fresh), 1)
    step_new = lax.rem(lax.broadcasted_iota(jnp.int32, (rows, fresh), 0), steps)
    for k in range(kv_heads):
        lanes = slice(k * HEAD_WIDTH, (k + 1) * HEAD_WIDTH)
        for i in range(group):
            h = k * group + i
            d, hh = h // per_device, h % per_device
            q_s[i * steps : (i + 1) * steps, :] = recv_ref[d, :, hh * HEAD_WIDTH : (hh + 1) * HEAD_WIDTH]
        query = q_s[...].astype(BF16).astype(F32)
        query = rope(query, cosine, sine).astype(BF16)
        key_now = rope(kv[:, lanes], cosine[:steps], sine[:steps]).astype(BF16).astype(F32)
        value_now = kv[:, kv_cols + k * HEAD_WIDTH : kv_cols + (k + 1) * HEAD_WIDTH].astype(BF16).astype(F32)
        ent_ref[:, lanes] = key_now
        ent_ref[:, kv_cols + k * HEAD_WIDTH : kv_cols + (k + 1) * HEAD_WIDTH] = value_now
        kn_s[:steps, :] = key_now
        vn_s[:steps, :] = value_now
        old = nt(query, k_ref[:, lanes]) * score_scale
        old = jnp.where(col_old < length, old, MASKED)
        new = nt(query, kn_s[...].astype(BF16)) * score_scale
        new = jnp.where((col_new < steps) & (col_new <= step_new), new, MASKED)
        top = jnp.maximum(jnp.max(old, axis=1, keepdims=True), jnp.max(new, axis=1, keepdims=True))
        e_old = jnp.exp(old - top)
        e_new = jnp.exp(new - top)
        total = jnp.sum(e_old, axis=1, keepdims=True) + jnp.sum(e_new, axis=1, keepdims=True)
        p_old = (e_old / total).astype(BF16)
        p_new = (e_new / total).astype(BF16)
        out = nn(p_old, v_ref[:, lanes]) + nn(p_new, vn_s[...].astype(BF16))
        out = out.astype(BF16).astype(F32)
        for i in range(group):
            h = k * group + i
            d, hh = h // per_device, h % per_device
            ctx_ref[d, :, hh * HEAD_WIDTH : (hh + 1) * HEAD_WIDTH] = out[i * steps : (i + 1) * steps, :]


def lower_kernel(ctx_ref, mask_ref, low_ref, x_ref, send_ref, x_s):
    devices, steps, _ = ctx_ref.shape
    rank = send_ref.shape[1]
    for r in range(devices):
        for t in range(steps):
            x_s[t * devices + r : t * devices + r + 1, :] = ctx_ref[r, t : t + 1, :]
    x = x_s[...].astype(BF16)
    x_ref[...] = x
    rows = x.shape[0]
    low = jnp.concatenate([low_ref[d, rank:] for d in range(devices)], axis=0)
    every = nt(low, x) * mask_ref[...]
    part = every[:rank]
    for d in range(1, devices):
        part = part + every[d * rank : (d + 1) * rank]
    if rows < send_ref.shape[2]:
        send_ref[...] = jnp.zeros_like(send_ref)
    for d in range(devices):
        send_ref[d, :, :rows] = part


def out_there_kernel(at_ref, x_ref, w_ref, o_ref):
    width = o_ref.shape[2]
    x = x_ref[...]
    for c in range(o_ref.shape[0]):
        start = pl.multiple_of((2 * c + 1 - at_ref[1]) * width, width)
        o_ref[c] = nn(x, w_ref[:, pl.ds(start, width)])


def out_here_kernel(at_ref, x_ref, w_ref, o_ref, w_s, sems):
    chips, _, width = o_ref.shape
    copies = []
    for c in range(chips):
        start = pl.multiple_of((2 * c + at_ref[1]) * width, width)
        copy = pltpu.make_async_copy(w_ref.at[:, pl.ds(start, width)], w_s.at[c], sems.at[c])
        copy.start()
        copies.append(copy)
    x = x_ref[...]
    for c in range(chips):
        copies[c].wait()
        o_ref[c] = nn(x, w_s[c])


def pair_kernel(at_ref, a_ref, b_ref, mask_ref, up_ref, other_ref, parts_ref, *outs):
    chips = len(outs)
    rows, width = outs[0].shape
    u = parts_ref[0]
    for d in range(1, parts_ref.shape[0]):
        u = u + parts_ref[d]
    u = u[:, :rows].astype(BF16).astype(F32)
    spread = jnp.concatenate([u * mask_ref[0:1, :], u * mask_ref[1:2, :]], axis=0).astype(BF16)
    for k, out in enumerate(outs):
        dest = lax.rem(at_ref[0] + k, chips)
        start = pl.multiple_of((2 * dest + at_ref[1]) * width, width)
        up = jnp.concatenate([up_ref[:, pl.ds(start, width)], other_ref[dest]], axis=0)
        out[...] = (a_ref[dest] + b_ref[dest] + SCALE * tn(spread, up)).astype(BF16)


def total_kernel(*refs):
    total = refs[0][...].astype(F32)
    for r in refs[1:-1]:
        total = total + r[...].astype(F32)
    refs[-1][...] = total.astype(BF16)


def body(
    tokens,
    query_weight,
    key_value_weight,
    output_weight,
    cached_rotated_keys,
    cached_values,
    lengths,
    request_adapter,
    adapter_pool_slot,
    adapter_down_maps,
    query_up_maps,
    key_up_maps,
    value_up_maps,
    result_lowering_factors,
    output_up_maps,
):
    both = ("tp", "sub")
    chips = lax.axis_size("tp")
    devices = lax.axis_size(both)
    lines = chips // 2
    me = lax.axis_index(both)
    core = lax.axis_index("sub")
    steps, requests, width = tokens.shape
    rows = steps * requests
    padded = -(-rows // 128) * 128
    cols = query_weight.shape[1]
    rank = key_up_maps.shape[1]
    assert devices == 2 * chips and chips % 2 == 0
    assert adapter_down_maps.shape[0] == 1 and requests == devices and cached_values.shape[0] == 1
    at = jnp.stack([lax.axis_index("tp"), core]).astype(jnp.int32)

    def swap_core(v):
        return lax.ppermute(v, "sub", [(0, 1), (1, 0)])

    def swap_y(v):
        return lax.ppermute(v, "tp", [(i, i ^ 1) for i in range(chips)])

    def shift_chip(v, k):
        if k == 0:
            return v
        return lax.ppermute(v, "tp", [(i, (i + k) % chips) for i in range(chips)])

    def exchange(v):
        return lax.all_to_all(v, both, 0, 0, tiled=True)

    x = tokens.reshape(rows, width)
    pieces = [shift_chip(x, 2 * k) for k in range(lines)]
    line = pl.pallas_call(
        stack_kernel,
        out_shape=jax.ShapeDtypeStruct((lines, rows, width), BF16),
        compiler_params=PARAMS,
    )(*pieces)
    across = swap_y(line)
    line_cross = swap_core(line)
    across_cross = swap_core(across)

    index = jnp.arange(devices, dtype=jnp.int32)
    slot = jnp.sum(
        jnp.where(request_adapter[:, None] == index[None, :], adapter_pool_slot[None, :], 0), axis=1
    )
    row_slot = jnp.tile(slot, steps)[None, :]
    spread_mask = (jnp.repeat(index, rank)[:, None] == row_slot).astype(F32)
    own_mask = (row_slot == me).astype(F32)
    pair_mask = (jnp.stack([me, me + 1 - 2 * core])[:, None] == row_slot).astype(F32)

    by_heads, half = pl.pallas_call(
        split_kernel,
        out_shape=(
            jax.ShapeDtypeStruct((devices, 2 * rank, cols), BF16),
            jax.ShapeDtypeStruct((chips, rank, width), BF16),
        ),
        in_specs=[SMEM, VMEM, VMEM, VMEM, ANY],
        compiler_params=PARAMS,
    )(at, query_up_maps[0], result_lowering_factors[0], output_up_maps[0], line)
    maps = exchange(by_heads)
    up_other = swap_core(half)

    query = query_stack(at, query_weight, line, False, False)
    query = query_stack(at, query_weight, line_cross, False, True, query)
    query = query_stack(at, query_weight, across, True, False, query)
    down = adapter_down_maps[0]
    early = pl.pallas_call(
        rank_early_kernel,
        out_shape=jax.ShapeDtypeStruct((down.shape[0], rows), F32),
        in_specs=[SMEM] + [VMEM] * 4,
        compiler_params=PARAMS,
    )(at, down, line, across, line_cross)
    rank_send, rank_rest = pl.pallas_call(
        rank_late_kernel,
        out_shape=(
            jax.ShapeDtypeStruct((devices, rank, padded), BF16),
            jax.ShapeDtypeStruct((2 * rank, rows), BF16),
        ),
        in_specs=[SMEM] + [VMEM] * 4,
        compiler_params=PARAMS,
    )(at, down, across_cross, early, own_mask)
    ranks = exchange(rank_send)
    kv_send = pl.pallas_call(
        kv_kernel,
        out_shape=jax.ShapeDtypeStruct((devices, steps, key_value_weight.shape[1]), F32),
        compiler_params=PARAMS,
    )(x, key_value_weight, rank_rest, key_up_maps[0], value_up_maps[0])
    kv = exchange(kv_send)
    query = query_stack(at, query_weight, across_cross, True, True, query)
    arrived = exchange(
        pl.pallas_call(
            finish_kernel,
            out_shape=jax.ShapeDtypeStruct((devices, steps, cols), F32),
            in_specs=[VMEM] * 4 + [ANY],
            compiler_params=PARAMS,
        )(query, ranks, spread_mask, maps, kv_send)
    )

    kv_cols = key_value_weight.shape[1] // 2
    half_width = HEAD_WIDTH // 2
    frequency = ROPE_BASE ** (-2.0 * jnp.arange(half_width, dtype=F32) / HEAD_WIDTH)
    positions = lengths[0] + jnp.arange(steps, dtype=jnp.int32)
    angles = positions.astype(F32)[:, None] * frequency
    cosine, sine = jnp.cos(angles), jnp.sin(angles)
    group = devices * cols // kv_cols
    cosine = jnp.tile(jnp.concatenate([cosine, cosine], axis=1), (group, 1))
    sine = jnp.tile(jnp.concatenate([-sine, sine], axis=1), (group, 1))
    context, fresh = pl.pallas_call(
        attend_kernel,
        out_shape=(
            jax.ShapeDtypeStruct((devices, steps, cols), F32),
            jax.ShapeDtypeStruct((steps, 2 * kv_cols), F32),
        ),
        in_specs=[SMEM] + [VMEM] * 6,
        scratch_shapes=[
            pltpu.VMEM((group * steps, HEAD_WIDTH), F32),
            pltpu.VMEM((16, HEAD_WIDTH), F32),
            pltpu.VMEM((16, HEAD_WIDTH), F32),
        ],
        compiler_params=PARAMS,
    )(lengths, arrived, kv, cosine, sine, cached_rotated_keys[0], cached_values[0])
    entries = fresh.astype(BF16)[:, None, :]

    by_head = exchange(context)
    lhs, part_send = pl.pallas_call(
        lower_kernel,
        out_shape=(
            jax.ShapeDtypeStruct((rows, cols), BF16),
            jax.ShapeDtypeStruct((devices, rank, padded), F32),
        ),
        scratch_shapes=[pltpu.VMEM((rows, cols), F32)],
        compiler_params=PARAMS,
    )(by_head, spread_mask, maps)
    parts = exchange(part_send)
    out_shape = jax.ShapeDtypeStruct((chips, rows, width), F32)
    out_there = pl.pallas_call(
        out_there_kernel,
        out_shape=out_shape,
        in_specs=[SMEM, VMEM, VMEM],
        compiler_params=PARAMS,
    )(at, lhs, output_weight)
    received = swap_core(out_there)
    out_here = pl.pallas_call(
        out_here_kernel,
        out_shape=out_shape,
        in_specs=[SMEM, VMEM, HBM],
        scratch_shapes=[
            pltpu.VMEM((chips, cols, width), BF16),
            pltpu.SemaphoreType.DMA((chips,)),
        ],
        compiler_params=WIDE,
    )(at, lhs, output_weight)
    chip_totals = pl.pallas_call(
        pair_kernel,
        out_shape=[jax.ShapeDtypeStruct((rows, width), BF16)] * chips,
        in_specs=[SMEM] + [VMEM] * 6,
        compiler_params=PARAMS,
    )(at, out_here, received, pair_mask, output_up_maps[0], up_other, parts)
    final = [shift_chip(v, k) for k, v in enumerate(chip_totals)]
    attended = pl.pallas_call(
        total_kernel,
        out_shape=jax.ShapeDtypeStruct((rows, width), BF16),
        compiler_params=PARAMS,
    )(*final)
    return attended.reshape(steps, requests, width), entries


def solution(mesh):
    placed = (
        P(None, "groups", ("tp", "sub")),
        P(None, ("tp", "sub")),
        P(("tp", "sub"), None),
        P(("tp", "sub"), None),
        P(("groups", "tp", "sub"), None, None),
        P(("groups", "tp", "sub"), None, None),
        P(("groups", "tp", "sub")),
        P("groups"),
        P(),
        P(("tp", "sub"), None, None),
        P(("tp", "sub"), None, None),
        P(("tp", "sub"), None, None),
        P(("tp", "sub"), None, None),
        P(("tp", "sub"), None, None),
        P(("tp", "sub"), None, None),
    )
    return jax.shard_map(
        body,
        mesh=mesh,
        in_specs=placed,
        out_specs=(P(None, "groups", ("tp", "sub")), P(None, ("groups", "tp", "sub"), None)),
        check_vma=False,
    )
```

time: 143 us -> 136 us (0.951)
  blocking collectives: 34.2 us -> 9.48 us
  starting transfers between devices: 26.8 us -> 38.3 us
  local copies, waits for them, and re-layouts: 11.4 us -> 16.5 us
  waiting for transfers between devices: 34.2 us -> 37.7 us
  Pallas kernels: 30.8 us -> 29.3 us
    all_to_all x2 -> x1, blocking collectives: 34.2 us -> 9.48 us  [exchange(): return lax.all_to_all(v, both, 0, 0, tiled=True)]
    ppermute x3 -> x15, starting transfers between devices: 0.59 us -> 17 us  [the longest x10 14.8 us: shift_chip(): return lax.ppermute(v, 'tp', [(i, (i + k) % chips) for i in range(chips)])]
    ppermute x3 -> x15, waiting for transfers between devices: 0.01 us -> 16.3 us  [the longest x10 11 us: shift_chip(): return lax.ppermute(v, 'tp', [(i, (i + k) % chips) for i in range(chips)])]
    all_to_all x6 -> x5, waiting for transfers between devices: 34.2 us -> 21.4 us  [exchange(): return lax.all_to_all(v, both, 0, 0, tiled=True)]
    unnamed x26 -> x28, local copies, waits for them, and re-layouts: 7.22 us -> 16.2 us
    all_to_all x6 -> x5, starting transfers between devices: 26.2 us -> 21.2 us  [exchange(): return lax.all_to_all(v, both, 0, 0, tiled=True)]
    pallas_call x8 -> x12, Pallas kernels: 26.7 us -> 25.2 us  [the longest x4 12.2 us: query_stack(): pl.pallas_call(functools.partial(query_kernel, flip, cross), out_shape=ja...]
  transfers between devices with their start and end apart: 9 -> 20, of which waited for: 4 -> 12; matrix products, arithmetic and copies ran while one was open for 6% -> 2% of each run, Pallas kernels for 12% -> 16%
where the time goes in v3:
time: 136 us; the launch traced here: 135 us
  starting transfers between devices  38.3 us (28%)
  waiting for transfers between devices  37.7 us (28%)
  Pallas kernels  29.3 us (22%)
  local copies, waits for them, and re-layouts  16.5 us (12%)
  blocking collectives  9.48 us (7%)
  other arithmetic  1.98 us (1%)
  between operations  1.55 us (1%)
    all_to_all x5, waiting for transfers between devices, exchange(): return lax.all_to_all(v, both, 0, 0, tiled=True)  21.4 us
    all_to_all x5, starting transfers between devices, exchange(): return lax.all_to_all(v, both, 0, 0, tiled=True)  21.2 us
    unnamed x28, local copies, waits for them, and re-layouts  16.2 us
    ppermute x10, starting transfers between devices, shift_chip(): return lax.ppermute(v, 'tp', [(i, (i + k) % chips) for i in range(chips)])  14.8 us
    pallas_call x4, Pallas kernels, query_stack(): pl.pallas_call(functools.partial(query_kernel, flip, cross), out_shape=ja...  12.2 us
    ppermute x10, waiting for transfers between devices, shift_chip(): return lax.ppermute(v, 'tp', [(i, (i + k) % chips) for i in range(chips)])  11 us
    all_to_all x1, blocking collectives, exchange(): return lax.all_to_all(v, both, 0, 0, tiled=True)  9.48 us
    ppermute x1, waiting for transfers between devices, swap_y(): return lax.ppermute(v, 'tp', [(i, i ^ 1) for i in range(chips)])  5.31 us
  transfers between devices with their start and end apart: 20, of which 12 were waited for; matrix products, arithmetic and copies ran while one was open for 2% of the time, Pallas kernels for 16%

profile of v3, /device:TPU:0, one launch (start us, length us, event | category | flops | bytes accessed | tf_op | source)
XLA Modules:
  0.0 134.7 jit_solution(921991182155150814)
XLA Ops:
  0.6 3.1 %collective-permute-start = (bf16[32,1024]{1,0:T(8,128)(2,1)}, bf16[32,1024]{1,0:T(8,128)(2,1)S(1)}, u32[]{:S(2)}, u32[]{:S(2)}) collective-permute-start(bf16[32,1024]{1,0:T(8,128)(2,1)} %bitcast.28), channel_id=1, source_target_pairs={{0,4},{2,6},{4,8},{6,10},{8,12},{10,14},{12,0},{14,2},{1,5},{3,7},... | collective-permute-start | bytes 196616 | tf_op jit(solution)/shard_map/ppermute | solution.py:318
  3.7 2.6 %collective-permute-start.1 = (bf16[32,1024]{1,0:T(8,128)(2,1)}, bf16[32,1024]{1,0:T(8,128)(2,1)S(1)}, u32[]{:S(2)}, u32[]{:S(2)}) collective-permute-start(bf16[32,1024]{1,0:T(8,128)(2,1)} %bitcast.29), channel_id=1, source_target_pairs={{0,8},{2,10},{4,12},{6,14},{8,0},{10,2},{12,4},{14,6},{1,9},{3,11}... | collective-permute-start | bytes 196616 | tf_op jit(solution)/shard_map/ppermute | solution.py:318
  6.3 1.3 %collective-permute-start.2 = (bf16[32,1024]{1,0:T(8,128)(2,1)}, bf16[32,1024]{1,0:T(8,128)(2,1)S(1)}, u32[]{:S(2)}, u32[]{:S(2)}) collective-permute-start(bf16[32,1024]{1,0:T(8,128)(2,1)} %bitcast.30), channel_id=1, source_target_pairs={{0,12},{2,14},{4,0},{6,2},{8,4},{10,6},{12,8},{14,10},{1,13},{3,15... | collective-permute-start | bytes 196616 | tf_op jit(solution)/shard_map/ppermute | solution.py:318
  7.6 0.8 collective-permute-done.refs_1_
  8.5 2.5 %collective-permute-done.1.refs_2_ = bf16[32,1024]{1,0:T(8,128)(2,1)S(1)} collective-permute-done((bf16[32,1024]{1,0:T(8,128)(2,1)}, bf16[32,1024]{1,0:T(8,128)(2,1)S(1)}, u32[]{:S(2)}, u32[]{:S(2)}) %collective-permute-start.1) | collective-permute-done | bytes 65568 | tf_op jit(solution)/shard_map/ppermute | solution.py:318
  11.0 0.2 collective-permute-done.2.refs_3_
  11.2 0.8 copy-done.10
  12.1 1.6 %collective-permute-start.3 = (bf16[4,32,1024]{2,1,0:T(8,128)(2,1)S(1)}, bf16[4,32,1024]{2,1,0:T(8,128)(2,1)S(1)}, u32[]{:S(2)}, u32[]{:S(2)}) collective-permute-start(bf16[4,32,1024]{2,1,0:T(8,128)(2,1)S(1)} %shard_map.158.refs_2_.a_ref.dep_ref), channel_id=1, source_target_pairs={{0,2},{2,0},{4,6},{6,4},{8,10},{10,8},{12,14},{14,12},{1,3},{3,1},... | collective-permute-start | bytes 786440 | tf_op jit(solution)/shard_map/ppermute | solution.py:313
  13.7 0.9 select_reduce_fusion
  14.6 5.3 %collective-permute-done.3.refs_2_.b_ref = bf16[4,32,1024]{2,1,0:T(8,128)(2,1)S(1)} collective-permute-done((bf16[4,32,1024]{2,1,0:T(8,128)(2,1)S(1)}, bf16[4,32,1024]{2,1,0:T(8,128)(2,1)S(1)}, u32[]{:S(2)}, u32[]{:S(2)}) %collective-permute-start.3) | collective-permute-done | bytes 262176 | tf_op jit(solution)/shard_map/ppermute | solution.py:313
  20.0 0.1 convert_element_type.22.own_ref
  20.0 0.1 pad_add_fusion.refs_0_.at_ref
  20.1 1.4 %copy-done.1 = bf16[1,48,16384]{2,1,0:T(8,128)(2,1)S(1)} copy-done((bf16[1,48,16384]{2,1,0:T(8,128)(2,1)S(1)}, bf16[1,48,16384]{2,1,0:T(8,128)(2,1)}, u32[]{:S(2)}) %copy-start.1) | copy-done | bytes 1572888
  21.5 1.0 shard_map.163.early_ref
  22.6 1.4 %copy-done.2 = bf16[1,48,16384]{2,1,0:T(8,128)(2,1)S(1)} copy-done((bf16[1,48,16384]{2,1,0:T(8,128)(2,1)S(1)}, bf16[1,48,16384]{2,1,0:T(8,128)(2,1)}, u32[]{:S(2)}) %copy-start.2) | copy-done | bytes 1572888
  24.0 1.4 %shard_map.164 = (bf16[16,16,128]{2,1,0:T(8,128)(2,1)}, bf16[32,32]{1,0:T(8,128)(2,1)S(1)}) custom-call(s32[2]{0:T(128)S(1)} %pad_add_fusion.refs_0_.at_ref, bf16[48,16384]{1,0:T(8,128)(2,1)S(1)} %bitcast.21, bf16[4,32,1024]{2,1,0:T(8,128)(2,1)S(1)} %collective-permute-done.4.refs_2_.x_ref, f32[48,32]{1,0:T(8,128)S(1)} %shard_map.163.early_ref, ...), custom_call_target="tpu_custom_call" | custom-call | tf_op jit(solution)/shard_map/pallas_call | solution.py:365
  25.4 4.1 %all-to-all-start = ((bf16[16,16,128]{2,1,0:T(8,128)(2,1)}), bf16[16,16,128]{2,1,0:T(8,128)(2,1)S(1)}, u32[]{:S(2)}, u32[]{:S(2)}) async-start(bf16[16,16,128]{2,1,0:T(8,128)(2,1)} %get-tuple-element.18), calls=%async_computation | async-start | bytes 131072 | tf_op jit(solution)/shard_map/all_to_all | solution.py:321
  29.5 1.0 copy-done.4
  30.6 0.9 copy-done.8
  31.5 0.9 copy-done.9
  32.5 1.4 %shard_map.165 = (bf16[16,32,512]{2,1,0:T(8,128)(2,1)}, bf16[8,16,1024]{2,1,0:T(8,128)(2,1)S(1)}) custom-call(s32[2]{0:T(128)S(1)} %pad_add_fusion.refs_0_.at_ref, bf16[16,8192]{1,0:T(8,128)(2,1)S(1)} %bitcast.26, bf16[16,8192]{1,0:T(8,128)(2,1)S(1)} %bitcast.27, bf16[16,16384]{1,0:T(8,128)(2,1)S(1)} %bitcast.22, ...), custom_call_target="tpu_custom_call" | custom-call | tf_op jit(solution)/shard_map/pallas_call | solution.py:343
  33.9 2.6 %all-to-all-done.ranks_ref = bf16[16,16,128]{2,1,0:T(8,128)(2,1)S(1)} async-done(((bf16[16,16,128]{2,1,0:T(8,128)(2,1)}), bf16[16,16,128]{2,1,0:T(8,128)(2,1)S(1)}, u32[]{:S(2)}, u32[]{:S(2)}) %all-to-all-start) | async-done | bytes 65568 | tf_op jit(solution)/shard_map/all_to_all | solution.py:321
  36.4 3.6 %all-to-all-start.1 = ((bf16[16,32,512]{2,1,0:T(8,128)(2,1)}), bf16[16,32,512]{2,1,0:T(8,128)(2,1)S(1)}, u32[]{:S(2)}, u32[]{:S(2)}) async-start(bf16[16,32,512]{2,1,0:T(8,128)(2,1)} %get-tuple-element.19), calls=%async_computation.1 | async-start | bytes 1048576 | tf_op jit(solution)/shard_map/all_to_all | solution.py:321
  40.7 1.6 %copy-done.3 = bf16[1024,1024]{1,0:T(8,128)(2,1)S(1)} copy-done((bf16[1024,1024]{1,0:T(8,128)(2,1)S(1)}, bf16[1024,1024]{1,0:T(8,128)(2,1)}, u32[]{:S(2)}) %copy-start.3) | copy-done | bytes 2097176
  42.3 0.8 copy-done.11
  43.1 0.7 copy-done.12
  43.8 0.7 copy-done.13
  44.5 1.2 shard_map.166.dep_ref
  45.7 8.7 %all-to-all-done.1.up_ref.low_ref = bf16[16,32,512]{2,1,0:T(8,128)(2,1)S(1)} async-done(((bf16[16,32,512]{2,1,0:T(8,128)(2,1)}), bf16[16,32,512]{2,1,0:T(8,128)(2,1)S(1)}, u32[]{:S(2)}, u32[]{:S(2)}) %all-to-all-start.1) | async-done | bytes 524320 | tf_op jit(solution)/shard_map/all_to_all | solution.py:321
  54.4 4.0 %all-to-all-start.3 = ((f32[16,2,1024]{2,1,0:T(2,128)}), f32[16,2,1024]{2,1,0:T(2,128)S(1)}, u32[]{:S(2)}, u32[]{:S(2)}) async-start(f32[16,2,1024]{2,1,0:T(2,128)} %shard_map.166.dep_ref), calls=%async_computation.3 | async-start | bytes 262144 | tf_op jit(solution)/shard_map/all_to_all | solution.py:321
  58.5 0.1 eq.66
  58.6 0.1 eq.64
  58.7 0.1 compare_convert_fusion.mask_ref
  58.8 3.1 %shard_map.159.refs_3_ = f32[32,512]{1,0:T(8,128)S(1)} custom-call(s32[2]{0:T(128)S(1)} %pad_add_fusion.refs_0_.at_ref, bf16[16384,512]{1,0:T(8,128)(2,1)} %refs_1_.7, bf16[4,32,1024]{2,1,0:T(8,128)(2,1)S(1)} %shard_map.158.refs_2_.a_ref.dep_ref), custom_call_target="tpu_custom_call" | custom-call | tf_op jit(solution)/shard_map/pallas_call | solution.py:74
  61.8 3.1 %shard_map.160.refs_3_ = f32[32,512]{1,0:T(8,128)S(1)} custom-call(s32[2]{0:T(128)S(1)} %pad_add_fusion.refs_0_.at_ref, bf16[16384,512]{1,0:T(8,128)(2,1)} %refs_1_.7, bf16[4,32,1024]{2,1,0:T(8,128)(2,1)S(1)} %collective-permute-done.5.refs_2_.c_ref, f32[32,512]{1,0:T(8,128)S(1)} %shard_map.159.refs_3_), custom_call_target="tpu_custom_call" | custom-call | tf_op jit(solution)/shard_map/pallas_call | solution.py:74
  64.9 3.1 %shard_map.161.refs_3_ = f32[32,512]{1,0:T(8,128)S(1)} custom-call(s32[2]{0:T(128)S(1)} %pad_add_fusion.refs_0_.at_ref, bf16[16384,512]{1,0:T(8,128)(2,1)} %refs_1_.7, bf16[4,32,1024]{2,1,0:T(8,128)(2,1)S(1)} %collective-permute-done.3.refs_2_.b_ref, f32[32,512]{1,0:T(8,128)S(1)} %shard_map.160.refs_3_), custom_call_target="tpu_custom_call" | custom-call | tf_op jit(solution)/shard_map/pallas_call | solution.py:74
  68.0 3.1 %shard_map.162.q_ref = f32[32,512]{1,0:T(8,128)S(1)} custom-call(s32[2]{0:T(128)S(1)} %pad_add_fusion.refs_0_.at_ref, bf16[16384,512]{1,0:T(8,128)(2,1)} %refs_1_.7, bf16[4,32,1024]{2,1,0:T(8,128)(2,1)S(1)} %collective-permute-done.4.refs_2_.x_ref, f32[32,512]{1,0:T(8,128)S(1)} %shard_map.161.refs_3_), custom_call_target="tpu_custom_call" | custom-call | tf_op jit(solution)/shard_map/pallas_call | solution.py:74
  71.0 0.8 shard_map.167
  71.9 6.0 %all-to-all-start.2 = ((f32[16,2,512]{2,1,0:T(2,128)}), f32[16,2,512]{2,1,0:T(2,128)S(1)}, u32[]{:S(2)}, u32[]{:S(2)}) async-start(f32[16,2,512]{2,1,0:T(2,128)} %shard_map.167), calls=%async_computation.2 | async-start | bytes 131072 | tf_op jit(solution)/shard_map/all_to_all | solution.py:321
  77.9 0.1 fusion
  78.0 0.1 pad_maximum_fusion
  78.1 6.7 %all-to-all-done.2.recv_ref = f32[16,2,512]{2,1,0:T(2,128)S(1)} async-done(((f32[16,2,512]{2,1,0:T(2,128)}), f32[16,2,512]{2,1,0:T(2,128)S(1)}, u32[]{:S(2)}, u32[]{:S(2)}) %all-to-all-start.2) | async-done | bytes 65568 | tf_op jit(solution)/shard_map/all_to_all | solution.py:321
  84.8 1.6 %shard_map.168 = (f32[16,2,512]{2,1,0:T(2,128)S(1)}, f32[2,1024]{1,0:T(2,128)S(1)}) custom-call(s32[1]{0:T(128)} %copy.17.len_ref, f32[16,2,512]{2,1,0:T(2,128)S(1)} %all-to-all-done.2.recv_ref, f32[16,2,1024]{2,1,0:T(2,128)S(1)} %all-to-all-done.3.kv_ref, f32[32,128]{1,0:T(8,128)S(1)} %bitcast.33, f32[32,128]{1,0:T(8,128)S(1)} %bitcast.34, ...), custom_call_target="tpu_custom_call" | custom-call | tf_op jit(solution)/shard_map/pallas_call | solution.py:400
  86.4 9.5 %all_to_all.30.ctx_ref = f32[16,2,512]{2,1,0:T(2,128)S(1)} all-to-all(f32[16,2,512]{2,1,0:T(2,128)S(1)} %get-tuple-element.21), channel_id=1, replica_groups=mesh['groups'=2,'tp'=8,'sub'=2] {'tp','sub'}, dimensions={0} | all-to-all | bytes 131072 | tf_op jit(solution)/shard_map/all_to_all | solution.py:321
  95.9 0.9 shard_map.169
  96.8 5.8 %copy-done = bf16[512,16384]{1,0:T(8,128)(2,1)S(1)} copy-done((bf16[512,16384]{1,0:T(8,128)(2,1)S(1)}, bf16[512,16384]{1,0:T(8,128)(2,1)}, u32[]{:S(2)}) %copy-start) | copy-done | bytes 16777240
  102.6 2.1 %shard_map.171 = f32[8,32,1024]{2,1,0:T(8,128)S(1)} custom-call(s32[2]{0:T(128)S(1)} %pad_add_fusion.refs_0_.at_ref, bf16[32,512]{1,0:T(8,128)(2,1)S(1)} %get-tuple-element.22.x_ref, bf16[512,16384]{1,0:T(8,128)(2,1)S(1)} %copy-done), custom_call_target="tpu_custom_call" | custom-call | tf_op jit(solution)/shard_map/pallas_call | solution.py:428
  104.7 0.5 collective-permute-start.7
  105.2 3.5 %all-to-all-start.5 = ((f32[16,16,128]{2,1,0:T(8,128)}), f32[16,16,128]{2,1,0:T(8,128)S(1)}, u32[]{:S(2)}, u32[]{:S(2)}) async-start(f32[16,16,128]{2,1,0:T(8,128)} %get-tuple-element.24), calls=%async_computation.5 | async-start | bytes 262144 | tf_op jit(solution)/shard_map/all_to_all | solution.py:321
  108.7 0.1 pad_add_fusion.1
  108.9 4.3 %shard_map.170.a_ref = f32[8,32,1024]{2,1,0:T(8,128)S(1)} custom-call(s32[2]{0:T(128)S(1)} %pad_add_fusion.refs_0_.at_ref, bf16[32,512]{1,0:T(8,128)(2,1)S(1)} %get-tuple-element.22.x_ref, bf16[512,16384]{1,0:T(8,128)(2,1)} %w_ref.5), custom_call_target="tpu_custom_call" | custom-call | tf_op jit(solution)/shard_map/pallas_call | solution.py:435
  113.2 3.4 %all-to-all-done.5.parts_ref = f32[16,16,128]{2,1,0:T(8,128)S(1)} async-done(((f32[16,16,128]{2,1,0:T(8,128)}), f32[16,16,128]{2,1,0:T(8,128)S(1)}, u32[]{:S(2)}, u32[]{:S(2)}) %all-to-all-start.5) | async-done | bytes 131104 | tf_op jit(solution)/shard_map/all_to_all | solution.py:321
  116.6 1.6 %shard_map.172 = (bf16[32,1024]{1,0:T(8,128)(2,1)S(1)}, bf16[32,1024]{1,0:T(8,128)(2,1)S(1)}, bf16[32,1024]{1,0:T(8,128)(2,1)S(1)}, bf16[32,1024]{1,0:T(8,128)(2...) custom-call(s32[2]{0:T(128)S(1)} %pad_add_fusion.refs_0_.at_ref, ...), custom_call_target="tpu_custom_call" | custom-call | tf_op jit(solution)/shard_map/pallas_call | solution.py:445
  118.3 1.8 %collective-permute-start.11 = (bf16[32,1024]{1,0:T(8,128)(2,1)S(1)}, bf16[32,1024]{1,0:T(8,128)(2,1)S(1)}, u32[]{:S(2)}, u32[]{:S(2)}) collective-permute-start(bf16[32,1024]{1,0:T(8,128)(2,1)S(1)} %get-tuple-element.29), channel_id=1, source_target_pairs={{0,8},{2,10},{4,12},{6,14},{8,0},{10,2},{12,4},{14,6},{1,9},{3,11}... | collective-permute-start | bytes 196616 | tf_op jit(solution)/shard_map/ppermute | solution.py:318
  120.1 2.4 %collective-permute-start.12 = (bf16[32,1024]{1,0:T(8,128)(2,1)S(1)}, bf16[32,1024]{1,0:T(8,128)(2,1)S(1)}, u32[]{:S(2)}, u32[]{:S(2)}) collective-permute-start(bf16[32,1024]{1,0:T(8,128)(2,1)S(1)} %get-tuple-element.30), channel_id=1, source_target_pairs={{0,10},{2,12},{4,14},{6,0},{8,2},{10,4},{12,6},{14,8},{1,11},{3,13... | collective-permute-start | bytes 196616 | tf_op jit(solution)/shard_map/ppermute | solution.py:318
  122.4 1.4 %collective-permute-start.13 = (bf16[32,1024]{1,0:T(8,128)(2,1)S(1)}, bf16[32,1024]{1,0:T(8,128)(2,1)S(1)}, u32[]{:S(2)}, u32[]{:S(2)}) collective-permute-start(bf16[32,1024]{1,0:T(8,128)(2,1)S(1)} %get-tuple-element.31), channel_id=1, source_target_pairs={{0,12},{2,14},{4,0},{6,2},{8,4},{10,6},{12,8},{14,10},{1,13},{3,15... | collective-permute-start | bytes 196616 | tf_op jit(solution)/shard_map/ppermute | solution.py:318
  123.9 1.4 %collective-permute-start.14 = (bf16[32,1024]{1,0:T(8,128)(2,1)S(1)}, bf16[32,1024]{1,0:T(8,128)(2,1)S(1)}, u32[]{:S(2)}, u32[]{:S(2)}) collective-permute-start(bf16[32,1024]{1,0:T(8,128)(2,1)S(1)} %get-tuple-element.32), channel_id=1, source_target_pairs={{0,14},{2,0},{4,2},{6,4},{8,6},{10,8},{12,10},{14,12},{1,15},{3,1}... | collective-permute-start | bytes 196616 | tf_op jit(solution)/shard_map/ppermute | solution.py:318
  125.3 1.2 collective-permute-done.10.refs_3_
  126.5 1.4 %collective-permute-done.11.refs_4_ = bf16[32,1024]{1,0:T(8,128)(2,1)S(1)} collective-permute-done((bf16[32,1024]{1,0:T(8,128)(2,1)S(1)}, bf16[32,1024]{1,0:T(8,128)(2,1)S(1)}, u32[]{:S(2)}, u32[]{:S(2)}) %collective-permute-start.11) | collective-permute-done | bytes 65568 | tf_op jit(solution)/shard_map/ppermute | solution.py:318
  127.9 0.7 collective-permute-start.9
  128.7 0.6 convert_bitcast_fusion
  129.3 4.5 %collective-permute-done.8.refs_1_ = bf16[32,1024]{1,0:T(8,128)(2,1)S(1)} collective-permute-done((bf16[32,1024]{1,0:T(8,128)(2,1)S(1)}, bf16[32,1024]{1,0:T(8,128)(2,1)S(1)}, u32[]{:S(2)}, u32[]{:S(2)}) %collective-permute-start.8) | collective-permute-done | bytes 65568 | tf_op jit(solution)/shard_map/ppermute | solution.py:318
  133.8 0.3 collective-permute-done.9.refs_2_
  134.0 0.7 shard_map.173
  (40 shorter events, 0.3 us)
Async XLA Ops:
  0.6 7.8 %collective-permute-start = (bf16[32,1024]{1,0:T(8,128)(2,1)}, bf16[32,1024]{1,0:T(8,128)(2,1)S(1)}, u32[]{:S(2)}, u32[]{:S(2)}) collective-permute-start(bf16[32,1024]{1,0:T(8,128)(2,1)} %bitcast.28), channel_id=1, source_target_pairs={{0,4},{2,6},{4,8},{6,10},{8,12},{10,14},{12,0},{14,2},{1,5},{3,7},... | collective-permute-start | bytes 196616 | tf_op jit(solution)/shard_map/ppermute | solution.py:318
  3.7 7.3 %collective-permute-start.1 = (bf16[32,1024]{1,0:T(8,128)(2,1)}, bf16[32,1024]{1,0:T(8,128)(2,1)S(1)}, u32[]{:S(2)}, u32[]{:S(2)}) collective-permute-start(bf16[32,1024]{1,0:T(8,128)(2,1)} %bitcast.29), channel_id=1, source_target_pairs={{0,8},{2,10},{4,12},{6,14},{8,0},{10,2},{12,4},{14,6},{1,9},{3,11}... | collective-permute-start | bytes 196616 | tf_op jit(solution)/shard_map/ppermute | solution.py:318
  6.3 4.9 %collective-permute-start.2 = (bf16[32,1024]{1,0:T(8,128)(2,1)}, bf16[32,1024]{1,0:T(8,128)(2,1)S(1)}, u32[]{:S(2)}, u32[]{:S(2)}) collective-permute-start(bf16[32,1024]{1,0:T(8,128)(2,1)} %bitcast.30), channel_id=1, source_target_pairs={{0,12},{2,14},{4,0},{6,2},{8,4},{10,6},{12,8},{14,10},{1,13},{3,15... | collective-permute-start | bytes 196616 | tf_op jit(solution)/shard_map/ppermute | solution.py:318
  11.2 0.8 copy-start.10
  12.1 7.9 %collective-permute-start.3 = (bf16[4,32,1024]{2,1,0:T(8,128)(2,1)S(1)}, bf16[4,32,1024]{2,1,0:T(8,128)(2,1)S(1)}, u32[]{:S(2)}, u32[]{:S(2)}) collective-permute-start(bf16[4,32,1024]{2,1,0:T(8,128)(2,1)S(1)} %shard_map.158.refs_2_.a_ref.dep_ref), channel_id=1, source_target_pairs={{0,2},{2,0},{4,6},{6,4},{8,10},{10,8},{12,14},{14,12},{1,3},{3,1},... | collective-permute-start | bytes 786440 | tf_op jit(solution)/shard_map/ppermute | solution.py:313
  14.6 5.6 %collective-permute-start.5 = (bf16[4,32,1024]{2,1,0:T(8,128)(2,1)S(1)}, bf16[4,32,1024]{2,1,0:T(8,128)(2,1)S(1)}, u32[]{:S(2)}, u32[]{:S(2)}) collective-permute-start(bf16[4,32,1024]{2,1,0:T(8,128)(2,1)S(1)} %shard_map.158.refs_2_.a_ref.dep_ref), channel_id=1, source_target_pairs={{0,1},{1,0},{2,3},{3,2},{4,5},{5,4},{6,7},{7,6},{8,9},{9,8},{10,11... | collective-permute-start | bytes 786440 | tf_op jit(solution)/shard_map/ppermute | solution.py:310
  19.9 2.6 %collective-permute-start.4 = (bf16[4,32,1024]{2,1,0:T(8,128)(2,1)S(1)}, bf16[4,32,1024]{2,1,0:T(8,128)(2,1)S(1)}, u32[]{:S(2)}, u32[]{:S(2)}) collective-permute-start(bf16[4,32,1024]{2,1,0:T(8,128)(2,1)S(1)} %collective-permute-done.3.refs_2_.b_ref), channel_id=1, source_target_pairs={{0,1},{1,0},{2,3},{3,2},{4,5},{5,4},{6,7},{7,6},{8,9},{9,8},{10,11... | collective-permute-start | bytes 786440 | tf_op jit(solution)/shard_map/ppermute | solution.py:310
  20.1 1.4 %copy-start.1 = (bf16[1,48,16384]{2,1,0:T(8,128)(2,1)S(1)}, bf16[1,48,16384]{2,1,0:T(8,128)(2,1)}, u32[]{:S(2)}) copy-start(bf16[1,48,16384]{2,1,0:T(8,128)(2,1)} %param.24) | copy-start | bytes 4718596
  22.5 1.4 %copy-start.2 = (bf16[1,48,16384]{2,1,0:T(8,128)(2,1)S(1)}, bf16[1,48,16384]{2,1,0:T(8,128)(2,1)}, u32[]{:S(2)}) copy-start(bf16[1,48,16384]{2,1,0:T(8,128)(2,1)} %param.24) | copy-start | bytes 4718596
  25.4 11.0 %all-to-all-start = ((bf16[16,16,128]{2,1,0:T(8,128)(2,1)}), bf16[16,16,128]{2,1,0:T(8,128)(2,1)S(1)}, u32[]{:S(2)}, u32[]{:S(2)}) async-start(bf16[16,16,128]{2,1,0:T(8,128)(2,1)} %get-tuple-element.18), calls=%async_computation | async-start | bytes 131072 | tf_op jit(solution)/shard_map/all_to_all | solution.py:321
  29.5 1.0 copy-start.4
  30.6 0.9 copy-start.8
  31.5 0.9 copy-start.9
  36.4 18.0 %all-to-all-start.1 = ((bf16[16,32,512]{2,1,0:T(8,128)(2,1)}), bf16[16,32,512]{2,1,0:T(8,128)(2,1)S(1)}, u32[]{:S(2)}, u32[]{:S(2)}) async-start(bf16[16,32,512]{2,1,0:T(8,128)(2,1)} %get-tuple-element.19), calls=%async_computation.1 | async-start | bytes 1048576 | tf_op jit(solution)/shard_map/all_to_all | solution.py:321
  40.7 1.6 %copy-start.3 = (bf16[1024,1024]{1,0:T(8,128)(2,1)S(1)}, bf16[1024,1024]{1,0:T(8,128)(2,1)}, u32[]{:S(2)}) copy-start(bf16[1024,1024]{1,0:T(8,128)(2,1)} %w_ref.3) | copy-start | bytes 6291460
  42.3 0.8 copy-start.11
  43.1 0.7 copy-start.12
  43.8 0.7 copy-start.13
  54.4 17.4 %all-to-all-start.3 = ((f32[16,2,1024]{2,1,0:T(2,128)}), f32[16,2,1024]{2,1,0:T(2,128)S(1)}, u32[]{:S(2)}, u32[]{:S(2)}) async-start(f32[16,2,1024]{2,1,0:T(2,128)} %shard_map.166.dep_ref), calls=%async_computation.3 | async-start | bytes 262144 | tf_op jit(solution)/shard_map/all_to_all | solution.py:321
  64.9 19.9 %copy-start.6 = (bf16[1,512,512]{2,1,0:T(8,128)(2,1)S(1)}, bf16[1,512,512]{2,1,0:T(8,128)(2,1)}, u32[]{:S(2)}) copy-start(bf16[1,512,512]{2,1,0:T(8,128)(2,1)} %param.19) | copy-start | bytes 1572868
  64.9 19.9 %copy-start.7 = (bf16[1,512,512]{2,1,0:T(8,128)(2,1)S(1)}, bf16[1,512,512]{2,1,0:T(8,128)(2,1)}, u32[]{:S(2)}) copy-start(bf16[1,512,512]{2,1,0:T(8,128)(2,1)} %param.20) | copy-start | bytes 1572868
  71.9 12.9 %all-to-all-start.2 = ((f32[16,2,512]{2,1,0:T(2,128)}), f32[16,2,512]{2,1,0:T(2,128)S(1)}, u32[]{:S(2)}, u32[]{:S(2)}) async-start(f32[16,2,512]{2,1,0:T(2,128)} %shard_map.167), calls=%async_computation.2 | async-start | bytes 131072 | tf_op jit(solution)/shard_map/all_to_all | solution.py:321
  96.8 5.8 %copy-start = (bf16[512,16384]{1,0:T(8,128)(2,1)S(1)}, bf16[512,16384]{1,0:T(8,128)(2,1)}, u32[]{:S(2)}) copy-start(bf16[512,16384]{1,0:T(8,128)(2,1)} %w_ref.5) | copy-start | bytes 50331652
  102.6 14.1 %copy-start.5 = (bf16[1,16,16384]{2,1,0:T(8,128)(2,1)S(1)}, bf16[1,16,16384]{2,1,0:T(8,128)(2,1)}, u32[]{:S(2)}) copy-start(bf16[1,16,16384]{2,1,0:T(8,128)(2,1)} %param.29) | copy-start | bytes 1572868
  104.7 11.9 %collective-permute-start.6 = (f32[8,32,1024]{2,1,0:T(8,128)S(1)}, f32[8,32,1024]{2,1,0:T(8,128)}, u32[]{:S(2)}, u32[]{:S(2)}) collective-permute-start(f32[8,32,1024]{2,1,0:T(8,128)S(1)} %shard_map.171), channel_id=1, source_target_pairs={{0,1},{1,0},{2,3},{3,2},{4,5},{5,4},{6,7},{7,6},{8,9},{9,8},{10,11... | collective-permute-start | bytes 3145736 | tf_op jit(solution)/shard_map/ppermute | solution.py:310
  104.7 8.5 %collective-permute-start.7 = (bf16[8,16,1024]{2,1,0:T(8,128)(2,1)S(1)}, bf16[8,16,1024]{2,1,0:T(8,128)(2,1)S(1)}, u32[]{:S(2)}, u32[]{:S(2)}) collective-permute-start(bf16[8,16,1024]{2,1,0:T(8,128)(2,1)S(1)} %get-tuple-element.23), channel_id=1, source_target_pairs={{0,1},{1,0},{2,3},{3,2},{4,5},{5,4},{6,7},{7,6},{8,9},{9,8},{10,11... | collective-permute-start | bytes 786440 | tf_op jit(solution)/shard_map/ppermute | solution.py:310
  105.2 11.4 %all-to-all-start.5 = ((f32[16,16,128]{2,1,0:T(8,128)}), f32[16,16,128]{2,1,0:T(8,128)S(1)}, u32[]{:S(2)}, u32[]{:S(2)}) async-start(f32[16,16,128]{2,1,0:T(8,128)} %get-tuple-element.24), calls=%async_computation.5 | async-start | bytes 262144 | tf_op jit(solution)/shard_map/all_to_all | solution.py:321
  118.2 8.3 %collective-permute-start.10 = (bf16[32,1024]{1,0:T(8,128)(2,1)S(1)}, bf16[32,1024]{1,0:T(8,128)(2,1)S(1)}, u32[]{:S(2)}, u32[]{:S(2)}) collective-permute-start(bf16[32,1024]{1,0:T(8,128)(2,1)S(1)} %get-tuple-element.28), channel_id=1, source_target_pairs={{0,6},{2,8},{4,10},{6,12},{8,14},{10,0},{12,2},{14,4},{1,7},{3,9},... | collective-permute-start | bytes 196616 | tf_op jit(solution)/shard_map/ppermute | solution.py:318
  118.3 9.7 %collective-permute-start.11 = (bf16[32,1024]{1,0:T(8,128)(2,1)S(1)}, bf16[32,1024]{1,0:T(8,128)(2,1)S(1)}, u32[]{:S(2)}, u32[]{:S(2)}) collective-permute-start(bf16[32,1024]{1,0:T(8,128)(2,1)S(1)} %get-tuple-element.29), channel_id=1, source_target_pairs={{0,8},{2,10},{4,12},{6,14},{8,0},{10,2},{12,4},{14,6},{1,9},{3,11}... | collective-permute-start | bytes 196616 | tf_op jit(solution)/shard_map/ppermute | solution.py:318
  120.1 9.2 %collective-permute-start.12 = (bf16[32,1024]{1,0:T(8,128)(2,1)S(1)}, bf16[32,1024]{1,0:T(8,128)(2,1)S(1)}, u32[]{:S(2)}, u32[]{:S(2)}) collective-permute-start(bf16[32,1024]{1,0:T(8,128)(2,1)S(1)} %get-tuple-element.30), channel_id=1, source_target_pairs={{0,10},{2,12},{4,14},{6,0},{8,2},{10,4},{12,6},{14,8},{1,11},{3,13... | collective-permute-start | bytes 196616 | tf_op jit(solution)/shard_map/ppermute | solution.py:318
  122.4 6.8 %collective-permute-start.13 = (bf16[32,1024]{1,0:T(8,128)(2,1)S(1)}, bf16[32,1024]{1,0:T(8,128)(2,1)S(1)}, u32[]{:S(2)}, u32[]{:S(2)}) collective-permute-start(bf16[32,1024]{1,0:T(8,128)(2,1)S(1)} %get-tuple-element.31), channel_id=1, source_target_pairs={{0,12},{2,14},{4,0},{6,2},{8,4},{10,6},{12,8},{14,10},{1,13},{3,15... | collective-permute-start | bytes 196616 | tf_op jit(solution)/shard_map/ppermute | solution.py:318
  123.9 5.4 %collective-permute-start.14 = (bf16[32,1024]{1,0:T(8,128)(2,1)S(1)}, bf16[32,1024]{1,0:T(8,128)(2,1)S(1)}, u32[]{:S(2)}, u32[]{:S(2)}) collective-permute-start(bf16[32,1024]{1,0:T(8,128)(2,1)S(1)} %get-tuple-element.32), channel_id=1, source_target_pairs={{0,14},{2,0},{4,2},{6,4},{8,6},{10,8},{12,10},{14,12},{1,15},{3,1}... | collective-permute-start | bytes 196616 | tf_op jit(solution)/shard_map/ppermute | solution.py:318
  126.5 7.2 %collective-permute-start.8 = (bf16[32,1024]{1,0:T(8,128)(2,1)S(1)}, bf16[32,1024]{1,0:T(8,128)(2,1)S(1)}, u32[]{:S(2)}, u32[]{:S(2)}) collective-permute-start(bf16[32,1024]{1,0:T(8,128)(2,1)S(1)} %get-tuple-element.26), channel_id=1, source_target_pairs={{0,2},{2,4},{4,6},{6,8},{8,10},{10,12},{12,14},{14,0},{1,3},{3,5},... | collective-permute-start | bytes 196616 | tf_op jit(solution)/shard_map/ppermute | solution.py:318
  127.9 6.1 %collective-permute-start.9 = (bf16[32,1024]{1,0:T(8,128)(2,1)S(1)}, bf16[32,1024]{1,0:T(8,128)(2,1)S(1)}, u32[]{:S(2)}, u32[]{:S(2)}) collective-permute-start(bf16[32,1024]{1,0:T(8,128)(2,1)S(1)} %get-tuple-element.27), channel_id=1, source_target_pairs={{0,4},{2,6},{4,8},{6,10},{8,12},{10,14},{12,0},{14,2},{1,5},{3,7},... | collective-permute-start | bytes 196616 | tf_op jit(solution)/shard_map/ppermute | solution.py:318

commit v4 on v3

v4 whole, which is shorter than its diff:
```python
import functools
import math

import jax
import jax.numpy as jnp
from jax import lax
from jax.experimental import pallas as pl
from jax.experimental.pallas import tpu as pltpu
from jax.sharding import PartitionSpec as P

HEAD_WIDTH = 128
ROPE_BASE = 500000.0
MASKED = -1e30
SCALE = 0.5
F32 = jnp.float32
BF16 = jnp.bfloat16

PARAMS = pltpu.CompilerParams(vmem_limit_bytes=16 * 1024 * 1024)


def nn(a, b):
    return lax.dot_general(a, b, (((1,), (0,)), ((), ())), preferred_element_type=F32)


def nt(a, b):
    return lax.dot_general(a, b, (((1,), (1,)), ((), ())), preferred_element_type=F32)


def tn(a, b):
    return lax.dot_general(a, b, (((0,), (0,)), ((), ())), preferred_element_type=F32)


WIDE = pltpu.CompilerParams(vmem_limit_bytes=52 * 1024 * 1024)
VMEM = pl.BlockSpec(memory_space=pltpu.VMEM)
SMEM = pl.BlockSpec(memory_space=pltpu.SMEM)
ANY = pl.BlockSpec(memory_space=pl.ANY)
KINDS = ((False, False), (True, False), (False, True), (True, True))


def piece_at(at_ref, chips, k, flip, cross):
    lines = chips // 2
    z = lax.rem(at_ref[0] // 2 + lines - k, lines)
    y = lax.rem(at_ref[0], 2)
    core = 1 - at_ref[1] if cross else at_ref[1]
    return 4 * z + 2 * (1 - y if flip else y) + core


def stack_kernel(*refs):
    for k, r in enumerate(refs[:-1]):
        refs[-1][k] = r[...]


def stack(pieces):
    return pl.pallas_call(
        stack_kernel,
        out_shape=jax.ShapeDtypeStruct((len(pieces),) + pieces[0].shape, pieces[0].dtype),
        compiler_params=PARAMS,
    )(*pieces)


def query_kernel(at_ref, w_ref, a_ref, b_ref, c_ref, d_ref, dep_ref, q_ref, w_s, sems):
    lines, _, width = a_ref.shape
    copies = []
    for flip, cross in KINDS:
        for k in range(lines):
            i = len(copies)
            start = pl.multiple_of(piece_at(at_ref, 2 * lines, k, flip, cross) * width, width)
            copy = pltpu.make_async_copy(w_ref.at[pl.ds(start, width)], w_s.at[i], sems.at[i])
            copy.start()
            copies.append(copy)
    total = None
    for i, copy in enumerate(copies):
        x_ref = (a_ref, b_ref, c_ref, d_ref)[i // lines]
        copy.wait()
        part = nn(x_ref[i % lines], w_s[i])
        total = part if total is None else total + part
    q_ref[...] = total


def rank_kernel(at_ref, d_ref, a_ref, b_ref, c_ref, e_ref, own_ref, dep_ref, send_ref, rest_ref):
    lines, rows, width = a_ref.shape
    devices, rank, _ = send_ref.shape
    total = None
    for x_ref, (flip, cross) in zip((a_ref, b_ref, c_ref, e_ref), KINDS):
        for k in range(lines):
            start = pl.multiple_of(piece_at(at_ref, 2 * lines, k, flip, cross) * width, width)
            part = nt(d_ref[:, pl.ds(start, width)], x_ref[k])
            total = part if total is None else total + part
    total = total.astype(BF16).astype(F32) * own_ref[...]
    rest_ref[...] = total[rank:].astype(BF16)
    first = total[:rank].astype(BF16)
    if rows < send_ref.shape[2]:
        send_ref[...] = jnp.zeros_like(send_ref)
    for d in range(devices):
        send_ref[d, :, :rows] = first


def split_kernel(q_ref, heads_ref):
    devices, _, cols = heads_ref.shape
    for d in range(devices):
        heads_ref[d] = q_ref[:, d * cols : (d + 1) * cols]


def kv_kernel(x_ref, w_ref, own_ref, kup_ref, vup_ref, o_ref):
    rank, half = kup_ref.shape
    own = own_ref[...]
    both = nn(x_ref[...], w_ref[...])
    o_ref[:, :half] = both[:, :half] + SCALE * tn(own[:rank], kup_ref[...])
    o_ref[:, half:] = both[:, half:] + SCALE * tn(own[rank:], vup_ref[...])


def finish_kernel(q_ref, kv_ref, ranks_ref, mask_ref, up_ref, o_ref):
    devices, steps, _ = o_ref.shape
    rows, cols = q_ref.shape
    u = ranks_ref[0].astype(F32)
    for d in range(1, devices):
        u = u + ranks_ref[d].astype(F32)
    u = u[:, :rows]
    spread = (jnp.concatenate([u] * devices, axis=0) * mask_ref[...]).astype(BF16)
    up = jnp.concatenate([up_ref[d] for d in range(devices)], axis=0)
    query = q_ref[...] + SCALE * tn(spread, up)
    for r in range(devices):
        for t in range(steps):
            m = t * devices + r
            o_ref[r, t : t + 1, :cols] = query[m : m + 1]
            o_ref[r, t : t + 1, cols:] = kv_ref[m : m + 1, :]


def rope(v, cosine, sine):
    return v * cosine + pltpu.roll(v, HEAD_WIDTH // 2, 1) * sine


def attend_kernel(len_ref, recv_ref, cos_ref, sin_ref, k_ref, v_ref, dep_ref, ctx_ref, ent_ref, q_s, kn_s, vn_s):
    devices, steps, cols = recv_ref.shape
    cols -= 2 * k_ref.shape[1]
    slots, kv_cols = k_ref.shape
    kv_heads = kv_cols // HEAD_WIDTH
    per_device = cols // HEAD_WIDTH
    group = devices * per_device // kv_heads
    rows = group * steps
    score_scale = 1.0 / math.sqrt(HEAD_WIDTH)
    length = len_ref[0]
    kv = recv_ref[0, :, cols:]
    for d in range(1, devices):
        kv = kv + recv_ref[d, :, cols:]
    cosine = cos_ref[...]
    sine = sin_ref[...]
    kn_s[...] = jnp.zeros_like(kn_s)
    vn_s[...] = jnp.zeros_like(vn_s)
    fresh = kn_s.shape[0]
    col_old = lax.broadcasted_iota(jnp.int32, (rows, slots), 1)
    col_new = lax.broadcasted_iota(jnp.int32, (rows, fresh), 1)
    step_new = lax.rem(lax.broadcasted_iota(jnp.int32, (rows, fresh), 0), steps)
    for k in range(kv_heads):
        lanes = slice(k * HEAD_WIDTH, (k + 1) * HEAD_WIDTH)
        for i in range(group):
            h = k * group + i
            d, hh = h // per_device, h % per_device
            q_s[i * steps : (i + 1) * steps, :] = recv_ref[d, :, hh * HEAD_WIDTH : (hh + 1) * HEAD_WIDTH]
        query = q_s[...].astype(BF16).astype(F32)
        query = rope(query, cosine, sine).astype(BF16)
        key_now = rope(kv[:, lanes], cosine[:steps], sine[:steps]).astype(BF16).astype(F32)
        value_now = kv[:, kv_cols + k * HEAD_WIDTH : kv_cols + (k + 1) * HEAD_WIDTH].astype(BF16).astype(F32)
        ent_ref[:, lanes] = key_now
        ent_ref[:, kv_cols + k * HEAD_WIDTH : kv_cols + (k + 1) * HEAD_WIDTH] = value_now
        kn_s[:steps, :] = key_now
        vn_s[:steps, :] = value_now
        old = nt(query, k_ref[:, lanes]) * score_scale
        old = jnp.where(col_old < length, old, MASKED)
        new = nt(query, kn_s[...].astype(BF16)) * score_scale
        new = jnp.where((col_new < steps) & (col_new <= step_new), new, MASKED)
        top = jnp.maximum(jnp.max(old, axis=1, keepdims=True), jnp.max(new, axis=1, keepdims=True))
        e_old = jnp.exp(old - top)
        e_new = jnp.exp(new - top)
        total = jnp.sum(e_old, axis=1, keepdims=True) + jnp.sum(e_new, axis=1, keepdims=True)
        p_old = (e_old / total).astype(BF16)
        p_new = (e_new / total).astype(BF16)
        out = nn(p_old, v_ref[:, lanes]) + nn(p_new, vn_s[...].astype(BF16))
        ctx_ref[k * rows : (k + 1) * rows, :] = out.astype(BF16)


def lower_kernel(at_ref, low_ref, own_ref, a_ref, b_ref, c_ref, d_ref, x_ref, rank_ref, c_s, x_s):
    lines, per_row, head = a_ref.shape
    devices = 4 * lines
    rows, cols = x_ref.shape
    steps = rows // devices
    for r, (flip, cross) in zip((a_ref, b_ref, c_ref, d_ref), KINDS):
        for k in range(lines):
            start = pl.multiple_of(piece_at(at_ref, 2 * lines, k, flip, cross) * per_row, per_row)
            c_s[pl.ds(start, per_row), :] = r[k].astype(F32)
    for h in range(per_row // steps):
        for t in range(steps):
            piece = c_s[pl.ds(h * steps + t, devices, stride=per_row), :]
            x_s[t * devices : (t + 1) * devices, h * head : (h + 1) * head] = piece.astype(BF16)
    rank_ref[...] = (nt(low_ref[...], x_s[...]).astype(BF16).astype(F32) * own_ref[...]).astype(BF16)
    start = pl.multiple_of((2 * at_ref[0] + at_ref[1]) * cols, cols)
    x_ref[...] = x_s[:, pl.ds(start, cols)]


def fetch_kernel(at_ref, w_ref, dep_ref, there_ref, here_ref, sems):
    chips, _, width = there_ref.shape
    copies = []
    for half, (core, out_ref) in enumerate(((1 - at_ref[1], there_ref), (at_ref[1], here_ref))):
        for c in range(chips):
            start = pl.multiple_of((2 * c + core) * width, width)
            copy = pltpu.make_async_copy(
                w_ref.at[:, pl.ds(start, width)], out_ref.at[c], sems.at[half * chips + c]
            )
            copy.start()
            copies.append(copy)
    for copy in copies:
        copy.wait()


def out_kernel(cross, at_ref, x_ref, w_ref, rank_ref, up_ref, o_ref):
    width = o_ref.shape[2]
    core = 1 - at_ref[1] if cross else at_ref[1]
    x = x_ref[...]
    rank = rank_ref[...]
    for c in range(o_ref.shape[0]):
        lanes = pl.ds(pl.multiple_of((2 * c + core) * width, width), width)
        o_ref[c] = nn(x, w_ref[c]) + SCALE * tn(rank, up_ref[:, lanes])


def pair_kernel(at_ref, a_ref, b_ref, *outs):
    chips = len(outs)
    for k, out in enumerate(outs):
        dest = lax.rem(at_ref[0] + k, chips)
        out[...] = (a_ref[dest] + b_ref[dest]).astype(BF16)


def total_kernel(*refs):
    total = refs[0][...].astype(F32)
    for r in refs[1:-1]:
        total = total + r[...].astype(F32)
    refs[-1][...] = total.astype(BF16)


def body(
    tokens,
    query_weight,
    key_value_weight,
    output_weight,
    cached_rotated_keys,
    cached_values,
    lengths,
    request_adapter,
    adapter_pool_slot,
    adapter_down_maps,
    query_up_maps,
    key_up_maps,
    value_up_maps,
    result_lowering_factors,
    output_up_maps,
):
    both = ("tp", "sub")
    chips = lax.axis_size("tp")
    devices = lax.axis_size(both)
    lines = chips // 2
    me = lax.axis_index(both)
    steps, requests, width = tokens.shape
    rows = steps * requests
    padded = -(-rows // 128) * 128
    cols = query_weight.shape[1]
    rank = key_up_maps.shape[1]
    assert devices == 2 * chips and chips % 2 == 0
    assert adapter_down_maps.shape[0] == 1 and requests == devices and cached_values.shape[0] == 1
    at = jnp.stack([lax.axis_index("tp"), lax.axis_index("sub")]).astype(jnp.int32)

    def swap_core(v):
        return lax.ppermute(v, "sub", [(0, 1), (1, 0)])

    def swap_y(v):
        return lax.ppermute(v, "tp", [(i, i ^ 1) for i in range(chips)])

    def shift_chip(v, k):
        if k == 0:
            return v
        return lax.ppermute(v, "tp", [(i, (i + k) % chips) for i in range(chips)])

    def exchange(v):
        return lax.all_to_all(v, both, 0, 0, tiled=True)

    def gather(v):
        line = stack([shift_chip(v, 2 * k) for k in range(lines)])
        across = swap_y(line)
        return line, across, swap_core(line), swap_core(across)

    x = tokens.reshape(rows, width)
    down = adapter_down_maps[0]
    gathered = gather(x)

    index = jnp.arange(devices, dtype=jnp.int32)
    slot = jnp.sum(
        jnp.where(request_adapter[:, None] == index[None, :], adapter_pool_slot[None, :], 0), axis=1
    )
    row_slot = jnp.tile(slot, steps)[None, :]
    spread_mask = (jnp.repeat(index, rank)[:, None] == row_slot).astype(F32)
    own_mask = (row_slot == me).astype(F32)

    ups = exchange(
        pl.pallas_call(
            split_kernel,
            out_shape=jax.ShapeDtypeStruct((devices, rank, cols), BF16),
            compiler_params=PARAMS,
        )(query_up_maps[0])
    )
    rank_send, rank_rest = pl.pallas_call(
        rank_kernel,
        out_shape=(
            jax.ShapeDtypeStruct((devices, rank, padded), BF16),
            jax.ShapeDtypeStruct((2 * rank, rows), BF16),
        ),
        in_specs=[SMEM] + [VMEM] * 6 + [ANY],
        compiler_params=PARAMS,
    )(at, down, *gathered, own_mask, ups)
    ranks = exchange(rank_send)
    query = pl.pallas_call(
        query_kernel,
        out_shape=jax.ShapeDtypeStruct((rows, cols), F32),
        in_specs=[SMEM, ANY] + [VMEM] * 4 + [ANY],
        scratch_shapes=[
            pltpu.VMEM((devices, width, cols), BF16),
            pltpu.SemaphoreType.DMA((devices,)),
        ],
        compiler_params=WIDE,
    )(at, query_weight, *gathered, rank_send)
    kv_width = key_value_weight.shape[1]
    kv = pl.pallas_call(
        kv_kernel,
        out_shape=jax.ShapeDtypeStruct((rows, kv_width), F32),
        compiler_params=PARAMS,
    )(x, key_value_weight, rank_rest, key_up_maps[0], value_up_maps[0])
    to_rows = pl.pallas_call(
        finish_kernel,
        out_shape=jax.ShapeDtypeStruct((devices, steps, cols + kv_width), F32),
        compiler_params=PARAMS,
    )(query, kv, ranks, spread_mask, ups)
    arrived = exchange(to_rows)
    fetched = pl.pallas_call(
        fetch_kernel,
        out_shape=[jax.ShapeDtypeStruct((chips, cols, width), BF16)] * 2,
        in_specs=[SMEM, ANY, ANY],
        out_specs=[ANY, ANY],
        scratch_shapes=[pltpu.SemaphoreType.DMA((devices,))],
        compiler_params=pltpu.CompilerParams(vmem_limit_bytes=36 * 1024 * 1024),
    )(at, output_weight, to_rows)

    half_width = HEAD_WIDTH // 2
    frequency = ROPE_BASE ** (-2.0 * jnp.arange(half_width, dtype=F32) / HEAD_WIDTH)
    positions = lengths[0] + jnp.arange(steps, dtype=jnp.int32)
    angles = positions.astype(F32)[:, None] * frequency
    cosine, sine = jnp.cos(angles), jnp.sin(angles)
    group = 2 * devices * cols // kv_width
    heads = devices * cols // HEAD_WIDTH
    cosine = jnp.tile(jnp.concatenate([cosine, cosine], axis=1), (group, 1))
    sine = jnp.tile(jnp.concatenate([-sine, sine], axis=1), (group, 1))
    context, fresh = pl.pallas_call(
        attend_kernel,
        out_shape=(
            jax.ShapeDtypeStruct((heads * steps, HEAD_WIDTH), BF16),
            jax.ShapeDtypeStruct((steps, kv_width), F32),
        ),
        in_specs=[SMEM] + [VMEM] * 5 + [ANY],
        scratch_shapes=[
            pltpu.VMEM((group * steps, HEAD_WIDTH), F32),
            pltpu.VMEM((16, HEAD_WIDTH), F32),
            pltpu.VMEM((16, HEAD_WIDTH), F32),
        ],
        compiler_params=PARAMS,
    )(lengths, arrived, cosine, sine, cached_rotated_keys[0], cached_values[0], fetched[0])
    entries = fresh.astype(BF16)[:, None, :]

    lhs, out_rank = pl.pallas_call(
        lower_kernel,
        out_shape=(
            jax.ShapeDtypeStruct((rows, cols), BF16),
            jax.ShapeDtypeStruct((rank, rows), BF16),
        ),
        in_specs=[SMEM] + [VMEM] * 6,
        scratch_shapes=[
            pltpu.VMEM((devices * heads * steps, HEAD_WIDTH), F32),
            pltpu.VMEM((rows, heads * HEAD_WIDTH), BF16),
        ],
        compiler_params=PARAMS,
    )(at, result_lowering_factors[0], own_mask, *gather(context))

    def out_half(cross):
        return pl.pallas_call(
            functools.partial(out_kernel, cross),
            out_shape=jax.ShapeDtypeStruct((chips, rows, width), F32),
            in_specs=[SMEM] + [VMEM] * 4,
            compiler_params=PARAMS,
        )(at, lhs, fetched[0 if cross else 1], out_rank, output_up_maps[0])

    received = swap_core(out_half(True))
    chip_totals = pl.pallas_call(
        pair_kernel,
        out_shape=[jax.ShapeDtypeStruct((rows, width), BF16)] * chips,
        in_specs=[SMEM, VMEM, VMEM],
        compiler_params=PARAMS,
    )(at, out_half(False), received)
    final = [shift_chip(v, k) for k, v in enumerate(chip_totals)]
    attended = pl.pallas_call(
        total_kernel,
        out_shape=jax.ShapeDtypeStruct((rows, width), BF16),
        compiler_params=PARAMS,
    )(*final)
    return attended.reshape(steps, requests, width), entries


def solution(mesh):
    placed = (
        P(None, "groups", ("tp", "sub")),
        P(None, ("tp", "sub")),
        P(("tp", "sub"), None),
        P(("tp", "sub"), None),
        P(("groups", "tp", "sub"), None, None),
        P(("groups", "tp", "sub"), None, None),
        P(("groups", "tp", "sub")),
        P("groups"),
        P(),
        P(("tp", "sub"), None, None),
        P(("tp", "sub"), None, None),
        P(("tp", "sub"), None, None),
        P(("tp", "sub"), None, None),
        P(("tp", "sub"), None, None),
        P(("tp", "sub"), None, None),
    )
    return jax.shard_map(
        body,
        mesh=mesh,
        in_specs=placed,
        out_specs=(P(None, "groups", ("tp", "sub")), P(None, ("groups", "tp", "sub"), None)),
        check_vma=False,
    )
```

time: 136 us -> 113 us (0.83)
  waiting for transfers between devices: 37.7 us -> 28.1 us
  blocking collectives: 9.48 us -> 0 us
  Pallas kernels: 29.3 us -> 26.1 us
    all_to_all x5 -> x3, waiting for transfers between devices: 21.4 us -> 7.52 us  [exchange(): return lax.all_to_all(v, both, 0, 0, tiled=True)]
    all_to_all x1 -> x0, blocking collectives: 9.48 us -> none  [exchange(): return lax.all_to_all(v, both, 0, 0, tiled=True)]
    all_to_all x5 -> x3, starting transfers between devices: 21.2 us -> 13 us  [exchange(): return lax.all_to_all(v, both, 0, 0, tiled=True)]
    ppermute x10 -> x13, starting transfers between devices: 14.8 us -> 20.6 us  [shift_chip(): return lax.ppermute(v, 'tp', [(i, (i + k) % chips) for i in range(chips)])]
    ppermute x10 -> x13, waiting for transfers between devices: 11 us -> 14.6 us  [shift_chip(): return lax.ppermute(v, 'tp', [(i, (i + k) % chips) for i in range(chips)])]
    pallas_call x12 -> x10, Pallas kernels: 25.2 us -> 22.4 us  [the longest x1 6.79 us: body(): pl.pallas_call(query_kernel, out_shape=jax.ShapeDtypeStruct((rows, cols),...]
    ppermute x4 -> x5, waiting for transfers between devices: 0.01 us -> 2.35 us  [swap_core(): return lax.ppermute(v, 'sub', [(0, 1), (1, 0)])]
    ppermute x1 -> x2, waiting for transfers between devices: 5.31 us -> 3.56 us  [swap_y(): return lax.ppermute(v, 'tp', [(i, i ^ 1) for i in range(chips)])]
  transfers between devices with their start and end apart: 20 -> 23, of which waited for: 12 -> 15; matrix products, arithmetic and copies ran while one was open for 2% -> 2% of each run, Pallas kernels for 16% -> 15%
where the time goes in v4:
time: 113 us; the launch traced here: 112 us
  starting transfers between devices  37.3 us (33%)
  waiting for transfers between devices  28.1 us (25%)
  Pallas kernels  26.1 us (23%)
  local copies, waits for them, and re-layouts  17.3 us (15%)
  other arithmetic  1.83 us (2%)
  between operations  1.49 us (1%)
    ppermute x13, starting transfers between devices, shift_chip(): return lax.ppermute(v, 'tp', [(i, (i + k) % chips) for i in range(chips)])  20.6 us
    unnamed x32, local copies, waits for them, and re-layouts  17 us
    ppermute x13, waiting for transfers between devices, shift_chip(): return lax.ppermute(v, 'tp', [(i, (i + k) % chips) for i in range(chips)])  14.6 us
    all_to_all x3, starting transfers between devices, exchange(): return lax.all_to_all(v, both, 0, 0, tiled=True)  13 us
    all_to_all x3, waiting for transfers between devices, exchange(): return lax.all_to_all(v, both, 0, 0, tiled=True)  7.52 us
    pallas_call x1, Pallas kernels, body(): pl.pallas_call(query_kernel, out_shape=jax.ShapeDtypeStruct((rows, cols),...  6.79 us
    pallas_call x1, Pallas kernels, body(): pl.pallas_call(fetch_kernel, out_shape=[jax.ShapeDtypeStruct((chips, cols...  6.54 us
    pallas_call x2, Pallas kernels, out_half(): pl.pallas_call(functools.partial(out_kernel, cross), out_shape=jax.ShapeD...  4.55 us
  transfers between devices with their start and end apart: 23, of which 15 were waited for; matrix products, arithmetic and copies ran while one was open for 2% of the time, Pallas kernels for 15%

profile of v4, /device:TPU:0, one launch (start us, length us, event | category | flops | bytes accessed | tf_op | source)
XLA Modules:
  0.0 112.1 jit_solution(10411417838343445516)
XLA Ops:
  0.6 5.1 %collective-permute-start.2 = (bf16[32,1024]{1,0:T(8,128)(2,1)}, bf16[32,1024]{1,0:T(8,128)(2,1)S(1)}, u32[]{:S(2)}, u32[]{:S(2)}) collective-permute-start(bf16[32,1024]{1,0:T(8,128)(2,1)} %bitcast.25), channel_id=1, source_target_pairs={{0,12},{2,14},{4,0},{6,2},{8,4},{10,6},{12,8},{14,10},{1,13},{3,15... | collective-permute-start | bytes 196616 | tf_op jit(solution)/shard_map/ppermute | solution.py:279
  5.7 1.0 collective-permute-start
  6.7 1.8 %collective-permute-done.2.refs_3_ = bf16[32,1024]{1,0:T(8,128)(2,1)S(1)} collective-permute-done((bf16[32,1024]{1,0:T(8,128)(2,1)}, bf16[32,1024]{1,0:T(8,128)(2,1)S(1)}, u32[]{:S(2)}, u32[]{:S(2)}) %collective-permute-start.2) | collective-permute-done | bytes 65568 | tf_op jit(solution)/shard_map/ppermute | solution.py:279
  8.5 3.9 %collective-permute-done.1.refs_2_ = bf16[32,1024]{1,0:T(8,128)(2,1)S(1)} collective-permute-done((bf16[32,1024]{1,0:T(8,128)(2,1)}, bf16[32,1024]{1,0:T(8,128)(2,1)S(1)}, u32[]{:S(2)}, u32[]{:S(2)}) %collective-permute-start.1) | collective-permute-done | bytes 65568 | tf_op jit(solution)/shard_map/ppermute | solution.py:279
  12.4 0.8 copy-done.12
  13.3 1.6 %collective-permute-start.3 = (bf16[4,32,1024]{2,1,0:T(8,128)(2,1)S(1)}, bf16[4,32,1024]{2,1,0:T(8,128)(2,1)S(1)}, u32[]{:S(2)}, u32[]{:S(2)}) collective-permute-start(bf16[4,32,1024]{2,1,0:T(8,128)(2,1)S(1)} %shard_map.158.a_ref), channel_id=1, source_target_pairs={{0,2},{2,0},{4,6},{6,4},{8,10},{10,8},{12,14},{14,12},{1,3},{3,1},... | collective-permute-start | bytes 786440 | tf_op jit(solution)/shard_map/ppermute | solution.py:274
  14.9 0.9 copy-done.10
  15.8 0.7 shard_map.159
  16.5 3.5 %all-to-all-start = ((bf16[16,16,512]{2,1,0:T(8,128)(2,1)}), bf16[16,16,512]{2,1,0:T(8,128)(2,1)S(1)}, u32[]{:S(2)}, u32[]{:S(2)}) async-start(bf16[16,16,512]{2,1,0:T(8,128)(2,1)} %shard_map.159), calls=%async_computation | async-start | bytes 524288 | tf_op jit(solution)/shard_map/all_to_all | solution.py:282
  20.1 0.9 select_reduce_fusion
  21.0 0.1 eq.53
  21.0 0.3 collective-permute-start.4
  21.3 0.1 collective-permute-done.3.b_ref
  21.4 0.2 collective-permute-start.5
  21.6 0.1 convert_element_type.19.own_ref
  21.7 0.1 eq.51
  21.7 0.1 pad_add_fusion.at_ref
  21.8 0.8 collective-permute-done.4.c_ref
  22.6 7.5 %all-to-all-done.dep_ref.up_ref = bf16[16,16,512]{2,1,0:T(8,128)(2,1)S(1)} async-done(((bf16[16,16,512]{2,1,0:T(8,128)(2,1)}), bf16[16,16,512]{2,1,0:T(8,128)(2,1)S(1)}, u32[]{:S(2)}, u32[]{:S(2)}) %all-to-all-start) | async-done | bytes 262176 | tf_op jit(solution)/shard_map/all_to_all | solution.py:282
  30.1 1.4 %copy-done.7 = bf16[1,48,16384]{2,1,0:T(8,128)(2,1)S(1)} copy-done((bf16[1,48,16384]{2,1,0:T(8,128)(2,1)S(1)}, bf16[1,48,16384]{2,1,0:T(8,128)(2,1)}, u32[]{:S(2)}) %copy-start.7) | copy-done | bytes 1572888
  31.5 1.7 %shard_map.160 = (bf16[16,16,128]{2,1,0:T(8,128)(2,1)}, bf16[32,32]{1,0:T(8,128)(2,1)S(1)}) custom-call(s32[2]{0:T(128)S(1)} %pad_add_fusion.at_ref, bf16[48,16384]{1,0:T(8,128)(2,1)S(1)} %bitcast.20, bf16[4,32,1024]{2,1,0:T(8,128)(2,1)S(1)} %shard_map.158.a_ref, bf16[4,32,1024]{2,1,0:T(8,128)(2,1)S(1)} %collective-permute-done.3.b_ref, ...), custom_call_target="tpu_custom_call" | custom-call | tf_op jit(solution)/shard_map/pallas_call | solution.py:308
  33.2 3.5 %all-to-all-start.1 = ((bf16[16,16,128]{2,1,0:T(8,128)(2,1)}), bf16[16,16,128]{2,1,0:T(8,128)(2,1)S(1)}, u32[]{:S(2)}, u32[]{:S(2)}) async-start(bf16[16,16,128]{2,1,0:T(8,128)(2,1)} %get-tuple-element.18.dep_ref), calls=%async_computation.1 | async-start | bytes 131072 | tf_op jit(solution)/shard_map/all_to_all | solution.py:282
  36.7 0.1 compare_convert_fusion.mask_ref
  37.5 1.6 %copy-done.6 = bf16[1024,1024]{1,0:T(8,128)(2,1)S(1)} copy-done((bf16[1024,1024]{1,0:T(8,128)(2,1)S(1)}, bf16[1024,1024]{1,0:T(8,128)(2,1)}, u32[]{:S(2)}) %copy-start.6) | copy-done | bytes 2097176
  39.1 0.8 copy-done.13
  40.0 0.7 copy-done.14
  40.7 0.7 copy-done.15
  41.4 0.5 shard_map.162.kv_ref
  41.9 6.8 %shard_map.161.q_ref = f32[32,512]{1,0:T(8,128)S(1)} custom-call(s32[2]{0:T(128)S(1)} %pad_add_fusion.at_ref, bf16[16384,512]{1,0:T(8,128)(2,1)} %w_ref.3, bf16[4,32,1024]{2,1,0:T(8,128)(2,1)S(1)} %shard_map.158.a_ref, bf16[4,32,1024]{2,1,0:T(8,128)(2,1)S(1)} %collective-permute-done.3.b_ref, bf16[4,32,1024]{2,1,0:T(8,128)(2,1)S(1)} %collective-permute-done.4.c_ref, ...), custom_call_target="tpu_custom_call" | custom-call | tf_op jit(solution)/shard_map/pallas_call | solution.py:318
  48.7 0.9 shard_map.163.dep_ref
  49.6 6.0 %all-to-all-start.2 = ((f32[16,2,1536]{2,1,0:T(2,128)}), f32[16,2,1536]{2,1,0:T(2,128)S(1)}, u32[]{:S(2)}, u32[]{:S(2)}) async-start(f32[16,2,1536]{2,1,0:T(2,128)} %shard_map.163.dep_ref), calls=%async_computation.2 | async-start | bytes 393216 | tf_op jit(solution)/shard_map/all_to_all | solution.py:282
  55.6 0.1 fusion
  55.7 0.1 pad_maximum_fusion
  55.8 6.5 %shard_map.164 = (bf16[8,512,1024]{2,1,0:T(8,128)(2,1)S(1)}, bf16[8,512,1024]{2,1,0:T(8,128)(2,1)S(1)}) custom-call(s32[2]{0:T(128)S(1)} %pad_add_fusion.at_ref, bf16[512,16384]{1,0:T(8,128)(2,1)} %w_ref.5, f32[16,2,1536]{2,1,0:T(2,128)} %shard_map.163.dep_ref), custom_call_target="tpu_custom_call" | custom-call | tf_op jit(solution)/shard_map/pallas_call | solution.py:340
  62.3 3.3 %copy-done = bf16[8,512,1024]{2,1,0:T(8,128)(2,1)} copy-done((bf16[8,512,1024]{2,1,0:T(8,128)(2,1)}, bf16[8,512,1024]{2,1,0:T(8,128)(2,1)S(1)}, u32[]{:S(2)}) %copy-start) | copy-done | bytes 8388632
  65.6 3.2 %copy-done.3 = bf16[8,512,1024]{2,1,0:T(8,128)(2,1)} copy-done((bf16[8,512,1024]{2,1,0:T(8,128)(2,1)}, bf16[8,512,1024]{2,1,0:T(8,128)(2,1)S(1)}, u32[]{:S(2)}) %copy-start.3) | copy-done | bytes 8388632
  68.9 3.4 %copy-done.1 = bf16[8,512,1024]{2,1,0:T(8,128)(2,1)S(1)} copy-done((bf16[8,512,1024]{2,1,0:T(8,128)(2,1)S(1)}, bf16[8,512,1024]{2,1,0:T(8,128)(2,1)}, u32[]{:S(2)}) %copy-start.1) | copy-done | bytes 8388632
  72.3 1.6 %shard_map.165 = (bf16[128,128]{1,0:T(8,128)(2,1)S(1)}, f32[2,1024]{1,0:T(2,128)S(1)}) custom-call(s32[1]{0:T(128)} %copy.18.len_ref, f32[16,2,1536]{2,1,0:T(2,128)S(1)} %all-to-all-done.2.recv_ref, f32[32,128]{1,0:T(8,128)S(1)} %bitcast.30, f32[32,128]{1,0:T(8,128)S(1)} %bitcast.31, bf16[512,512]{1,0:T(8,128)(2,1)S(1)} %bitcast.21, ...), custom_call_target="tpu_custom_call" | custom-call | tf_op jit(solution)/shard_map/pallas_call | solution.py:358
  73.9 3.8 %collective-permute-start.8 = (bf16[128,128]{1,0:T(8,128)(2,1)S(1)}, bf16[128,128]{1,0:T(8,128)(2,1)S(1)}, u32[]{:S(2)}, u32[]{:S(2)}) collective-permute-start(bf16[128,128]{1,0:T(8,128)(2,1)S(1)} %get-tuple-element.21.refs_0_), channel_id=1, source_target_pairs={{0,12},{2,14},{4,0},{6,2},{8,4},{10,6},{12,8},{14,10},{1,13},{3,15... | collective-permute-start | bytes 98312 | tf_op jit(solution)/shard_map/ppermute | solution.py:279
  77.7 1.1 %collective-permute-start.6 = (bf16[128,128]{1,0:T(8,128)(2,1)S(1)}, bf16[128,128]{1,0:T(8,128)(2,1)S(1)}, u32[]{:S(2)}, u32[]{:S(2)}) collective-permute-start(bf16[128,128]{1,0:T(8,128)(2,1)S(1)} %get-tuple-element.21.refs_0_), channel_id=1, source_target_pairs={{0,4},{2,6},{4,8},{6,10},{8,12},{10,14},{12,0},{14,2},{1,5},{3,7},... | collective-permute-start | bytes 98312 | tf_op jit(solution)/shard_map/ppermute | solution.py:279
  78.8 0.5 collective-permute-done.8.refs_3_
  79.3 3.3 %collective-permute-done.7.refs_2_ = bf16[128,128]{1,0:T(8,128)(2,1)S(1)} collective-permute-done((bf16[128,128]{1,0:T(8,128)(2,1)S(1)}, bf16[128,128]{1,0:T(8,128)(2,1)S(1)}, u32[]{:S(2)}, u32[]{:S(2)}) %collective-permute-start.7) | collective-permute-done | bytes 32800 | tf_op jit(solution)/shard_map/ppermute | solution.py:279
  82.6 0.7 collective-permute-done.6.refs_1_
  83.4 1.5 %collective-permute-start.9 = (bf16[4,128,128]{2,1,0:T(8,128)(2,1)S(1)}, bf16[4,128,128]{2,1,0:T(8,128)(2,1)S(1)}, u32[]{:S(2)}, u32[]{:S(2)}) collective-permute-start(bf16[4,128,128]{2,1,0:T(8,128)(2,1)S(1)} %shard_map.166.a_ref), channel_id=1, source_target_pairs={{0,2},{2,0},{4,6},{6,4},{8,10},{10,8},{12,14},{14,12},{1,3},{3,1},... | collective-permute-start | bytes 393224 | tf_op jit(solution)/shard_map/ppermute | solution.py:274
  84.9 3.5 %collective-permute-done.9.b_ref = bf16[4,128,128]{2,1,0:T(8,128)(2,1)S(1)} collective-permute-done((bf16[4,128,128]{2,1,0:T(8,128)(2,1)S(1)}, bf16[4,128,128]{2,1,0:T(8,128)(2,1)S(1)}, u32[]{:S(2)}, u32[]{:S(2)}) %collective-permute-start.9) | collective-permute-done | bytes 131104 | tf_op jit(solution)/shard_map/ppermute | solution.py:274
  88.4 1.3 %collective-permute-done.11.d_ref = bf16[4,128,128]{2,1,0:T(8,128)(2,1)S(1)} collective-permute-done((bf16[4,128,128]{2,1,0:T(8,128)(2,1)S(1)}, bf16[4,128,128]{2,1,0:T(8,128)(2,1)S(1)}, u32[]{:S(2)}, u32[]{:S(2)}) %collective-permute-start.11) | collective-permute-done | bytes 131104 | tf_op jit(solution)/shard_map/ppermute | solution.py:271
  89.8 1.5 %shard_map.167 = (bf16[32,512]{1,0:T(8,128)(2,1)S(1)}, bf16[16,32]{1,0:T(8,128)(2,1)S(1)}) custom-call(s32[2]{0:T(128)S(1)} %pad_add_fusion.at_ref, bf16[16,8192]{1,0:T(8,128)(2,1)S(1)} %bitcast.24, f32[1,32]{1,0:T(1,128)S(1)} %convert_element_type.19.own_ref, bf16[4,128,128]{2,1,0:T(8,128)(2,1)S(1)} %shard_map.166.a_ref, ...), custom_call_target="tpu_custom_call" | custom-call | tf_op jit(solution)/shard_map/pallas_call | solution.py:374
  91.2 2.3 %shard_map.169 = f32[8,32,1024]{2,1,0:T(8,128)S(1)} custom-call(s32[2]{0:T(128)S(1)} %pad_add_fusion.at_ref, bf16[32,512]{1,0:T(8,128)(2,1)S(1)} %get-tuple-element.22.x_ref, bf16[8,512,1024]{2,1,0:T(8,128)(2,1)S(1)} %copy-done.2, bf16[16,32]{1,0:T(8,128)(2,1)S(1)} %get-tuple-element.24.rank_ref, bf16[16,16384]{1,0:T(8,128)(2,1)S(1)} %bitcast.18), custom_call_target="tpu_custom_call" | custom-call | tf_op jit(solution)/shard_map/pallas_call | solution.py:389
  93.5 0.2 collective-permute-start.12
  93.7 2.3 %shard_map.168.a_ref = f32[8,32,1024]{2,1,0:T(8,128)S(1)} custom-call(s32[2]{0:T(128)S(1)} %pad_add_fusion.at_ref, bf16[32,512]{1,0:T(8,128)(2,1)S(1)} %get-tuple-element.22.x_ref, bf16[8,512,1024]{2,1,0:T(8,128)(2,1)S(1)} %copy-done.4, bf16[16,32]{1,0:T(8,128)(2,1)S(1)} %get-tuple-element.24.rank_ref, bf16[16,16384]{1,0:T(8,128)(2,1)S(1)} %bitcast.19), custom_call_target="tpu_custom_call" | custom-call | tf_op jit(solution)/shard_map/pallas_call | solution.py:389
  96.0 0.2 collective-permute-done.12.b_ref
  96.2 0.6 shard_map.170
  96.8 1.5 %collective-permute-start.13 = (bf16[32,1024]{1,0:T(8,128)(2,1)S(1)}, bf16[32,1024]{1,0:T(8,128)(2,1)S(1)}, u32[]{:S(2)}, u32[]{:S(2)}) collective-permute-start(bf16[32,1024]{1,0:T(8,128)(2,1)S(1)} %get-tuple-element.26), channel_id=1, source_target_pairs={{0,2},{2,4},{4,6},{6,8},{8,10},{10,12},{12,14},{14,0},{1,3},{3,5},... | collective-permute-start | bytes 196616 | tf_op jit(solution)/shard_map/ppermute | solution.py:279
  98.4 1.2 %collective-permute-start.15 = (bf16[32,1024]{1,0:T(8,128)(2,1)S(1)}, bf16[32,1024]{1,0:T(8,128)(2,1)S(1)}, u32[]{:S(2)}, u32[]{:S(2)}) collective-permute-start(bf16[32,1024]{1,0:T(8,128)(2,1)S(1)} %get-tuple-element.28), channel_id=1, source_target_pairs={{0,6},{2,8},{4,10},{6,12},{8,14},{10,0},{12,2},{14,4},{1,7},{3,9},... | collective-permute-start | bytes 196616 | tf_op jit(solution)/shard_map/ppermute | solution.py:279
  99.5 2.7 %collective-permute-start.16 = (bf16[32,1024]{1,0:T(8,128)(2,1)S(1)}, bf16[32,1024]{1,0:T(8,128)(2,1)S(1)}, u32[]{:S(2)}, u32[]{:S(2)}) collective-permute-start(bf16[32,1024]{1,0:T(8,128)(2,1)S(1)} %get-tuple-element.29), channel_id=1, source_target_pairs={{0,8},{2,10},{4,12},{6,14},{8,0},{10,2},{12,4},{14,6},{1,9},{3,11}... | collective-permute-start | bytes 196616 | tf_op jit(solution)/shard_map/ppermute | solution.py:279
  102.2 1.1 collective-permute-start.17
  103.3 1.3 %collective-permute-done.13.refs_1_ = bf16[32,1024]{1,0:T(8,128)(2,1)S(1)} collective-permute-done((bf16[32,1024]{1,0:T(8,128)(2,1)S(1)}, bf16[32,1024]{1,0:T(8,128)(2,1)S(1)}, u32[]{:S(2)}, u32[]{:S(2)}) %collective-permute-start.13) | collective-permute-done | bytes 65568 | tf_op jit(solution)/shard_map/ppermute | solution.py:279
  104.6 1.6 %collective-permute-start.18 = (bf16[32,1024]{1,0:T(8,128)(2,1)S(1)}, bf16[32,1024]{1,0:T(8,128)(2,1)S(1)}, u32[]{:S(2)}, u32[]{:S(2)}) collective-permute-start(bf16[32,1024]{1,0:T(8,128)(2,1)S(1)} %get-tuple-element.31), channel_id=1, source_target_pairs={{0,12},{2,14},{4,0},{6,2},{8,4},{10,6},{12,8},{14,10},{1,13},{3,15... | collective-permute-start | bytes 196616 | tf_op jit(solution)/shard_map/ppermute | solution.py:279
  106.2 1.5 %collective-permute-start.19 = (bf16[32,1024]{1,0:T(8,128)(2,1)S(1)}, bf16[32,1024]{1,0:T(8,128)(2,1)S(1)}, u32[]{:S(2)}, u32[]{:S(2)}) collective-permute-start(bf16[32,1024]{1,0:T(8,128)(2,1)S(1)} %get-tuple-element.32), channel_id=1, source_target_pairs={{0,14},{2,0},{4,2},{6,4},{8,6},{10,8},{12,10},{14,12},{1,15},{3,1}... | collective-permute-start | bytes 196616 | tf_op jit(solution)/shard_map/ppermute | solution.py:279
  107.7 0.6 convert_bitcast_fusion
  108.3 1.2 %collective-permute-done.15.refs_3_ = bf16[32,1024]{1,0:T(8,128)(2,1)S(1)} collective-permute-done((bf16[32,1024]{1,0:T(8,128)(2,1)S(1)}, bf16[32,1024]{1,0:T(8,128)(2,1)S(1)}, u32[]{:S(2)}, u32[]{:S(2)}) %collective-permute-start.15) | collective-permute-done | bytes 65568 | tf_op jit(solution)/shard_map/ppermute | solution.py:279
  109.5 0.4 collective-permute-done.16.refs_4_
  109.9 1.5 %collective-permute-done.18.refs_6_ = bf16[32,1024]{1,0:T(8,128)(2,1)S(1)} collective-permute-done((bf16[32,1024]{1,0:T(8,128)(2,1)S(1)}, bf16[32,1024]{1,0:T(8,128)(2,1)S(1)}, u32[]{:S(2)}, u32[]{:S(2)}) %collective-permute-start.18) | collective-permute-done | bytes 65568 | tf_op jit(solution)/shard_map/ppermute | solution.py:279
  111.4 0.7 shard_map.171
  (45 shorter events, 0.2 us)
Async XLA Ops:
  0.6 7.9 %collective-permute-start.2 = (bf16[32,1024]{1,0:T(8,128)(2,1)}, bf16[32,1024]{1,0:T(8,128)(2,1)S(1)}, u32[]{:S(2)}, u32[]{:S(2)}) collective-permute-start(bf16[32,1024]{1,0:T(8,128)(2,1)} %bitcast.25), channel_id=1, source_target_pairs={{0,12},{2,14},{4,0},{6,2},{8,4},{10,6},{12,8},{14,10},{1,13},{3,15... | collective-permute-start | bytes 196616 | tf_op jit(solution)/shard_map/ppermute | solution.py:279
  5.7 6.7 %collective-permute-start.1 = (bf16[32,1024]{1,0:T(8,128)(2,1)}, bf16[32,1024]{1,0:T(8,128)(2,1)S(1)}, u32[]{:S(2)}, u32[]{:S(2)}) collective-permute-start(bf16[32,1024]{1,0:T(8,128)(2,1)} %bitcast.26), channel_id=1, source_target_pairs={{0,8},{2,10},{4,12},{6,14},{8,0},{10,2},{12,4},{14,6},{1,9},{3,11}... | collective-permute-start | bytes 196616 | tf_op jit(solution)/shard_map/ppermute | solution.py:279
  5.7 6.7 %collective-permute-start = (bf16[32,1024]{1,0:T(8,128)(2,1)}, bf16[32,1024]{1,0:T(8,128)(2,1)S(1)}, u32[]{:S(2)}, u32[]{:S(2)}) collective-permute-start(bf16[32,1024]{1,0:T(8,128)(2,1)} %bitcast.27), channel_id=1, source_target_pairs={{0,4},{2,6},{4,8},{6,10},{8,12},{10,14},{12,0},{14,2},{1,5},{3,7},... | collective-permute-start | bytes 196616 | tf_op jit(solution)/shard_map/ppermute | solution.py:279
  12.4 0.8 copy-start.12
  13.3 8.1 %collective-permute-start.3 = (bf16[4,32,1024]{2,1,0:T(8,128)(2,1)S(1)}, bf16[4,32,1024]{2,1,0:T(8,128)(2,1)S(1)}, u32[]{:S(2)}, u32[]{:S(2)}) collective-permute-start(bf16[4,32,1024]{2,1,0:T(8,128)(2,1)S(1)} %shard_map.158.a_ref), channel_id=1, source_target_pairs={{0,2},{2,0},{4,6},{6,4},{8,10},{10,8},{12,14},{14,12},{1,3},{3,1},... | collective-permute-start | bytes 786440 | tf_op jit(solution)/shard_map/ppermute | solution.py:274
  14.9 0.9 copy-start.10
  16.5 13.5 %all-to-all-start = ((bf16[16,16,512]{2,1,0:T(8,128)(2,1)}), bf16[16,16,512]{2,1,0:T(8,128)(2,1)S(1)}, u32[]{:S(2)}, u32[]{:S(2)}) async-start(bf16[16,16,512]{2,1,0:T(8,128)(2,1)} %shard_map.159), calls=%async_computation | async-start | bytes 524288 | tf_op jit(solution)/shard_map/all_to_all | solution.py:282
  21.0 1.5 %collective-permute-start.4 = (bf16[4,32,1024]{2,1,0:T(8,128)(2,1)S(1)}, bf16[4,32,1024]{2,1,0:T(8,128)(2,1)S(1)}, u32[]{:S(2)}, u32[]{:S(2)}) collective-permute-start(bf16[4,32,1024]{2,1,0:T(8,128)(2,1)S(1)} %shard_map.158.a_ref), channel_id=1, source_target_pairs={{0,1},{1,0},{2,3},{3,2},{4,5},{5,4},{6,7},{7,6},{8,9},{9,8},{10,11... | collective-permute-start | bytes 786440 | tf_op jit(solution)/shard_map/ppermute | solution.py:271
  21.4 8.7 %collective-permute-start.5 = (bf16[4,32,1024]{2,1,0:T(8,128)(2,1)S(1)}, bf16[4,32,1024]{2,1,0:T(8,128)(2,1)S(1)}, u32[]{:S(2)}, u32[]{:S(2)}) collective-permute-start(bf16[4,32,1024]{2,1,0:T(8,128)(2,1)S(1)} %collective-permute-done.3.b_ref), channel_id=1, source_target_pairs={{0,1},{1,0},{2,3},{3,2},{4,5},{5,4},{6,7},{7,6},{8,9},{9,8},{10,11... | collective-permute-start | bytes 786440 | tf_op jit(solution)/shard_map/ppermute | solution.py:271
  30.1 1.4 %copy-start.7 = (bf16[1,48,16384]{2,1,0:T(8,128)(2,1)S(1)}, bf16[1,48,16384]{2,1,0:T(8,128)(2,1)}, u32[]{:S(2)}) copy-start(bf16[1,48,16384]{2,1,0:T(8,128)(2,1)} %param.24) | copy-start | bytes 4718596
  33.2 15.4 %all-to-all-start.1 = ((bf16[16,16,128]{2,1,0:T(8,128)(2,1)}), bf16[16,16,128]{2,1,0:T(8,128)(2,1)S(1)}, u32[]{:S(2)}, u32[]{:S(2)}) async-start(bf16[16,16,128]{2,1,0:T(8,128)(2,1)} %get-tuple-element.18.dep_ref), calls=%async_computation.1 | async-start | bytes 131072 | tf_op jit(solution)/shard_map/all_to_all | solution.py:282
  37.5 1.6 %copy-start.6 = (bf16[1024,1024]{1,0:T(8,128)(2,1)S(1)}, bf16[1024,1024]{1,0:T(8,128)(2,1)}, u32[]{:S(2)}) copy-start(bf16[1024,1024]{1,0:T(8,128)(2,1)} %w_ref.4) | copy-start | bytes 6291460
  39.1 0.8 copy-start.13
  40.0 0.7 copy-start.14
  40.7 0.7 copy-start.15
  49.6 19.3 %all-to-all-start.2 = ((f32[16,2,1536]{2,1,0:T(2,128)}), f32[16,2,1536]{2,1,0:T(2,128)S(1)}, u32[]{:S(2)}, u32[]{:S(2)}) async-start(f32[16,2,1536]{2,1,0:T(2,128)} %shard_map.163.dep_ref), calls=%async_computation.2 | async-start | bytes 393216 | tf_op jit(solution)/shard_map/all_to_all | solution.py:282
  55.8 13.1 %copy-start.8 = (bf16[1,512,512]{2,1,0:T(8,128)(2,1)S(1)}, bf16[1,512,512]{2,1,0:T(8,128)(2,1)}, u32[]{:S(2)}) copy-start(bf16[1,512,512]{2,1,0:T(8,128)(2,1)} %param.19) | copy-start | bytes 1572868
  55.8 13.1 %copy-start.9 = (bf16[1,512,512]{2,1,0:T(8,128)(2,1)S(1)}, bf16[1,512,512]{2,1,0:T(8,128)(2,1)}, u32[]{:S(2)}) copy-start(bf16[1,512,512]{2,1,0:T(8,128)(2,1)} %param.20) | copy-start | bytes 1572868
  55.8 34.0 %copy-start.11 = (bf16[1,16,8192]{2,1,0:T(8,128)(2,1)S(1)}, bf16[1,16,8192]{2,1,0:T(8,128)(2,1)}, u32[]{:S(2)}) copy-start(bf16[1,16,8192]{2,1,0:T(8,128)(2,1)} %param.28) | copy-start | bytes 786436
  55.8 35.5 %copy-start.5 = (bf16[1,16,16384]{2,1,0:T(8,128)(2,1)S(1)}, bf16[1,16,16384]{2,1,0:T(8,128)(2,1)}, u32[]{:S(2)}) copy-start(bf16[1,16,16384]{2,1,0:T(8,128)(2,1)} %param.29) | copy-start | bytes 1572868
  62.3 3.3 %copy-start = (bf16[8,512,1024]{2,1,0:T(8,128)(2,1)}, bf16[8,512,1024]{2,1,0:T(8,128)(2,1)S(1)}, u32[]{:S(2)}) copy-start(bf16[8,512,1024]{2,1,0:T(8,128)(2,1)S(1)} %get-tuple-element.20.dep_ref.w_ref) | copy-start | bytes 25165828
  65.6 3.2 %copy-start.3 = (bf16[8,512,1024]{2,1,0:T(8,128)(2,1)}, bf16[8,512,1024]{2,1,0:T(8,128)(2,1)S(1)}, u32[]{:S(2)}) copy-start(bf16[8,512,1024]{2,1,0:T(8,128)(2,1)S(1)} %get-tuple-element.23.w_ref) | copy-start | bytes 25165828
  68.9 3.4 %copy-start.1 = (bf16[8,512,1024]{2,1,0:T(8,128)(2,1)S(1)}, bf16[8,512,1024]{2,1,0:T(8,128)(2,1)}, u32[]{:S(2)}) copy-start(bf16[8,512,1024]{2,1,0:T(8,128)(2,1)} %copy-done) | copy-start | bytes 25165828
  72.3 19.0 %copy-start.2 = (bf16[8,512,1024]{2,1,0:T(8,128)(2,1)S(1)}, bf16[8,512,1024]{2,1,0:T(8,128)(2,1)}, u32[]{:S(2)}) copy-start(bf16[8,512,1024]{2,1,0:T(8,128)(2,1)} %copy-done) | copy-start | bytes 25165828
  72.3 21.4 %copy-start.4 = (bf16[8,512,1024]{2,1,0:T(8,128)(2,1)S(1)}, bf16[8,512,1024]{2,1,0:T(8,128)(2,1)}, u32[]{:S(2)}) copy-start(bf16[8,512,1024]{2,1,0:T(8,128)(2,1)} %copy-done.3) | copy-start | bytes 25165828
  73.9 5.4 %collective-permute-start.8 = (bf16[128,128]{1,0:T(8,128)(2,1)S(1)}, bf16[128,128]{1,0:T(8,128)(2,1)S(1)}, u32[]{:S(2)}, u32[]{:S(2)}) collective-permute-start(bf16[128,128]{1,0:T(8,128)(2,1)S(1)} %get-tuple-element.21.refs_0_), channel_id=1, source_target_pairs={{0,12},{2,14},{4,0},{6,2},{8,4},{10,6},{12,8},{14,10},{1,13},{3,15... | collective-permute-start | bytes 98312 | tf_op jit(solution)/shard_map/ppermute | solution.py:279
  77.7 5.0 %collective-permute-start.7 = (bf16[128,128]{1,0:T(8,128)(2,1)S(1)}, bf16[128,128]{1,0:T(8,128)(2,1)S(1)}, u32[]{:S(2)}, u32[]{:S(2)}) collective-permute-start(bf16[128,128]{1,0:T(8,128)(2,1)S(1)} %get-tuple-element.21.refs_0_), channel_id=1, source_target_pairs={{0,8},{2,10},{4,12},{6,14},{8,0},{10,2},{12,4},{14,6},{1,9},{3,11}... | collective-permute-start | bytes 98312 | tf_op jit(solution)/shard_map/ppermute | solution.py:279
  77.7 5.7 %collective-permute-start.6 = (bf16[128,128]{1,0:T(8,128)(2,1)S(1)}, bf16[128,128]{1,0:T(8,128)(2,1)S(1)}, u32[]{:S(2)}, u32[]{:S(2)}) collective-permute-start(bf16[128,128]{1,0:T(8,128)(2,1)S(1)} %get-tuple-element.21.refs_0_), channel_id=1, source_target_pairs={{0,4},{2,6},{4,8},{6,10},{8,12},{10,14},{12,0},{14,2},{1,5},{3,7},... | collective-permute-start | bytes 98312 | tf_op jit(solution)/shard_map/ppermute | solution.py:279
  83.4 5.0 %collective-permute-start.9 = (bf16[4,128,128]{2,1,0:T(8,128)(2,1)S(1)}, bf16[4,128,128]{2,1,0:T(8,128)(2,1)S(1)}, u32[]{:S(2)}, u32[]{:S(2)}) collective-permute-start(bf16[4,128,128]{2,1,0:T(8,128)(2,1)S(1)} %shard_map.166.a_ref), channel_id=1, source_target_pairs={{0,2},{2,0},{4,6},{6,4},{8,10},{10,8},{12,14},{14,12},{1,3},{3,1},... | collective-permute-start | bytes 393224 | tf_op jit(solution)/shard_map/ppermute | solution.py:274
  84.9 3.5 %collective-permute-start.10 = (bf16[4,128,128]{2,1,0:T(8,128)(2,1)S(1)}, bf16[4,128,128]{2,1,0:T(8,128)(2,1)S(1)}, u32[]{:S(2)}, u32[]{:S(2)}) collective-permute-start(bf16[4,128,128]{2,1,0:T(8,128)(2,1)S(1)} %shard_map.166.a_ref), channel_id=1, source_target_pairs={{0,1},{1,0},{2,3},{3,2},{4,5},{5,4},{6,7},{7,6},{8,9},{9,8},{10,11... | collective-permute-start | bytes 393224 | tf_op jit(solution)/shard_map/ppermute | solution.py:271
  88.4 1.3 %collective-permute-start.11 = (bf16[4,128,128]{2,1,0:T(8,128)(2,1)S(1)}, bf16[4,128,128]{2,1,0:T(8,128)(2,1)S(1)}, u32[]{:S(2)}, u32[]{:S(2)}) collective-permute-start(bf16[4,128,128]{2,1,0:T(8,128)(2,1)S(1)} %collective-permute-done.9.b_ref), channel_id=1, source_target_pairs={{0,1},{1,0},{2,3},{3,2},{4,5},{5,4},{6,7},{7,6},{8,9},{9,8},{10,11... | collective-permute-start | bytes 393224 | tf_op jit(solution)/shard_map/ppermute | solution.py:271
  93.5 2.7 %collective-permute-start.12 = (f32[8,32,1024]{2,1,0:T(8,128)S(1)}, f32[8,32,1024]{2,1,0:T(8,128)S(1)}, u32[]{:S(2)}, u32[]{:S(2)}) collective-permute-start(f32[8,32,1024]{2,1,0:T(8,128)S(1)} %shard_map.169), channel_id=1, source_target_pairs={{0,1},{1,0},{2,3},{3,2},{4,5},{5,4},{6,7},{7,6},{8,9},{9,8},{10,11... | collective-permute-start | bytes 3145736 | tf_op jit(solution)/shard_map/ppermute | solution.py:271
  96.8 7.8 %collective-permute-start.13 = (bf16[32,1024]{1,0:T(8,128)(2,1)S(1)}, bf16[32,1024]{1,0:T(8,128)(2,1)S(1)}, u32[]{:S(2)}, u32[]{:S(2)}) collective-permute-start(bf16[32,1024]{1,0:T(8,128)(2,1)S(1)} %get-tuple-element.26), channel_id=1, source_target_pairs={{0,2},{2,4},{4,6},{6,8},{8,10},{10,12},{12,14},{14,0},{1,3},{3,5},... | collective-permute-start | bytes 196616 | tf_op jit(solution)/shard_map/ppermute | solution.py:279
  98.4 7.9 %collective-permute-start.14 = (bf16[32,1024]{1,0:T(8,128)(2,1)S(1)}, bf16[32,1024]{1,0:T(8,128)(2,1)S(1)}, u32[]{:S(2)}, u32[]{:S(2)}) collective-permute-start(bf16[32,1024]{1,0:T(8,128)(2,1)S(1)} %get-tuple-element.27), channel_id=1, source_target_pairs={{0,4},{2,6},{4,8},{6,10},{8,12},{10,14},{12,0},{14,2},{1,5},{3,7},... | collective-permute-start | bytes 196616 | tf_op jit(solution)/shard_map/ppermute | solution.py:279
  98.4 11.1 %collective-permute-start.15 = (bf16[32,1024]{1,0:T(8,128)(2,1)S(1)}, bf16[32,1024]{1,0:T(8,128)(2,1)S(1)}, u32[]{:S(2)}, u32[]{:S(2)}) collective-permute-start(bf16[32,1024]{1,0:T(8,128)(2,1)S(1)} %get-tuple-element.28), channel_id=1, source_target_pairs={{0,6},{2,8},{4,10},{6,12},{8,14},{10,0},{12,2},{14,4},{1,7},{3,9},... | collective-permute-start | bytes 196616 | tf_op jit(solution)/shard_map/ppermute | solution.py:279
  99.5 10.3 %collective-permute-start.16 = (bf16[32,1024]{1,0:T(8,128)(2,1)S(1)}, bf16[32,1024]{1,0:T(8,128)(2,1)S(1)}, u32[]{:S(2)}, u32[]{:S(2)}) collective-permute-start(bf16[32,1024]{1,0:T(8,128)(2,1)S(1)} %get-tuple-element.29), channel_id=1, source_target_pairs={{0,8},{2,10},{4,12},{6,14},{8,0},{10,2},{12,4},{14,6},{1,9},{3,11}... | collective-permute-start | bytes 196616 | tf_op jit(solution)/shard_map/ppermute | solution.py:279
  102.2 7.6 %collective-permute-start.17 = (bf16[32,1024]{1,0:T(8,128)(2,1)S(1)}, bf16[32,1024]{1,0:T(8,128)(2,1)S(1)}, u32[]{:S(2)}, u32[]{:S(2)}) collective-permute-start(bf16[32,1024]{1,0:T(8,128)(2,1)S(1)} %get-tuple-element.30), channel_id=1, source_target_pairs={{0,10},{2,12},{4,14},{6,0},{8,2},{10,4},{12,6},{14,8},{1,11},{3,13... | collective-permute-start | bytes 196616 | tf_op jit(solution)/shard_map/ppermute | solution.py:279
  104.6 6.8 %collective-permute-start.18 = (bf16[32,1024]{1,0:T(8,128)(2,1)S(1)}, bf16[32,1024]{1,0:T(8,128)(2,1)S(1)}, u32[]{:S(2)}, u32[]{:S(2)}) collective-permute-start(bf16[32,1024]{1,0:T(8,128)(2,1)S(1)} %get-tuple-element.31), channel_id=1, source_target_pairs={{0,12},{2,14},{4,0},{6,2},{8,4},{10,6},{12,8},{14,10},{1,13},{3,15... | collective-permute-start | bytes 196616 | tf_op jit(solution)/shard_map/ppermute | solution.py:279
  106.2 5.2 %collective-permute-start.19 = (bf16[32,1024]{1,0:T(8,128)(2,1)S(1)}, bf16[32,1024]{1,0:T(8,128)(2,1)S(1)}, u32[]{:S(2)}, u32[]{:S(2)}) collective-permute-start(bf16[32,1024]{1,0:T(8,128)(2,1)S(1)} %get-tuple-element.32), channel_id=1, source_target_pairs={{0,14},{2,0},{4,2},{6,4},{8,6},{10,8},{12,10},{14,12},{1,15},{3,1}... | collective-permute-start | bytes 196616 | tf_op jit(solution)/shard_map/ppermute | solution.py:279

commit v5 on v4

--- a/solution.py
+++ b/solution.py
@@ -30,7 +30,7 @@
     return lax.dot_general(a, b, (((0,), (0,)), ((), ())), preferred_element_type=F32)
 
 
-WIDE = pltpu.CompilerParams(vmem_limit_bytes=52 * 1024 * 1024)
+WIDE = pltpu.CompilerParams(vmem_limit_bytes=24 * 1024 * 1024)
 VMEM = pl.BlockSpec(memory_space=pltpu.VMEM)
 SMEM = pl.BlockSpec(memory_space=pltpu.SMEM)
 ANY = pl.BlockSpec(memory_space=pl.ANY)
@@ -77,7 +77,7 @@
     q_ref[...] = total
 
 
-def rank_kernel(at_ref, d_ref, a_ref, b_ref, c_ref, e_ref, own_ref, dep_ref, send_ref, rest_ref):
+def rank_kernel(at_ref, d_ref, a_ref, b_ref, c_ref, e_ref, own_ref, send_ref, rest_ref):
     lines, rows, width = a_ref.shape
     devices, rank, _ = send_ref.shape
     total = None
@@ -95,10 +95,42 @@
         send_ref[d, :, :rows] = first
 
 
-def split_kernel(q_ref, heads_ref):
+def run_copies(pairs, sems):
+    copies = [pltpu.make_async_copy(a, b, sems.at[i]) for i, (a, b) in enumerate(pairs)]
+    for copy in copies:
+        copy.start()
+    for copy in copies:
+        copy.wait()
+
+
+def split_kernel(m_ref, x_ref, heads_ref, out_ref, sems):
     devices, _, cols = heads_ref.shape
-    for d in range(devices):
-        heads_ref[d] = q_ref[:, d * cols : (d + 1) * cols]
+    pieces = [(m_ref.at[:, d * cols : (d + 1) * cols], heads_ref.at[d]) for d in range(devices)]
+    run_copies([(x_ref, out_ref)] + pieces, sems)
+
+
+def ahead_kernel(dep_ref, *refs):
+    count = (len(refs) - 1) // 2
+    run_copies(list(zip(refs[:count], refs[count : 2 * count])), refs[-1])
+
+
+def in_hbm(v):
+    return pltpu.with_memory_space_constraint(v, pltpu.HBM)
+
+
+def ahead(dep, *arrays):
+    return pl.pallas_call(
+        ahead_kernel,
+        out_shape=[jax.ShapeDtypeStruct(v.shape, v.dtype) for v in arrays],
+        in_specs=[ANY] * (1 + len(arrays)),
+        out_specs=[ANY] * len(arrays),
+        scratch_shapes=[pltpu.SemaphoreType.DMA((len(arrays),))],
+        compiler_params=PARAMS,
+    )(dep, *[in_hbm(v) for v in arrays])
+
+
+def pass_kernel(x_ref, dep_ref, o_ref):
+    o_ref[...] = x_ref[...]
 
 
 def kv_kernel(x_ref, w_ref, own_ref, kup_ref, vup_ref, o_ref):
@@ -212,21 +244,21 @@
         copy.wait()
 
 
-def out_kernel(cross, at_ref, x_ref, w_ref, rank_ref, up_ref, o_ref):
+def out_kernel(cross, places, at_ref, x_ref, w_ref, rank_ref, up_ref, o_ref):
     width = o_ref.shape[2]
+    chips = w_ref.shape[0]
     core = 1 - at_ref[1] if cross else at_ref[1]
     x = x_ref[...]
     rank = rank_ref[...]
-    for c in range(o_ref.shape[0]):
-        lanes = pl.ds(pl.multiple_of((2 * c + core) * width, width), width)
-        o_ref[c] = nn(x, w_ref[c]) + SCALE * tn(rank, up_ref[:, lanes])
-
-
-def pair_kernel(at_ref, a_ref, b_ref, *outs):
-    chips = len(outs)
-    for k, out in enumerate(outs):
+    for i, k in enumerate(places):
         dest = lax.rem(at_ref[0] + k, chips)
-        out[...] = (a_ref[dest] + b_ref[dest]).astype(BF16)
+        lanes = pl.ds(pl.multiple_of((2 * dest + core) * width, width), width)
+        o_ref[i] = nn(x, w_ref[dest]) + SCALE * tn(rank, up_ref[:, lanes])
+
+
+def pair_kernel(a_ref, b_ref, *outs):
+    for i, out in enumerate(outs):
+        out[...] = (a_ref[i] + b_ref[i]).astype(BF16)
 
 
 def total_kernel(*refs):
@@ -281,14 +313,43 @@
     def exchange(v):
         return lax.all_to_all(v, both, 0, 0, tiled=True)
 
-    def gather(v):
-        line = stack([shift_chip(v, 2 * k) for k in range(lines)])
+    def gather(v, own, after=None):
+        line = stack([own] + [shift_chip(v, 2 * k) for k in range(1, lines)])
         across = swap_y(line)
+        if after is not None:
+            across = pl.pallas_call(
+                pass_kernel,
+                out_shape=jax.ShapeDtypeStruct(across.shape, across.dtype),
+                in_specs=[VMEM, ANY],
+                compiler_params=PARAMS,
+            )(across, after)
         return line, across, swap_core(line), swap_core(across)
 
     x = tokens.reshape(rows, width)
-    down = adapter_down_maps[0]
-    gathered = gather(x)
+    by_heads, own_x = pl.pallas_call(
+        split_kernel,
+        out_shape=(
+            jax.ShapeDtypeStruct((devices, rank, cols), BF16),
+            jax.ShapeDtypeStruct((rows, width), BF16),
+        ),
+        in_specs=[ANY, ANY],
+        out_specs=(ANY, ANY),
+        scratch_shapes=[pltpu.SemaphoreType.DMA((devices + 1,))],
+        compiler_params=PARAMS,
+    )(in_hbm(query_up_maps[0]), in_hbm(x))
+    ups = exchange(by_heads)
+    gathered = gather(x, own_x, ups)
+    down, kv_weight, key_up, value_up, old_keys, old_values, lowering, out_up = ahead(
+        gathered[0],
+        adapter_down_maps[0],
+        key_value_weight,
+        key_up_maps[0],
+        value_up_maps[0],
+        cached_rotated_keys[0],
+        cached_values[0],
+        result_lowering_factors[0],
+        output_up_maps[0],
+    )
 
     index = jnp.arange(devices, dtype=jnp.int32)
     slot = jnp.sum(
@@ -298,22 +359,15 @@
     spread_mask = (jnp.repeat(index, rank)[:, None] == row_slot).astype(F32)
     own_mask = (row_slot == me).astype(F32)
 
-    ups = exchange(
-        pl.pallas_call(
-            split_kernel,
-            out_shape=jax.ShapeDtypeStruct((devices, rank, cols), BF16),
-            compiler_params=PARAMS,
-        )(query_up_maps[0])
-    )
     rank_send, rank_rest = pl.pallas_call(
         rank_kernel,
         out_shape=(
             jax.ShapeDtypeStruct((devices, rank, padded), BF16),
             jax.ShapeDtypeStruct((2 * rank, rows), BF16),
         ),
-        in_specs=[SMEM] + [VMEM] * 6 + [ANY],
-        compiler_params=PARAMS,
-    )(at, down, *gathered, own_mask, ups)
+        in_specs=[SMEM] + [VMEM] * 6,
+        compiler_params=PARAMS,
+    )(at, down, *gathered, own_mask)
     ranks = exchange(rank_send)
     query = pl.pallas_call(
         query_kernel,
@@ -324,13 +378,13 @@
             pltpu.SemaphoreType.DMA((devices,)),
         ],
         compiler_params=WIDE,
-    )(at, query_weight, *gathered, rank_send)
+    )(at, in_hbm(query_weight), *gathered, rank_send)
     kv_width = key_value_weight.shape[1]
     kv = pl.pallas_call(
         kv_kernel,
         out_shape=jax.ShapeDtypeStruct((rows, kv_width), F32),
         compiler_params=PARAMS,
-    )(x, key_value_weight, rank_rest, key_up_maps[0], value_up_maps[0])
+    )(own_x, kv_weight, rank_rest, key_up, value_up)
     to_rows = pl.pallas_call(
         finish_kernel,
         out_shape=jax.ShapeDtypeStruct((devices, steps, cols + kv_width), F32),
@@ -343,8 +397,8 @@
         in_specs=[SMEM, ANY, ANY],
         out_specs=[ANY, ANY],
         scratch_shapes=[pltpu.SemaphoreType.DMA((devices,))],
-        compiler_params=pltpu.CompilerParams(vmem_limit_bytes=36 * 1024 * 1024),
-    )(at, output_weight, to_rows)
+        compiler_params=PARAMS,
+    )(at, in_hbm(output_weight), to_rows)
 
     half_width = HEAD_WIDTH // 2
     frequency = ROPE_BASE ** (-2.0 * jnp.arange(half_width, dtype=F32) / HEAD_WIDTH)
@@ -368,7 +422,7 @@
             pltpu.VMEM((16, HEAD_WIDTH), F32),
         ],
         compiler_params=PARAMS,
-    )(lengths, arrived, cosine, sine, cached_rotated_keys[0], cached_values[0], fetched[0])
+    )(lengths, arrived, cosine, sine, old_keys, old_values, fetched[0])
     entries = fresh.astype(BF16)[:, None, :]
 
     lhs, out_rank = pl.pallas_call(
@@ -383,24 +437,26 @@
             pltpu.VMEM((rows, heads * HEAD_WIDTH), BF16),
         ],
         compiler_params=PARAMS,
-    )(at, result_lowering_factors[0], own_mask, *gather(context))
-
-    def out_half(cross):
+    )(at, lowering, own_mask, *gather(context, context))
+
+    def out_half(cross, places):
         return pl.pallas_call(
-            functools.partial(out_kernel, cross),
-            out_shape=jax.ShapeDtypeStruct((chips, rows, width), F32),
+            functools.partial(out_kernel, cross, places),
+            out_shape=jax.ShapeDtypeStruct((len(places), rows, width), F32),
             in_specs=[SMEM] + [VMEM] * 4,
             compiler_params=PARAMS,
-        )(at, lhs, fetched[0 if cross else 1], out_rank, output_up_maps[0])
-
-    received = swap_core(out_half(True))
-    chip_totals = pl.pallas_call(
-        pair_kernel,
-        out_shape=[jax.ShapeDtypeStruct((rows, width), BF16)] * chips,
-        in_specs=[SMEM, VMEM, VMEM],
-        compiler_params=PARAMS,
-    )(at, out_half(False), received)
-    final = [shift_chip(v, k) for k, v in enumerate(chip_totals)]
+        )(at, lhs, fetched[0 if cross else 1], out_rank, out_up)
+
+    final = []
+    first = list(range(chips // 4, chips - chips // 4))
+    for places in (first, [k for k in range(chips) if k not in first]):
+        received = swap_core(out_half(True, places))
+        totals = pl.pallas_call(
+            pair_kernel,
+            out_shape=[jax.ShapeDtypeStruct((rows, width), BF16)] * len(places),
+            compiler_params=PARAMS,
+        )(out_half(False, places), received)
+        final += [shift_chip(v, k) for k, v in zip(places, totals)]
     attended = pl.pallas_call(
         total_kernel,
         out_shape=jax.ShapeDtypeStruct((rows, width), BF16),

time: 113 us -> 130 us (1.15)
  Pallas kernels: 26.1 us -> 40.3 us
  starting transfers between devices: 37.3 us -> 44.9 us
  local copies, waits for them, and re-layouts: 17.3 us -> 12.9 us
  waiting for transfers between devices: 28.1 us -> 26.6 us
    pallas_call x3 -> x7, Pallas kernels: 5.28 us -> 17.8 us  [the longest x1 9.2 us: body(): pl.pallas_call(split_kernel, out_shape=(jax.ShapeDtypeStruct((devices, ra...]
    all_to_all x3, waiting for transfers between devices: 7.52 us -> 0.01 us  [exchange(): return lax.all_to_all(v, both, 0, 0, tiled=True)]
    all_to_all x3, starting transfers between devices: 13 us -> 18.9 us  [exchange(): return lax.all_to_all(v, both, 0, 0, tiled=True)]
    ppermute x2, waiting for transfers between devices: 3.56 us -> 8.49 us  [swap_y(): return lax.ppermute(v, 'tp', [(i, i ^ 1) for i in range(chips)])]
    unnamed x32 -> x40, local copies, waits for them, and re-layouts: 17 us -> 12.6 us
    ppermute x13, waiting for transfers between devices: 14.6 us -> 16.8 us  [shift_chip(): return lax.ppermute(v, 'tp', [(i, (i + k) % chips) for i in range(chips)])]
    ppermute x13, starting transfers between devices: 20.6 us -> 22.3 us  [shift_chip(): return lax.ppermute(v, 'tp', [(i, (i + k) % chips) for i in range(chips)])]
  transfers between devices with their start and end apart: 23 -> 24, of which waited for: 15 -> 11; matrix products, arithmetic and copies ran while one was open for 2% -> 3% of each run, Pallas kernels for 15% -> 17%
where the time goes in v5:
time: 130 us; the launch traced here: 129 us
  starting transfers between devices  44.9 us (35%)
  Pallas kernels  40.3 us (31%)
  waiting for transfers between devices  26.6 us (20%)
  local copies, waits for them, and re-layouts  12.9 us (10%)
  other arithmetic  2.99 us (2%)
  between operations  1.64 us (1%)
    ppermute x13, starting transfers between devices, shift_chip(): return lax.ppermute(v, 'tp', [(i, (i + k) % chips) for i in range(chips)])  22.3 us
    all_to_all x3, starting transfers between devices, exchange(): return lax.all_to_all(v, both, 0, 0, tiled=True)  18.9 us
    ppermute x13, waiting for transfers between devices, shift_chip(): return lax.ppermute(v, 'tp', [(i, (i + k) % chips) for i in range(chips)])  16.8 us
    unnamed x40, local copies, waits for them, and re-layouts  12.6 us
    pallas_call x1, Pallas kernels, body(): pl.pallas_call(split_kernel, out_shape=(jax.ShapeDtypeStruct((devices, ra...  9.2 us
    ppermute x2, waiting for transfers between devices, swap_y(): return lax.ppermute(v, 'tp', [(i, i ^ 1) for i in range(chips)])  8.49 us
    pallas_call x1, Pallas kernels, body(): pl.pallas_call(query_kernel, out_shape=jax.ShapeDtypeStruct((rows, cols),...  7.32 us
    pallas_call x1, Pallas kernels, body(): pl.pallas_call(fetch_kernel, out_shape=[jax.ShapeDtypeStruct((chips, cols...  6.55 us
  transfers between devices with their start and end apart: 24, of which 11 were waited for; matrix products, arithmetic and copies ran while one was open for 3% of the time, Pallas kernels for 17%

profile of v5, /device:TPU:0, one launch (start us, length us, event | category | flops | bytes accessed | tf_op | source)
XLA Modules:
  0.0 129.4 jit_solution(17514061446419217033)
XLA Ops:
  0.6 9.2 %shard_map.158 = (bf16[16,16,512]{2,1,0:T(8,128)(2,1)}, bf16[32,1024]{1,0:T(8,128)(2,1)S(1)}) custom-call(bf16[16,8192]{1,0:T(8,128)(2,1)} %bitcast.27, bf16[32,1024]{1,0:T(8,128)(2,1)} %bitcast.28), custom_call_target="tpu_custom_call" | custom-call | tf_op jit(solution)/shard_map/pallas_call | solution.py:329
  9.8 7.4 %all-to-all-start = ((bf16[16,16,512]{2,1,0:T(8,128)(2,1)}), bf16[16,16,512]{2,1,0:T(8,128)(2,1)S(1)}, u32[]{:S(2)}, u32[]{:S(2)}) async-start(bf16[16,16,512]{2,1,0:T(8,128)(2,1)} %get-tuple-element.30), calls=%async_computation | async-start | bytes 524288 | tf_op jit(solution)/shard_map/all_to_all | solution.py:314
  17.3 1.9 %collective-permute-start = (bf16[32,1024]{1,0:T(8,128)(2,1)}, bf16[32,1024]{1,0:T(8,128)(2,1)S(1)}, u32[]{:S(2)}, u32[]{:S(2)}) collective-permute-start(bf16[32,1024]{1,0:T(8,128)(2,1)} %bitcast.29), channel_id=1, source_target_pairs={{0,4},{2,6},{4,8},{6,10},{8,12},{10,14},{12,0},{14,2},{1,5},{3,7},... | collective-permute-start | bytes 196616 | tf_op jit(solution)/shard_map/ppermute | solution.py:311
  19.2 2.4 %collective-permute-start.1 = (bf16[32,1024]{1,0:T(8,128)(2,1)}, bf16[32,1024]{1,0:T(8,128)(2,1)S(1)}, u32[]{:S(2)}, u32[]{:S(2)}) collective-permute-start(bf16[32,1024]{1,0:T(8,128)(2,1)} %bitcast.30), channel_id=1, source_target_pairs={{0,8},{2,10},{4,12},{6,14},{8,0},{10,2},{12,4},{14,6},{1,9},{3,11}... | collective-permute-start | bytes 196616 | tf_op jit(solution)/shard_map/ppermute | solution.py:311
  21.5 1.5 %collective-permute-start.2 = (bf16[32,1024]{1,0:T(8,128)(2,1)}, bf16[32,1024]{1,0:T(8,128)(2,1)S(1)}, u32[]{:S(2)}, u32[]{:S(2)}) collective-permute-start(bf16[32,1024]{1,0:T(8,128)(2,1)} %bitcast.31), channel_id=1, source_target_pairs={{0,12},{2,14},{4,0},{6,2},{8,4},{10,6},{12,8},{14,10},{1,13},{3,15... | collective-permute-start | bytes 196616 | tf_op jit(solution)/shard_map/ppermute | solution.py:311
  23.0 5.3 %collective-permute-done.refs_1_ = bf16[32,1024]{1,0:T(8,128)(2,1)S(1)} collective-permute-done((bf16[32,1024]{1,0:T(8,128)(2,1)}, bf16[32,1024]{1,0:T(8,128)(2,1)S(1)}, u32[]{:S(2)}, u32[]{:S(2)}) %collective-permute-start) | collective-permute-done | bytes 65568 | tf_op jit(solution)/shard_map/ppermute | solution.py:311
  28.3 3.3 %collective-permute-done.1.refs_2_ = bf16[32,1024]{1,0:T(8,128)(2,1)S(1)} collective-permute-done((bf16[32,1024]{1,0:T(8,128)(2,1)}, bf16[32,1024]{1,0:T(8,128)(2,1)S(1)}, u32[]{:S(2)}, u32[]{:S(2)}) %collective-permute-start.1) | collective-permute-done | bytes 65568 | tf_op jit(solution)/shard_map/ppermute | solution.py:311
  31.6 1.5 %collective-permute-start.3 = (bf16[4,32,1024]{2,1,0:T(8,128)(2,1)S(1)}, bf16[4,32,1024]{2,1,0:T(8,128)(2,1)S(1)}, u32[]{:S(2)}, u32[]{:S(2)}) collective-permute-start(bf16[4,32,1024]{2,1,0:T(8,128)(2,1)S(1)} %shard_map.159.dep_ref.a_ref), channel_id=1, source_target_pairs={{0,2},{2,0},{4,6},{6,4},{8,10},{10,8},{12,14},{14,12},{1,3},{3,1},... | collective-permute-start | bytes 786440 | tf_op jit(solution)/shard_map/ppermute | solution.py:306
  33.1 0.9 select_reduce_fusion
  34.0 0.1 collective-permute-start.4
  34.1 5.0 %collective-permute-done.3.x_ref = bf16[4,32,1024]{2,1,0:T(8,128)(2,1)S(1)} collective-permute-done((bf16[4,32,1024]{2,1,0:T(8,128)(2,1)S(1)}, bf16[4,32,1024]{2,1,0:T(8,128)(2,1)S(1)}, u32[]{:S(2)}, u32[]{:S(2)}) %collective-permute-start.3) | collective-permute-done | bytes 262176 | tf_op jit(solution)/shard_map/ppermute | solution.py:306
  39.1 0.1 collective-permute-start.5
  39.2 0.1 convert_element_type.19.own_ref
  39.3 0.1 eq.53
  39.4 0.1 eq.51
  39.4 0.1 pad_add_fusion.at_ref
  39.5 2.6 %shard_map.160 = (bf16[48,16384]{1,0:T(8,128)(2,1)S(1)}, bf16[1024,1024]{1,0:T(8,128)(2,1)S(1)}, bf16[16,512]{1,0:T(8,128)(2,1)S(1)}, bf16[16,512]{1,0:T(8,128)(...) custom-call(bf16[4,32,1024]{2,1,0:T(8,128)(2,1)S(1)} %shard_map.159., ...), custom_call_target="tpu_custom_call" | custom-call | tf_op jit(solution)/shard_map/pallas_call | solution.py:122
  42.2 2.6 %shard_map.162 = (bf16[16,16,128]{2,1,0:T(8,128)(2,1)}, bf16[32,32]{1,0:T(8,128)(2,1)S(1)}) custom-call(s32[2]{0:T(128)S(1)} %pad_add_fusion.at_ref, bf16[48,16384]{1,0:T(8,128)(2,1)S(1)} %get-tuple-element.31.d_ref, bf16[4,32,1024]{2,1,0:T(8,128)(2,1)S(1)} %shard_map.159.dep_ref.a_ref, bf16[4,32,1024]{2,1,0:T(8,128)(2,1)S(1)} %shard_map.161.b_ref, ...), custom_call_target="tpu_custom_call" | custom-call | tf_op jit(solution)/shard_map/pallas_call | solution.py:362
  44.9 5.5 %all-to-all-start.1 = ((bf16[16,16,128]{2,1,0:T(8,128)(2,1)}), bf16[16,16,128]{2,1,0:T(8,128)(2,1)}, u32[]{:S(2)}, u32[]{:S(2)}) async-start(bf16[16,16,128]{2,1,0:T(8,128)(2,1)} %get-tuple-element.32.dep_ref), calls=%async_computation.1 | async-start | bytes 131072 | tf_op jit(solution)/shard_map/all_to_all | solution.py:314
  50.4 0.8 compare_convert_fusion.mask_ref
  51.8 0.5 multiply_power_fusion
  52.3 0.8 copy-done.12
  53.1 0.7 copy-done.14
  53.9 0.7 copy-done.16
  54.6 0.5 shard_map.164.kv_ref
  55.1 7.3 %shard_map.163.q_ref = f32[32,512]{1,0:T(8,128)S(1)} custom-call(s32[2]{0:T(128)S(1)} %pad_add_fusion.at_ref, bf16[16384,512]{1,0:T(8,128)(2,1)} %w_ref.2, bf16[4,32,1024]{2,1,0:T(8,128)(2,1)S(1)} %shard_map.159.dep_ref.a_ref, bf16[4,32,1024]{2,1,0:T(8,128)(2,1)S(1)} %shard_map.161.b_ref, bf16[4,32,1024]{2,1,0:T(8,128)(2,1)} %collective-permute-done.4.c_ref, ...), custom_call_target="tpu_custom_call" | custom-call | tf_op jit(solution)/shard_map/pallas_call | solution.py:372
  62.4 1.7 %shard_map.165.dep_ref = f32[16,2,1536]{2,1,0:T(2,128)} custom-call(f32[32,512]{1,0:T(8,128)S(1)} %shard_map.163.q_ref, f32[32,1024]{1,0:T(8,128)S(1)} %shard_map.164.kv_ref, bf16[16,16,128]{2,1,0:T(8,128)(2,1)} %all-to-all-done.1.ranks_ref, f32[256,32]{1,0:T(8,128)S(1)} %copy-done.8, bf16[16,16,512]{2,1,0:T(8,128)(2,1)S(1)} %all-to-all-done.dep_ref.up_ref), custom_call_target="tpu_custom_call" | custom-call | tf_op jit(solution)/shard_map/pallas_call | solution.py:388
  64.2 6.0 %all-to-all-start.2 = ((f32[16,2,1536]{2,1,0:T(2,128)}), f32[16,2,1536]{2,1,0:T(2,128)S(1)}, u32[]{:S(2)}, u32[]{:S(2)}) async-start(f32[16,2,1536]{2,1,0:T(2,128)} %shard_map.165.dep_ref), calls=%async_computation.2 | async-start | bytes 393216 | tf_op jit(solution)/shard_map/all_to_all | solution.py:314
  70.1 0.1 fusion
  70.3 0.1 pad_maximum_fusion
  70.3 6.5 %shard_map.166 = (bf16[8,512,1024]{2,1,0:T(8,128)(2,1)S(1)}, bf16[8,512,1024]{2,1,0:T(8,128)(2,1)S(1)}) custom-call(s32[2]{0:T(128)S(1)} %pad_add_fusion.at_ref, bf16[512,16384]{1,0:T(8,128)(2,1)} %w_ref.3, f32[16,2,1536]{2,1,0:T(2,128)} %shard_map.165.dep_ref), custom_call_target="tpu_custom_call" | custom-call | tf_op jit(solution)/shard_map/pallas_call | solution.py:394
  76.9 3.3 %copy-done = bf16[8,512,1024]{2,1,0:T(8,128)(2,1)} copy-done((bf16[8,512,1024]{2,1,0:T(8,128)(2,1)}, bf16[8,512,1024]{2,1,0:T(8,128)(2,1)S(1)}, u32[]{:S(2)}) %copy-start) | copy-done | bytes 8388632
  80.2 3.3 %copy-done.3 = bf16[8,512,1024]{2,1,0:T(8,128)(2,1)} copy-done((bf16[8,512,1024]{2,1,0:T(8,128)(2,1)}, bf16[8,512,1024]{2,1,0:T(8,128)(2,1)S(1)}, u32[]{:S(2)}) %copy-start.3) | copy-done | bytes 8388632
  83.6 3.4 %copy-done.1 = bf16[8,512,1024]{2,1,0:T(8,128)(2,1)S(1)} copy-done((bf16[8,512,1024]{2,1,0:T(8,128)(2,1)S(1)}, bf16[8,512,1024]{2,1,0:T(8,128)(2,1)}, u32[]{:S(2)}) %copy-start.1) | copy-done | bytes 8388632
  86.9 1.6 %shard_map.167 = (bf16[128,128]{1,0:T(8,128)(2,1)S(1)}, f32[2,1024]{1,0:T(2,128)S(1)}) custom-call(s32[1]{0:T(128)} %copy.18.len_ref, f32[16,2,1536]{2,1,0:T(2,128)S(1)} %all-to-all-done.2.recv_ref, f32[32,128]{1,0:T(8,128)S(1)} %bitcast.20, f32[32,128]{1,0:T(8,128)S(1)} %bitcast.21, bf16[512,512]{1,0:T(8,128)(2,1)S(1)} %copy-done.5, ...), custom_call_target="tpu_custom_call" | custom-call | tf_op jit(solution)/shard_map/pallas_call | solution.py:412
  88.5 2.0 %collective-permute-start.6 = (bf16[128,128]{1,0:T(8,128)(2,1)S(1)}, bf16[128,128]{1,0:T(8,128)(2,1)S(1)}, u32[]{:S(2)}, u32[]{:S(2)}) collective-permute-start(bf16[128,128]{1,0:T(8,128)(2,1)S(1)} %get-tuple-element.40.refs_0_), channel_id=1, source_target_pairs={{0,4},{2,6},{4,8},{6,10},{8,12},{10,14},{12,0},{14,2},{1,5},{3,7},... | collective-permute-start | bytes 98312 | tf_op jit(solution)/shard_map/ppermute | solution.py:311
  90.5 2.4 %collective-permute-start.7 = (bf16[128,128]{1,0:T(8,128)(2,1)S(1)}, bf16[128,128]{1,0:T(8,128)(2,1)S(1)}, u32[]{:S(2)}, u32[]{:S(2)}) collective-permute-start(bf16[128,128]{1,0:T(8,128)(2,1)S(1)} %get-tuple-element.40.refs_0_), channel_id=1, source_target_pairs={{0,8},{2,10},{4,12},{6,14},{8,0},{10,2},{12,4},{14,6},{1,9},{3,11}... | collective-permute-start | bytes 98312 | tf_op jit(solution)/shard_map/ppermute | solution.py:311
  92.9 1.5 %collective-permute-start.8 = (bf16[128,128]{1,0:T(8,128)(2,1)S(1)}, bf16[128,128]{1,0:T(8,128)(2,1)S(1)}, u32[]{:S(2)}, u32[]{:S(2)}) collective-permute-start(bf16[128,128]{1,0:T(8,128)(2,1)S(1)} %get-tuple-element.40.refs_0_), channel_id=1, source_target_pairs={{0,12},{2,14},{4,0},{6,2},{8,4},{10,6},{12,8},{14,10},{1,13},{3,15... | collective-permute-start | bytes 98312 | tf_op jit(solution)/shard_map/ppermute | solution.py:311
  94.3 0.1 collective-permute-done.6.refs_1_
  94.4 1.4 %collective-permute-done.7.refs_2_ = bf16[128,128]{1,0:T(8,128)(2,1)S(1)} collective-permute-done((bf16[128,128]{1,0:T(8,128)(2,1)S(1)}, bf16[128,128]{1,0:T(8,128)(2,1)S(1)}, u32[]{:S(2)}, u32[]{:S(2)}) %collective-permute-start.7) | collective-permute-done | bytes 32800 | tf_op jit(solution)/shard_map/ppermute | solution.py:311
  95.8 1.0 collective-permute-done.8.refs_3_
  96.8 1.5 %collective-permute-start.9 = (bf16[4,128,128]{2,1,0:T(8,128)(2,1)S(1)}, bf16[4,128,128]{2,1,0:T(8,128)(2,1)S(1)}, u32[]{:S(2)}, u32[]{:S(2)}) collective-permute-start(bf16[4,128,128]{2,1,0:T(8,128)(2,1)S(1)} %shard_map.168.a_ref), channel_id=1, source_target_pairs={{0,2},{2,0},{4,6},{6,4},{8,10},{10,8},{12,14},{14,12},{1,3},{3,1},... | collective-permute-start | bytes 393224 | tf_op jit(solution)/shard_map/ppermute | solution.py:306
  98.3 3.5 %collective-permute-done.9.b_ref = bf16[4,128,128]{2,1,0:T(8,128)(2,1)S(1)} collective-permute-done((bf16[4,128,128]{2,1,0:T(8,128)(2,1)S(1)}, bf16[4,128,128]{2,1,0:T(8,128)(2,1)S(1)}, u32[]{:S(2)}, u32[]{:S(2)}) %collective-permute-start.9) | collective-permute-done | bytes 131104 | tf_op jit(solution)/shard_map/ppermute | solution.py:306
  101.8 1.3 %collective-permute-done.11.d_ref = bf16[4,128,128]{2,1,0:T(8,128)(2,1)S(1)} collective-permute-done((bf16[4,128,128]{2,1,0:T(8,128)(2,1)S(1)}, bf16[4,128,128]{2,1,0:T(8,128)(2,1)S(1)}, u32[]{:S(2)}, u32[]{:S(2)}) %collective-permute-start.11) | collective-permute-done | bytes 131104 | tf_op jit(solution)/shard_map/ppermute | solution.py:303
  103.2 1.5 %shard_map.169 = (bf16[32,512]{1,0:T(8,128)(2,1)S(1)}, bf16[16,32]{1,0:T(8,128)(2,1)S(1)}) custom-call(s32[2]{0:T(128)S(1)} %pad_add_fusion.at_ref, bf16[16,8192]{1,0:T(8,128)(2,1)S(1)} %copy-done.10, f32[1,32]{1,0:T(1,128)S(1)} %convert_element_type.19.own_ref, bf16[4,128,128]{2,1,0:T(8,128)(2,1)S(1)} %shard_map.168.a_ref, ...), custom_call_target="tpu_custom_call" | custom-call | tf_op jit(solution)/shard_map/pallas_call | solution.py:428
  104.6 1.5 %shard_map.174 = f32[4,32,1024]{2,1,0:T(8,128)S(1)} custom-call(s32[2]{0:T(128)S(1)} %pad_add_fusion.at_ref, bf16[32,512]{1,0:T(8,128)(2,1)S(1)} %get-tuple-element.41.x_ref, bf16[8,512,1024]{2,1,0:T(8,128)(2,1)S(1)} %copy-done.2, bf16[16,32]{1,0:T(8,128)(2,1)S(1)} %get-tuple-element.43.rank_ref, bf16[16,16384]{1,0:T(8,128)(2,1)S(1)} %get-tuple-element.44.up_ref), custom_call_target="tpu_custom_call" | custom-call | tf_op jit(solution)/shard_map/pallas_call | solution.py:443
  106.1 0.2 collective-permute-start.17
  106.4 1.5 %shard_map.171 = f32[4,32,1024]{2,1,0:T(8,128)S(1)} custom-call(s32[2]{0:T(128)S(1)} %pad_add_fusion.at_ref, bf16[32,512]{1,0:T(8,128)(2,1)S(1)} %get-tuple-element.41.x_ref, bf16[8,512,1024]{2,1,0:T(8,128)(2,1)S(1)} %copy-done.2, bf16[16,32]{1,0:T(8,128)(2,1)S(1)} %get-tuple-element.43.rank_ref, bf16[16,16384]{1,0:T(8,128)(2,1)S(1)} %get-tuple-element.44.up_ref), custom_call_target="tpu_custom_call" | custom-call | tf_op jit(solution)/shard_map/pallas_call | solution.py:443
  107.8 0.4 collective-permute-start.12
  108.2 0.3 slice-done.1
  108.5 1.5 %shard_map.173.a_ref = f32[4,32,1024]{2,1,0:T(8,128)S(1)} custom-call(s32[2]{0:T(128)S(1)} %pad_add_fusion.at_ref, bf16[32,512]{1,0:T(8,128)(2,1)S(1)} %get-tuple-element.41.x_ref, bf16[8,512,1024]{2,1,0:T(8,128)(2,1)S(1)} %bitcast.19, bf16[16,32]{1,0:T(8,128)(2,1)S(1)} %get-tuple-element.43.rank_ref, bf16[16,16384]{1,0:T(8,128)(2,1)S(1)} %get-tuple-element.44.up_ref), custom_call_target="tpu_custom_call" | custom-call | tf_op jit(solution)/shard_map/pallas_call | solution.py:443
  110.0 0.1 shard_map.175
  110.1 1.5 %collective-permute-start.18 = (bf16[32,1024]{1,0:T(8,128)(2,1)S(1)}, bf16[32,1024]{1,0:T(8,128)(2,1)S(1)}, u32[]{:S(2)}, u32[]{:S(2)}) collective-permute-start(bf16[32,1024]{1,0:T(8,128)(2,1)S(1)} %get-tuple-element.50), channel_id=1, source_target_pairs={{0,2},{2,4},{4,6},{6,8},{8,10},{10,12},{12,14},{14,0},{1,3},{3,5},... | collective-permute-start | bytes 196616 | tf_op jit(solution)/shard_map/ppermute | solution.py:311
  111.6 3.3 %collective-permute-start.19 = (bf16[32,1024]{1,0:T(8,128)(2,1)S(1)}, bf16[32,1024]{1,0:T(8,128)(2,1)S(1)}, u32[]{:S(2)}, u32[]{:S(2)}) collective-permute-start(bf16[32,1024]{1,0:T(8,128)(2,1)S(1)} %get-tuple-element.51), channel_id=1, source_target_pairs={{0,12},{2,14},{4,0},{6,2},{8,4},{10,6},{12,8},{14,10},{1,13},{3,15... | collective-permute-start | bytes 196616 | tf_op jit(solution)/shard_map/ppermute | solution.py:311
  114.8 1.5 %shard_map.170.a_ref = f32[4,32,1024]{2,1,0:T(8,128)S(1)} custom-call(s32[2]{0:T(128)S(1)} %pad_add_fusion.at_ref, bf16[32,512]{1,0:T(8,128)(2,1)S(1)} %get-tuple-element.41.x_ref, bf16[8,512,1024]{2,1,0:T(8,128)(2,1)S(1)} %bitcast.19, bf16[16,32]{1,0:T(8,128)(2,1)S(1)} %get-tuple-element.43.rank_ref, bf16[16,16384]{1,0:T(8,128)(2,1)S(1)} %get-tuple-element.44.up_ref), custom_call_target="tpu_custom_call" | custom-call | tf_op jit(solution)/shard_map/pallas_call | solution.py:443
  116.3 1.5 %collective-permute-start.20 = (bf16[32,1024]{1,0:T(8,128)(2,1)S(1)}, bf16[32,1024]{1,0:T(8,128)(2,1)S(1)}, u32[]{:S(2)}, u32[]{:S(2)}) collective-permute-start(bf16[32,1024]{1,0:T(8,128)(2,1)S(1)} %get-tuple-element.52), channel_id=1, source_target_pairs={{0,14},{2,0},{4,2},{6,4},{8,6},{10,8},{12,10},{14,12},{1,15},{3,1}... | collective-permute-start | bytes 196616 | tf_op jit(solution)/shard_map/ppermute | solution.py:311
  117.8 0.6 collective-permute-start.13
  118.5 3.8 %collective-permute-start.15 = (bf16[32,1024]{1,0:T(8,128)(2,1)S(1)}, bf16[32,1024]{1,0:T(8,128)(2,1)S(1)}, u32[]{:S(2)}, u32[]{:S(2)}) collective-permute-start(bf16[32,1024]{1,0:T(8,128)(2,1)S(1)} %get-tuple-element.47), channel_id=1, source_target_pairs={{0,8},{2,10},{4,12},{6,14},{8,0},{10,2},{12,4},{14,6},{1,9},{3,11}... | collective-permute-start | bytes 196616 | tf_op jit(solution)/shard_map/ppermute | solution.py:311
  122.3 0.1 collective-permute-start.16
  122.4 0.6 convert_bitcast_fusion
  123.0 1.5 %collective-permute-done.13.refs_0_ = bf16[32,1024]{1,0:T(8,128)(2,1)S(1)} collective-permute-done((bf16[32,1024]{1,0:T(8,128)(2,1)S(1)}, bf16[32,1024]{1,0:T(8,128)(2,1)S(1)}, u32[]{:S(2)}, u32[]{:S(2)}) %collective-permute-start.13) | collective-permute-done | bytes 65568 | tf_op jit(solution)/shard_map/ppermute | solution.py:311
  124.5 2.3 %collective-permute-done.14.refs_1_ = bf16[32,1024]{1,0:T(8,128)(2,1)S(1)} collective-permute-done((bf16[32,1024]{1,0:T(8,128)(2,1)S(1)}, bf16[32,1024]{1,0:T(8,128)(2,1)S(1)}, u32[]{:S(2)}, u32[]{:S(2)}) %collective-permute-start.14) | collective-permute-done | bytes 65568 | tf_op jit(solution)/shard_map/ppermute | solution.py:311
  126.8 1.9 %collective-permute-done.15.refs_2_ = bf16[32,1024]{1,0:T(8,128)(2,1)S(1)} collective-permute-done((bf16[32,1024]{1,0:T(8,128)(2,1)S(1)}, bf16[32,1024]{1,0:T(8,128)(2,1)S(1)}, u32[]{:S(2)}, u32[]{:S(2)}) %collective-permute-start.15) | collective-permute-done | bytes 65568 | tf_op jit(solution)/shard_map/ppermute | solution.py:311
  128.7 0.7 shard_map.176
  (61 shorter events, 0.3 us)
Async XLA Ops:
  9.8 21.8 %copy-start.11 = (bf16[32,1024]{1,0:T(8,128)(2,1)}, bf16[32,1024]{1,0:T(8,128)(2,1)S(1)}, u32[]{:S(2)}) copy-start(bf16[32,1024]{1,0:T(8,128)(2,1)S(1)} %get-tuple-element.28.refs_0_.x_ref) | copy-start | bytes 196612
  9.8 29.2 %all-to-all-start = ((bf16[16,16,512]{2,1,0:T(8,128)(2,1)}), bf16[16,16,512]{2,1,0:T(8,128)(2,1)S(1)}, u32[]{:S(2)}, u32[]{:S(2)}) async-start(bf16[16,16,512]{2,1,0:T(8,128)(2,1)} %get-tuple-element.30), calls=%async_computation | async-start | bytes 524288 | tf_op jit(solution)/shard_map/all_to_all | solution.py:314
  17.3 11.0 %collective-permute-start = (bf16[32,1024]{1,0:T(8,128)(2,1)}, bf16[32,1024]{1,0:T(8,128)(2,1)S(1)}, u32[]{:S(2)}, u32[]{:S(2)}) collective-permute-start(bf16[32,1024]{1,0:T(8,128)(2,1)} %bitcast.29), channel_id=1, source_target_pairs={{0,4},{2,6},{4,8},{6,10},{8,12},{10,14},{12,0},{14,2},{1,5},{3,7},... | collective-permute-start | bytes 196616 | tf_op jit(solution)/shard_map/ppermute | solution.py:311
  19.2 12.4 %collective-permute-start.1 = (bf16[32,1024]{1,0:T(8,128)(2,1)}, bf16[32,1024]{1,0:T(8,128)(2,1)S(1)}, u32[]{:S(2)}, u32[]{:S(2)}) collective-permute-start(bf16[32,1024]{1,0:T(8,128)(2,1)} %bitcast.30), channel_id=1, source_target_pairs={{0,8},{2,10},{4,12},{6,14},{8,0},{10,2},{12,4},{14,6},{1,9},{3,11}... | collective-permute-start | bytes 196616 | tf_op jit(solution)/shard_map/ppermute | solution.py:311
  21.5 10.0 %collective-permute-start.2 = (bf16[32,1024]{1,0:T(8,128)(2,1)}, bf16[32,1024]{1,0:T(8,128)(2,1)S(1)}, u32[]{:S(2)}, u32[]{:S(2)}) collective-permute-start(bf16[32,1024]{1,0:T(8,128)(2,1)} %bitcast.31), channel_id=1, source_target_pairs={{0,12},{2,14},{4,0},{6,2},{8,4},{10,6},{12,8},{14,10},{1,13},{3,15... | collective-permute-start | bytes 196616 | tf_op jit(solution)/shard_map/ppermute | solution.py:311
  31.6 7.4 %collective-permute-start.3 = (bf16[4,32,1024]{2,1,0:T(8,128)(2,1)S(1)}, bf16[4,32,1024]{2,1,0:T(8,128)(2,1)S(1)}, u32[]{:S(2)}, u32[]{:S(2)}) collective-permute-start(bf16[4,32,1024]{2,1,0:T(8,128)(2,1)S(1)} %shard_map.159.dep_ref.a_ref), channel_id=1, source_target_pairs={{0,2},{2,0},{4,6},{6,4},{8,10},{10,8},{12,14},{14,12},{1,3},{3,1},... | collective-permute-start | bytes 786440 | tf_op jit(solution)/shard_map/ppermute | solution.py:306
  34.0 8.2 %collective-permute-start.4 = (bf16[4,32,1024]{2,1,0:T(8,128)(2,1)S(1)}, bf16[4,32,1024]{2,1,0:T(8,128)(2,1)}, u32[]{:S(2)}, u32[]{:S(2)}) collective-permute-start(bf16[4,32,1024]{2,1,0:T(8,128)(2,1)S(1)} %shard_map.159.dep_ref.a_ref), channel_id=1, source_target_pairs={{0,1},{1,0},{2,3},{3,2},{4,5},{5,4},{6,7},{7,6},{8,9},{9,8},{10,11... | collective-permute-start | bytes 786440 | tf_op jit(solution)/shard_map/ppermute | solution.py:303
  39.1 3.2 %collective-permute-start.5 = (bf16[4,32,1024]{2,1,0:T(8,128)(2,1)S(1)}, bf16[4,32,1024]{2,1,0:T(8,128)(2,1)}, u32[]{:S(2)}, u32[]{:S(2)}) collective-permute-start(bf16[4,32,1024]{2,1,0:T(8,128)(2,1)S(1)} %shard_map.161.b_ref), channel_id=1, source_target_pairs={{0,1},{1,0},{2,3},{3,2},{4,5},{5,4},{6,7},{7,6},{8,9},{9,8},{10,11... | collective-permute-start | bytes 786440 | tf_op jit(solution)/shard_map/ppermute | solution.py:303
  42.2 2.7 %copy-start.4 = (bf16[512,512]{1,0:T(8,128)(2,1)}, bf16[512,512]{1,0:T(8,128)(2,1)S(1)}, u32[]{:S(2)}) copy-start(bf16[512,512]{1,0:T(8,128)(2,1)S(1)} %get-tuple-element.37.k_ref) | copy-start | bytes 1572868
  42.2 2.7 %copy-start.6 = (bf16[512,512]{1,0:T(8,128)(2,1)}, bf16[512,512]{1,0:T(8,128)(2,1)S(1)}, u32[]{:S(2)}) copy-start(bf16[512,512]{1,0:T(8,128)(2,1)S(1)} %get-tuple-element.38.v_ref) | copy-start | bytes 1572868
  42.2 2.7 %copy-start.9 = (bf16[16,8192]{1,0:T(8,128)(2,1)}, bf16[16,8192]{1,0:T(8,128)(2,1)S(1)}, u32[]{:S(2)}) copy-start(bf16[16,8192]{1,0:T(8,128)(2,1)S(1)} %get-tuple-element.29.low_ref) | copy-start | bytes 786436
  42.2 10.1 %copy-start.13 = (bf16[16,512]{1,0:T(8,128)(2,1)}, bf16[16,512]{1,0:T(8,128)(2,1)S(1)}, u32[]{:S(2)}) copy-start(bf16[16,512]{1,0:T(8,128)(2,1)S(1)} %get-tuple-element.35.kup_ref) | copy-start | bytes 49156
  42.2 10.1 %copy-start.15 = (bf16[16,512]{1,0:T(8,128)(2,1)}, bf16[16,512]{1,0:T(8,128)(2,1)S(1)}, u32[]{:S(2)}) copy-start(bf16[16,512]{1,0:T(8,128)(2,1)S(1)} %get-tuple-element.36.vup_ref) | copy-start | bytes 49156
  44.9 17.6 %all-to-all-start.1 = ((bf16[16,16,128]{2,1,0:T(8,128)(2,1)}), bf16[16,16,128]{2,1,0:T(8,128)(2,1)}, u32[]{:S(2)}, u32[]{:S(2)}) async-start(bf16[16,16,128]{2,1,0:T(8,128)(2,1)} %get-tuple-element.32.dep_ref), calls=%async_computation.1 | async-start | bytes 131072 | tf_op jit(solution)/shard_map/all_to_all | solution.py:314
  52.3 0.8 copy-start.12
  53.1 0.7 copy-start.14
  53.9 0.7 copy-start.16
  55.1 7.4 %copy-start.8 = (f32[256,32]{1,0:T(8,128)S(1)}, f32[256,32]{1,0:T(8,128)}, u32[]{:S(2)}) copy-start(f32[256,32]{1,0:T(8,128)} %compare_convert_fusion.mask_ref) | copy-start | bytes 98308
  55.1 15.1 %copy-start.17 = (f32[64]{0:T(128)S(1)}, f32[64]{0:T(128)}, u32[]{:S(2)}) copy-start(f32[64]{0:T(128)} %multiply_power_fusion) | copy-start | bytes 772
  64.2 19.3 %all-to-all-start.2 = ((f32[16,2,1536]{2,1,0:T(2,128)}), f32[16,2,1536]{2,1,0:T(2,128)S(1)}, u32[]{:S(2)}, u32[]{:S(2)}) async-start(f32[16,2,1536]{2,1,0:T(2,128)} %shard_map.165.dep_ref), calls=%async_computation.2 | async-start | bytes 393216 | tf_op jit(solution)/shard_map/all_to_all | solution.py:314
  70.3 13.2 %copy-start.5 = (bf16[512,512]{1,0:T(8,128)(2,1)S(1)}, bf16[512,512]{1,0:T(8,128)(2,1)}, u32[]{:S(2)}) copy-start(bf16[512,512]{1,0:T(8,128)(2,1)} %copy-done.4) | copy-start | bytes 1572868
  70.3 13.2 %copy-start.7 = (bf16[512,512]{1,0:T(8,128)(2,1)S(1)}, bf16[512,512]{1,0:T(8,128)(2,1)}, u32[]{:S(2)}) copy-start(bf16[512,512]{1,0:T(8,128)(2,1)} %copy-done.6) | copy-start | bytes 1572868
  70.3 32.8 %copy-start.10 = (bf16[16,8192]{1,0:T(8,128)(2,1)S(1)}, bf16[16,8192]{1,0:T(8,128)(2,1)}, u32[]{:S(2)}) copy-start(bf16[16,8192]{1,0:T(8,128)(2,1)} %copy-done.9) | copy-start | bytes 786436
  76.9 3.3 %copy-start = (bf16[8,512,1024]{2,1,0:T(8,128)(2,1)}, bf16[8,512,1024]{2,1,0:T(8,128)(2,1)S(1)}, u32[]{:S(2)}) copy-start(bf16[8,512,1024]{2,1,0:T(8,128)(2,1)S(1)} %get-tuple-element.39.dep_ref.w_ref) | copy-start | bytes 25165828
  80.2 3.3 %copy-start.3 = (bf16[8,512,1024]{2,1,0:T(8,128)(2,1)}, bf16[8,512,1024]{2,1,0:T(8,128)(2,1)S(1)}, u32[]{:S(2)}) copy-start(bf16[8,512,1024]{2,1,0:T(8,128)(2,1)S(1)} %get-tuple-element.42.w_ref) | copy-start | bytes 25165828
  83.5 3.4 %copy-start.1 = (bf16[8,512,1024]{2,1,0:T(8,128)(2,1)S(1)}, bf16[8,512,1024]{2,1,0:T(8,128)(2,1)}, u32[]{:S(2)}) copy-start(bf16[8,512,1024]{2,1,0:T(8,128)(2,1)} %copy-done) | copy-start | bytes 25165828
  86.9 17.7 %copy-start.2 = (bf16[8,512,1024]{2,1,0:T(8,128)(2,1)S(1)}, bf16[8,512,1024]{2,1,0:T(8,128)(2,1)}, u32[]{:S(2)}) copy-start(bf16[8,512,1024]{2,1,0:T(8,128)(2,1)} %copy-done) | copy-start | bytes 25165828
  88.5 5.9 %collective-permute-start.6 = (bf16[128,128]{1,0:T(8,128)(2,1)S(1)}, bf16[128,128]{1,0:T(8,128)(2,1)S(1)}, u32[]{:S(2)}, u32[]{:S(2)}) collective-permute-start(bf16[128,128]{1,0:T(8,128)(2,1)S(1)} %get-tuple-element.40.refs_0_), channel_id=1, source_target_pairs={{0,4},{2,6},{4,8},{6,10},{8,12},{10,14},{12,0},{14,2},{1,5},{3,7},... | collective-permute-start | bytes 98312 | tf_op jit(solution)/shard_map/ppermute | solution.py:311
  90.5 5.3 %collective-permute-start.7 = (bf16[128,128]{1,0:T(8,128)(2,1)S(1)}, bf16[128,128]{1,0:T(8,128)(2,1)S(1)}, u32[]{:S(2)}, u32[]{:S(2)}) collective-permute-start(bf16[128,128]{1,0:T(8,128)(2,1)S(1)} %get-tuple-element.40.refs_0_), channel_id=1, source_target_pairs={{0,8},{2,10},{4,12},{6,14},{8,0},{10,2},{12,4},{14,6},{1,9},{3,11}... | collective-permute-start | bytes 98312 | tf_op jit(solution)/shard_map/ppermute | solution.py:311
  92.9 3.9 %collective-permute-start.8 = (bf16[128,128]{1,0:T(8,128)(2,1)S(1)}, bf16[128,128]{1,0:T(8,128)(2,1)S(1)}, u32[]{:S(2)}, u32[]{:S(2)}) collective-permute-start(bf16[128,128]{1,0:T(8,128)(2,1)S(1)} %get-tuple-element.40.refs_0_), channel_id=1, source_target_pairs={{0,12},{2,14},{4,0},{6,2},{8,4},{10,6},{12,8},{14,10},{1,13},{3,15... | collective-permute-start | bytes 98312 | tf_op jit(solution)/shard_map/ppermute | solution.py:311
  96.8 5.0 %collective-permute-start.9 = (bf16[4,128,128]{2,1,0:T(8,128)(2,1)S(1)}, bf16[4,128,128]{2,1,0:T(8,128)(2,1)S(1)}, u32[]{:S(2)}, u32[]{:S(2)}) collective-permute-start(bf16[4,128,128]{2,1,0:T(8,128)(2,1)S(1)} %shard_map.168.a_ref), channel_id=1, source_target_pairs={{0,2},{2,0},{4,6},{6,4},{8,10},{10,8},{12,14},{14,12},{1,3},{3,1},... | collective-permute-start | bytes 393224 | tf_op jit(solution)/shard_map/ppermute | solution.py:306
  98.3 3.5 %collective-permute-start.10 = (bf16[4,128,128]{2,1,0:T(8,128)(2,1)S(1)}, bf16[4,128,128]{2,1,0:T(8,128)(2,1)S(1)}, u32[]{:S(2)}, u32[]{:S(2)}) collective-permute-start(bf16[4,128,128]{2,1,0:T(8,128)(2,1)S(1)} %shard_map.168.a_ref), channel_id=1, source_target_pairs={{0,1},{1,0},{2,3},{3,2},{4,5},{5,4},{6,7},{7,6},{8,9},{9,8},{10,11... | collective-permute-start | bytes 393224 | tf_op jit(solution)/shard_map/ppermute | solution.py:303
  101.8 1.3 %collective-permute-start.11 = (bf16[4,128,128]{2,1,0:T(8,128)(2,1)S(1)}, bf16[4,128,128]{2,1,0:T(8,128)(2,1)S(1)}, u32[]{:S(2)}, u32[]{:S(2)}) collective-permute-start(bf16[4,128,128]{2,1,0:T(8,128)(2,1)S(1)} %collective-permute-done.9.b_ref), channel_id=1, source_target_pairs={{0,1},{1,0},{2,3},{3,2},{4,5},{5,4},{6,7},{7,6},{8,9},{9,8},{10,11... | collective-permute-start | bytes 393224 | tf_op jit(solution)/shard_map/ppermute | solution.py:303
  104.6 3.6 %slice-start = ((s8[8388608]{0:T(1024)(128)(4,1)}), s8[4194304]{0:T(1024)(128)(4,1)S(1)}, s32[]{:S(2)}) async-start(s8[8388608]{0:T(1024)(128)(4,1)} %bitcast.18), calls=%async_computation.3 | async-start | bytes 8388608
  106.1 2.4 %slice-start.1 = ((s8[8388608]{0:T(1024)(128)(4,1)}), s8[4194304]{0:T(1024)(128)(4,1)S(1)}, s32[]{:S(2)}) async-start(s8[8388608]{0:T(1024)(128)(4,1)} %bitcast.18), calls=%async_computation.4 | async-start | bytes 8388608
  106.1 3.8 %collective-permute-start.17 = (f32[4,32,1024]{2,1,0:T(8,128)S(1)}, f32[4,32,1024]{2,1,0:T(8,128)S(1)}, u32[]{:S(2)}, u32[]{:S(2)}) collective-permute-start(f32[4,32,1024]{2,1,0:T(8,128)S(1)} %shard_map.174), channel_id=1, source_target_pairs={{0,1},{1,0},{2,3},{3,2},{4,5},{5,4},{6,7},{7,6},{8,9},{9,8},{10,11... | collective-permute-start | bytes 1572872 | tf_op jit(solution)/shard_map/ppermute | solution.py:303
  107.8 9.9 %collective-permute-start.12 = (f32[4,32,1024]{2,1,0:T(8,128)S(1)}, f32[4,32,1024]{2,1,0:T(8,128)S(1)}, u32[]{:S(2)}, u32[]{:S(2)}) collective-permute-start(f32[4,32,1024]{2,1,0:T(8,128)S(1)} %shard_map.171), channel_id=1, source_target_pairs={{0,1},{1,0},{2,3},{3,2},{4,5},{5,4},{6,7},{7,6},{8,9},{9,8},{10,11... | collective-permute-start | bytes 1572872 | tf_op jit(solution)/shard_map/ppermute | solution.py:303
  110.1 8.4 %collective-permute-start.18 = (bf16[32,1024]{1,0:T(8,128)(2,1)S(1)}, bf16[32,1024]{1,0:T(8,128)(2,1)S(1)}, u32[]{:S(2)}, u32[]{:S(2)}) collective-permute-start(bf16[32,1024]{1,0:T(8,128)(2,1)S(1)} %get-tuple-element.50), channel_id=1, source_target_pairs={{0,2},{2,4},{4,6},{6,8},{8,10},{10,12},{12,14},{14,0},{1,3},{3,5},... | collective-permute-start | bytes 196616 | tf_op jit(solution)/shard_map/ppermute | solution.py:311
  111.6 10.7 %collective-permute-start.19 = (bf16[32,1024]{1,0:T(8,128)(2,1)S(1)}, bf16[32,1024]{1,0:T(8,128)(2,1)S(1)}, u32[]{:S(2)}, u32[]{:S(2)}) collective-permute-start(bf16[32,1024]{1,0:T(8,128)(2,1)S(1)} %get-tuple-element.51), channel_id=1, source_target_pairs={{0,12},{2,14},{4,0},{6,2},{8,4},{10,6},{12,8},{14,10},{1,13},{3,15... | collective-permute-start | bytes 196616 | tf_op jit(solution)/shard_map/ppermute | solution.py:311
  116.3 6.6 %collective-permute-start.20 = (bf16[32,1024]{1,0:T(8,128)(2,1)S(1)}, bf16[32,1024]{1,0:T(8,128)(2,1)S(1)}, u32[]{:S(2)}, u32[]{:S(2)}) collective-permute-start(bf16[32,1024]{1,0:T(8,128)(2,1)S(1)} %get-tuple-element.52), channel_id=1, source_target_pairs={{0,14},{2,0},{4,2},{6,4},{8,6},{10,8},{12,10},{14,12},{1,15},{3,1}... | collective-permute-start | bytes 196616 | tf_op jit(solution)/shard_map/ppermute | solution.py:311
  117.8 6.7 %collective-permute-start.13 = (bf16[32,1024]{1,0:T(8,128)(2,1)S(1)}, bf16[32,1024]{1,0:T(8,128)(2,1)S(1)}, u32[]{:S(2)}, u32[]{:S(2)}) collective-permute-start(bf16[32,1024]{1,0:T(8,128)(2,1)S(1)} %get-tuple-element.45), channel_id=1, source_target_pairs={{0,4},{2,6},{4,8},{6,10},{8,12},{10,14},{12,0},{14,2},{1,5},{3,7},... | collective-permute-start | bytes 196616 | tf_op jit(solution)/shard_map/ppermute | solution.py:311
  118.5 8.3 %collective-permute-start.14 = (bf16[32,1024]{1,0:T(8,128)(2,1)S(1)}, bf16[32,1024]{1,0:T(8,128)(2,1)S(1)}, u32[]{:S(2)}, u32[]{:S(2)}) collective-permute-start(bf16[32,1024]{1,0:T(8,128)(2,1)S(1)} %get-tuple-element.46), channel_id=1, source_target_pairs={{0,6},{2,8},{4,10},{6,12},{8,14},{10,0},{12,2},{14,4},{1,7},{3,9},... | collective-permute-start | bytes 196616 | tf_op jit(solution)/shard_map/ppermute | solution.py:311
  118.5 10.2 %collective-permute-start.15 = (bf16[32,1024]{1,0:T(8,128)(2,1)S(1)}, bf16[32,1024]{1,0:T(8,128)(2,1)S(1)}, u32[]{:S(2)}, u32[]{:S(2)}) collective-permute-start(bf16[32,1024]{1,0:T(8,128)(2,1)S(1)} %get-tuple-element.47), channel_id=1, source_target_pairs={{0,8},{2,10},{4,12},{6,14},{8,0},{10,2},{12,4},{14,6},{1,9},{3,11}... | collective-permute-start | bytes 196616 | tf_op jit(solution)/shard_map/ppermute | solution.py:311
  122.3 6.4 %collective-permute-start.16 = (bf16[32,1024]{1,0:T(8,128)(2,1)S(1)}, bf16[32,1024]{1,0:T(8,128)(2,1)S(1)}, u32[]{:S(2)}, u32[]{:S(2)}) collective-permute-start(bf16[32,1024]{1,0:T(8,128)(2,1)S(1)} %get-tuple-element.48), channel_id=1, source_target_pairs={{0,10},{2,12},{4,14},{6,0},{8,2},{10,4},{12,6},{14,8},{1,11},{3,13... | collective-permute-start | bytes 196616 | tf_op jit(solution)/shard_map/ppermute | solution.py:311

commit v6 on v4

--- a/solution.py
+++ b/solution.py
@@ -30,7 +30,7 @@
     return lax.dot_general(a, b, (((0,), (0,)), ((), ())), preferred_element_type=F32)
 
 
-WIDE = pltpu.CompilerParams(vmem_limit_bytes=52 * 1024 * 1024)
+WIDE = pltpu.CompilerParams(vmem_limit_bytes=24 * 1024 * 1024)
 VMEM = pl.BlockSpec(memory_space=pltpu.VMEM)
 SMEM = pl.BlockSpec(memory_space=pltpu.SMEM)
 ANY = pl.BlockSpec(memory_space=pl.ANY)
@@ -45,39 +45,52 @@
     return 4 * z + 2 * (1 - y if flip else y) + core
 
 
-def stack_kernel(*refs):
-    for k, r in enumerate(refs[:-1]):
-        refs[-1][k] = r[...]
-
-
-def stack(pieces):
+def stack_kernel(count, *refs):
+    for k in range(count):
+        refs[-1][k] = refs[k][...]
+
+
+def stack(pieces, *deps):
     return pl.pallas_call(
-        stack_kernel,
+        functools.partial(stack_kernel, len(pieces)),
         out_shape=jax.ShapeDtypeStruct((len(pieces),) + pieces[0].shape, pieces[0].dtype),
-        compiler_params=PARAMS,
-    )(*pieces)
-
-
-def query_kernel(at_ref, w_ref, a_ref, b_ref, c_ref, d_ref, dep_ref, q_ref, w_s, sems):
+        in_specs=[VMEM] * len(pieces) + [ANY] * len(deps),
+        compiler_params=PARAMS,
+    )(*pieces, *deps)
+
+
+def query_kernel(at_ref, w_ref, kw_ref, kup_ref, vup_ref, own_ref, x_ref, a_ref, b_ref, c_ref, d_ref, *refs):
+    dep_ref, q_ref, kv_ref, w_s, kw_s, kup_s, vup_s, sems, kv_sems = refs
     lines, _, width = a_ref.shape
+    kv_copies = [
+        pltpu.make_async_copy(source, target, kv_sems.at[i])
+        for i, (source, target) in enumerate(((kw_ref, kw_s), (kup_ref, kup_s), (vup_ref, vup_s)))
+    ]
     copies = []
     for flip, cross in KINDS:
         for k in range(lines):
             i = len(copies)
             start = pl.multiple_of(piece_at(at_ref, 2 * lines, k, flip, cross) * width, width)
-            copy = pltpu.make_async_copy(w_ref.at[pl.ds(start, width)], w_s.at[i], sems.at[i])
-            copy.start()
-            copies.append(copy)
+            copies.append(pltpu.make_async_copy(w_ref.at[pl.ds(start, width)], w_s.at[i], sems.at[i]))
+    for copy in kv_copies + copies:
+        copy.start()
+    for copy in kv_copies:
+        copy.wait()
+    rank, half = kup_s.shape
+    own = own_ref[...]
+    both = nn(x_ref[...], kw_s[...])
+    kv_ref[:, :half] = both[:, :half] + SCALE * tn(own[:rank], kup_s[...])
+    kv_ref[:, half:] = both[:, half:] + SCALE * tn(own[rank:], vup_s[...])
     total = None
     for i, copy in enumerate(copies):
-        x_ref = (a_ref, b_ref, c_ref, d_ref)[i // lines]
+        stack_ref = (a_ref, b_ref, c_ref, d_ref)[i // lines]
         copy.wait()
-        part = nn(x_ref[i % lines], w_s[i])
+        part = nn(stack_ref[i % lines], w_s[i])
         total = part if total is None else total + part
     q_ref[...] = total
 
 
-def rank_kernel(at_ref, d_ref, a_ref, b_ref, c_ref, e_ref, own_ref, dep_ref, send_ref, rest_ref):
+def rank_kernel(at_ref, d_ref, a_ref, b_ref, c_ref, e_ref, own_ref, send_ref, rest_ref):
     lines, rows, width = a_ref.shape
     devices, rank, _ = send_ref.shape
     total = None
@@ -95,18 +108,42 @@
         send_ref[d, :, :rows] = first
 
 
-def split_kernel(q_ref, heads_ref):
+def run_copies(pairs, sems):
+    copies = [pltpu.make_async_copy(a, b, sems.at[i]) for i, (a, b) in enumerate(pairs)]
+    for copy in copies:
+        copy.start()
+    for copy in copies:
+        copy.wait()
+
+
+def split_kernel(m_ref, dep_ref, heads_ref):
     devices, _, cols = heads_ref.shape
     for d in range(devices):
-        heads_ref[d] = q_ref[:, d * cols : (d + 1) * cols]
-
-
-def kv_kernel(x_ref, w_ref, own_ref, kup_ref, vup_ref, o_ref):
-    rank, half = kup_ref.shape
-    own = own_ref[...]
-    both = nn(x_ref[...], w_ref[...])
-    o_ref[:, :half] = both[:, :half] + SCALE * tn(own[:rank], kup_ref[...])
-    o_ref[:, half:] = both[:, half:] + SCALE * tn(own[rank:], vup_ref[...])
+        heads_ref[d] = m_ref[:, d * cols : (d + 1) * cols]
+
+
+def ahead_kernel(dep_ref, *refs):
+    count = (len(refs) - 1) // 2
+    run_copies(list(zip(refs[:count], refs[count : 2 * count])), refs[-1])
+
+
+def in_hbm(v):
+    return pltpu.with_memory_space_constraint(v, pltpu.HBM)
+
+
+def ahead(dep, *arrays):
+    return pl.pallas_call(
+        ahead_kernel,
+        out_shape=[jax.ShapeDtypeStruct(v.shape, v.dtype) for v in arrays],
+        in_specs=[ANY] * (1 + len(arrays)),
+        out_specs=[ANY] * len(arrays),
+        scratch_shapes=[pltpu.SemaphoreType.DMA((len(arrays),))],
+        compiler_params=PARAMS,
+    )(dep, *[in_hbm(v) for v in arrays])
+
+
+def pass_kernel(x_ref, dep_ref, o_ref):
+    o_ref[...] = x_ref[...]
 
 
 def finish_kernel(q_ref, kv_ref, ranks_ref, mask_ref, up_ref, o_ref):
@@ -130,7 +167,13 @@
     return v * cosine + pltpu.roll(v, HEAD_WIDTH // 2, 1) * sine
 
 
-def attend_kernel(len_ref, recv_ref, cos_ref, sin_ref, k_ref, v_ref, dep_ref, ctx_ref, ent_ref, q_s, kn_s, vn_s):
+def attend_kernel(len_ref, recv_ref, cos_ref, sin_ref, k_hbm, v_hbm, ctx_ref, ent_ref, q_s, kn_s, vn_s, k_ref, v_ref, sems):
+    copies = [
+        pltpu.make_async_copy(k_hbm, k_ref, sems.at[0]),
+        pltpu.make_async_copy(v_hbm, v_ref, sems.at[1]),
+    ]
+    for copy in copies:
+        copy.start()
     devices, steps, cols = recv_ref.shape
     cols -= 2 * k_ref.shape[1]
     slots, kv_cols = k_ref.shape
@@ -151,6 +194,8 @@
     col_old = lax.broadcasted_iota(jnp.int32, (rows, slots), 1)
     col_new = lax.broadcasted_iota(jnp.int32, (rows, fresh), 1)
     step_new = lax.rem(lax.broadcasted_iota(jnp.int32, (rows, fresh), 0), steps)
+    for copy in copies:
+        copy.wait()
     for k in range(kv_heads):
         lanes = slice(k * HEAD_WIDTH, (k + 1) * HEAD_WIDTH)
         for i in range(group):
@@ -197,36 +242,28 @@
     x_ref[...] = x_s[:, pl.ds(start, cols)]
 
 
-def fetch_kernel(at_ref, w_ref, dep_ref, there_ref, here_ref, sems):
-    chips, _, width = there_ref.shape
-    copies = []
-    for half, (core, out_ref) in enumerate(((1 - at_ref[1], there_ref), (at_ref[1], here_ref))):
-        for c in range(chips):
-            start = pl.multiple_of((2 * c + core) * width, width)
-            copy = pltpu.make_async_copy(
-                w_ref.at[:, pl.ds(start, width)], out_ref.at[c], sems.at[half * chips + c]
-            )
-            copy.start()
-            copies.append(copy)
-    for copy in copies:
-        copy.wait()
+def fetch_kernel(cross, at_ref, w_ref, dep_ref, out_ref, sems):
+    chips, _, width = out_ref.shape
+    core = 1 - at_ref[1] if cross else at_ref[1]
+    starts = [pl.multiple_of((2 * c + core) * width, width) for c in range(chips)]
+    run_copies([(w_ref.at[:, pl.ds(start, width)], out_ref.at[c]) for c, start in enumerate(starts)], sems)
 
 
 def out_kernel(cross, at_ref, x_ref, w_ref, rank_ref, up_ref, o_ref):
     width = o_ref.shape[2]
+    chips = w_ref.shape[0]
     core = 1 - at_ref[1] if cross else at_ref[1]
     x = x_ref[...]
     rank = rank_ref[...]
-    for c in range(o_ref.shape[0]):
-        lanes = pl.ds(pl.multiple_of((2 * c + core) * width, width), width)
-        o_ref[c] = nn(x, w_ref[c]) + SCALE * tn(rank, up_ref[:, lanes])
-
-
-def pair_kernel(at_ref, a_ref, b_ref, *outs):
-    chips = len(outs)
-    for k, out in enumerate(outs):
-        dest = lax.rem(at_ref[0] + k, chips)
-        out[...] = (a_ref[dest] + b_ref[dest]).astype(BF16)
+    for i in range(chips):
+        dest = lax.rem(at_ref[0] + i, chips)
+        lanes = pl.ds(pl.multiple_of((2 * dest + core) * width, width), width)
+        o_ref[i] = nn(x, w_ref[dest]) + SCALE * tn(rank, up_ref[:, lanes])
+
+
+def pair_kernel(a_ref, b_ref, *outs):
+    for i, out in enumerate(outs):
+        out[...] = (a_ref[i] + b_ref[i]).astype(BF16)
 
 
 def total_kernel(*refs):
@@ -281,14 +318,29 @@
     def exchange(v):
         return lax.all_to_all(v, both, 0, 0, tiled=True)
 
-    def gather(v):
-        line = stack([shift_chip(v, 2 * k) for k in range(lines)])
+    def gather(pieces, first, second):
+        line = stack(pieces, *first)
         across = swap_y(line)
+        across = pl.pallas_call(
+            pass_kernel,
+            out_shape=jax.ShapeDtypeStruct(across.shape, across.dtype),
+            in_specs=[VMEM, ANY],
+            compiler_params=PARAMS,
+        )(across, second(line))
         return line, across, swap_core(line), swap_core(across)
 
     x = tokens.reshape(rows, width)
-    down = adapter_down_maps[0]
-    gathered = gather(x)
+    pieces = [shift_chip(x, 2 * k) for k in range(lines)]
+    ups = exchange(
+        pl.pallas_call(
+            split_kernel,
+            out_shape=jax.ShapeDtypeStruct((devices, rank, cols), BF16),
+            in_specs=[VMEM, ANY],
+            compiler_params=PARAMS,
+        )(query_up_maps[0], pieces[1])
+    )
+    gathered = gather(pieces, (), lambda line: ups)
+    (down,) = ahead(ups, adapter_down_maps[0])
 
     index = jnp.arange(devices, dtype=jnp.int32)
     slot = jnp.sum(
@@ -298,53 +350,50 @@
     spread_mask = (jnp.repeat(index, rank)[:, None] == row_slot).astype(F32)
     own_mask = (row_slot == me).astype(F32)
 
-    ups = exchange(
-        pl.pallas_call(
-            split_kernel,
-            out_shape=jax.ShapeDtypeStruct((devices, rank, cols), BF16),
-            compiler_params=PARAMS,
-        )(query_up_maps[0])
-    )
     rank_send, rank_rest = pl.pallas_call(
         rank_kernel,
         out_shape=(
             jax.ShapeDtypeStruct((devices, rank, padded), BF16),
             jax.ShapeDtypeStruct((2 * rank, rows), BF16),
         ),
-        in_specs=[SMEM] + [VMEM] * 6 + [ANY],
-        compiler_params=PARAMS,
-    )(at, down, *gathered, own_mask, ups)
+        in_specs=[SMEM] + [VMEM] * 6,
+        compiler_params=PARAMS,
+    )(at, down, *gathered, own_mask)
     ranks = exchange(rank_send)
-    query = pl.pallas_call(
+    kv_width = key_value_weight.shape[1]
+    query, kv = pl.pallas_call(
         query_kernel,
-        out_shape=jax.ShapeDtypeStruct((rows, cols), F32),
-        in_specs=[SMEM, ANY] + [VMEM] * 4 + [ANY],
+        out_shape=(
+            jax.ShapeDtypeStruct((rows, cols), F32),
+            jax.ShapeDtypeStruct((rows, kv_width), F32),
+        ),
+        in_specs=[SMEM] + [ANY] * 4 + [VMEM] * 6 + [ANY],
         scratch_shapes=[
             pltpu.VMEM((devices, width, cols), BF16),
+            pltpu.VMEM(key_value_weight.shape, BF16),
+            pltpu.VMEM(key_up_maps.shape[1:], BF16),
+            pltpu.VMEM(value_up_maps.shape[1:], BF16),
             pltpu.SemaphoreType.DMA((devices,)),
+            pltpu.SemaphoreType.DMA((3,)),
         ],
         compiler_params=WIDE,
-    )(at, query_weight, *gathered, rank_send)
-    kv_width = key_value_weight.shape[1]
-    kv = pl.pallas_call(
-        kv_kernel,
-        out_shape=jax.ShapeDtypeStruct((rows, kv_width), F32),
-        compiler_params=PARAMS,
-    )(x, key_value_weight, rank_rest, key_up_maps[0], value_up_maps[0])
+    )(
+        at,
+        in_hbm(query_weight),
+        in_hbm(key_value_weight),
+        in_hbm(key_up_maps[0]),
+        in_hbm(value_up_maps[0]),
+        rank_rest,
+        x,
+        *gathered,
+        rank_send,
+    )
     to_rows = pl.pallas_call(
         finish_kernel,
         out_shape=jax.ShapeDtypeStruct((devices, steps, cols + kv_width), F32),
         compiler_params=PARAMS,
     )(query, kv, ranks, spread_mask, ups)
     arrived = exchange(to_rows)
-    fetched = pl.pallas_call(
-        fetch_kernel,
-        out_shape=[jax.ShapeDtypeStruct((chips, cols, width), BF16)] * 2,
-        in_specs=[SMEM, ANY, ANY],
-        out_specs=[ANY, ANY],
-        scratch_shapes=[pltpu.SemaphoreType.DMA((devices,))],
-        compiler_params=pltpu.CompilerParams(vmem_limit_bytes=36 * 1024 * 1024),
-    )(at, output_weight, to_rows)
 
     half_width = HEAD_WIDTH // 2
     frequency = ROPE_BASE ** (-2.0 * jnp.arange(half_width, dtype=F32) / HEAD_WIDTH)
@@ -361,16 +410,36 @@
             jax.ShapeDtypeStruct((heads * steps, HEAD_WIDTH), BF16),
             jax.ShapeDtypeStruct((steps, kv_width), F32),
         ),
-        in_specs=[SMEM] + [VMEM] * 5 + [ANY],
+        in_specs=[SMEM] + [VMEM] * 3 + [ANY] * 2,
         scratch_shapes=[
             pltpu.VMEM((group * steps, HEAD_WIDTH), F32),
             pltpu.VMEM((16, HEAD_WIDTH), F32),
             pltpu.VMEM((16, HEAD_WIDTH), F32),
+            pltpu.VMEM(cached_rotated_keys.shape[1:], BF16),
+            pltpu.VMEM(cached_values.shape[1:], BF16),
+            pltpu.SemaphoreType.DMA((2,)),
         ],
         compiler_params=PARAMS,
-    )(lengths, arrived, cosine, sine, cached_rotated_keys[0], cached_values[0], fetched[0])
+    )(lengths, arrived, cosine, sine, in_hbm(cached_rotated_keys[0]), in_hbm(cached_values[0]))
     entries = fresh.astype(BF16)[:, None, :]
 
+    def fetch(cross, after):
+        return pl.pallas_call(
+            functools.partial(fetch_kernel, cross),
+            out_shape=jax.ShapeDtypeStruct((chips, cols, width), BF16),
+            in_specs=[SMEM, ANY, ANY],
+            out_specs=ANY,
+            scratch_shapes=[pltpu.SemaphoreType.DMA((chips,))],
+            compiler_params=PARAMS,
+        )(at, in_hbm(output_weight), after)
+
+    fetched = [fetch(True, context)]
+
+    def fetch_rest(line):
+        fetched.append(fetch(False, line))
+        return fetched[1]
+
+    contexts = gather([shift_chip(context, 2 * k) for k in range(lines)], fetched[:1], fetch_rest)
     lhs, out_rank = pl.pallas_call(
         lower_kernel,
         out_shape=(
@@ -383,7 +452,7 @@
             pltpu.VMEM((rows, heads * HEAD_WIDTH), BF16),
         ],
         compiler_params=PARAMS,
-    )(at, result_lowering_factors[0], own_mask, *gather(context))
+    )(at, result_lowering_factors[0], own_mask, *contexts)
 
     def out_half(cross):
         return pl.pallas_call(
@@ -397,9 +466,8 @@
     chip_totals = pl.pallas_call(
         pair_kernel,
         out_shape=[jax.ShapeDtypeStruct((rows, width), BF16)] * chips,
-        in_specs=[SMEM, VMEM, VMEM],
-        compiler_params=PARAMS,
-    )(at, out_half(False), received)
+        compiler_params=PARAMS,
+    )(out_half(False), received)
     final = [shift_chip(v, k) for k, v in enumerate(chip_totals)]
     attended = pl.pallas_call(
         total_kernel,

time: 113 us -> 111 us (0.982)
  local copies, waits for them, and re-layouts: 17.3 us -> 2.08 us
  Pallas kernels: 26.1 us -> 33.1 us
  waiting for transfers between devices: 28.1 us -> 32.4 us
  starting transfers between devices: 37.3 us -> 39.3 us
    unnamed x32 -> x10, local copies, waits for them, and re-layouts: 17 us -> 1.81 us
    pallas_call x5 -> x8, Pallas kernels: 13.9 us -> 20.1 us  [the longest x1 10.6 us: body(): pl.pallas_call(query_kernel, out_shape=(jax.ShapeDtypeStruct((rows, cols)...]
    ppermute x13, waiting for transfers between devices: 14.6 us -> 17.1 us  [shift_chip(): return lax.ppermute(v, 'tp', [(i, (i + k) % chips) for i in range(chips)])]
    ppermute x2, waiting for transfers between devices: 3.56 us -> 5.45 us  [swap_y(): return lax.ppermute(v, 'tp', [(i, i ^ 1) for i in range(chips)])]
    all_to_all x3, starting transfers between devices: 13 us -> 14.4 us  [exchange(): return lax.all_to_all(v, both, 0, 0, tiled=True)]
    ppermute x5, waiting for transfers between devices: 2.35 us -> 1.02 us  [swap_core(): return lax.ppermute(v, 'sub', [(0, 1), (1, 0)])]
    all_to_all x3, waiting for transfers between devices: 7.52 us -> 8.8 us  [exchange(): return lax.all_to_all(v, both, 0, 0, tiled=True)]
    pallas_call x1, Pallas kernels: 1.58 us -> 2.81 us  [body(): pl.pallas_call(attend_kernel, out_shape=(jax.ShapeDtypeStruct((heads * st...]
  transfers between devices with their start and end apart: 23 -> 23, of which waited for: 15 -> 9; matrix products, arithmetic and copies ran while one was open for 2% -> 2% of each run, Pallas kernels for 15% -> 20%
where the time goes in v6:
time: 111 us; the launch traced here: 110 us
  starting transfers between devices  39.3 us (35%)
  Pallas kernels  33.1 us (30%)
  waiting for transfers between devices  32.4 us (29%)
  local copies, waits for them, and re-layouts  2.08 us (2%)
  other arithmetic  1.83 us (2%)
  between operations  1.53 us (1%)
    ppermute x13, starting transfers between devices, shift_chip(): return lax.ppermute(v, 'tp', [(i, (i + k) % chips) for i in range(chips)])  21.4 us
    ppermute x13, waiting for transfers between devices, shift_chip(): return lax.ppermute(v, 'tp', [(i, (i + k) % chips) for i in range(chips)])  17.1 us
    all_to_all x3, starting transfers between devices, exchange(): return lax.all_to_all(v, both, 0, 0, tiled=True)  14.4 us
    pallas_call x1, Pallas kernels, body(): pl.pallas_call(query_kernel, out_shape=(jax.ShapeDtypeStruct((rows, cols)...  10.6 us
    all_to_all x3, waiting for transfers between devices, exchange(): return lax.all_to_all(v, both, 0, 0, tiled=True)  8.8 us
    pallas_call x2, Pallas kernels, fetch(): pl.pallas_call(functools.partial(fetch_kernel, cross), out_shape=jax.Shap...  8.1 us
    ppermute x2, waiting for transfers between devices, swap_y(): return lax.ppermute(v, 'tp', [(i, i ^ 1) for i in range(chips)])  5.45 us
    pallas_call x2, Pallas kernels, out_half(): pl.pallas_call(functools.partial(out_kernel, cross), out_shape=jax.ShapeD...  4.54 us
  transfers between devices with their start and end apart: 23, of which 9 were waited for; matrix products, arithmetic and copies ran while one was open for 2% of the time, Pallas kernels for 20%

profile of v6, /device:TPU:0, one launch (start us, length us, event | category | flops | bytes accessed | tf_op | source)
XLA Modules:
  0.0 110.3 jit_solution(15192372921663504726)
XLA Ops:
  0.6 0.0 copy-start.2
  0.6 3.1 %collective-permute-start = (bf16[32,1024]{1,0:T(8,128)(2,1)}, bf16[32,1024]{1,0:T(8,128)(2,1)S(1)}, u32[]{:S(2)}, u32[]{:S(2)}) collective-permute-start(bf16[32,1024]{1,0:T(8,128)(2,1)} %bitcast.20), channel_id=1, source_target_pairs={{0,4},{2,6},{4,8},{6,10},{8,12},{10,14},{12,0},{14,2},{1,5},{3,7},... | collective-permute-start | bytes 196616 | tf_op jit(solution)/shard_map/ppermute | solution.py:316
  3.7 4.5 %collective-permute-done.dep_ref.refs_1_ = bf16[32,1024]{1,0:T(8,128)(2,1)S(1)} collective-permute-done((bf16[32,1024]{1,0:T(8,128)(2,1)}, bf16[32,1024]{1,0:T(8,128)(2,1)S(1)}, u32[]{:S(2)}, u32[]{:S(2)}) %collective-permute-start) | collective-permute-done | bytes 65568 | tf_op jit(solution)/shard_map/ppermute | solution.py:316
  8.2 0.9 copy-done.3
  9.2 0.7 shard_map.158
  9.9 4.3 %all-to-all-start = ((bf16[16,16,512]{2,1,0:T(8,128)(2,1)}), bf16[16,16,512]{2,1,0:T(8,128)(2,1)S(1)}, u32[]{:S(2)}, u32[]{:S(2)}) async-start(bf16[16,16,512]{2,1,0:T(8,128)(2,1)} %shard_map.158), calls=%async_computation | async-start | bytes 524288 | tf_op jit(solution)/shard_map/all_to_all | solution.py:319
  14.2 3.7 %collective-permute-start.2 = (bf16[32,1024]{1,0:T(8,128)(2,1)}, bf16[32,1024]{1,0:T(8,128)(2,1)S(1)}, u32[]{:S(2)}, u32[]{:S(2)}) collective-permute-start(bf16[32,1024]{1,0:T(8,128)(2,1)} %bitcast.21), channel_id=1, source_target_pairs={{0,12},{2,14},{4,0},{6,2},{8,4},{10,6},{12,8},{14,10},{1,13},{3,15... | collective-permute-start | bytes 196616 | tf_op jit(solution)/shard_map/ppermute | solution.py:316
  18.0 0.0 collective-permute-start.1
  18.0 4.7 %collective-permute-done.2.refs_3_ = bf16[32,1024]{1,0:T(8,128)(2,1)S(1)} collective-permute-done((bf16[32,1024]{1,0:T(8,128)(2,1)}, bf16[32,1024]{1,0:T(8,128)(2,1)S(1)}, u32[]{:S(2)}, u32[]{:S(2)}) %collective-permute-start.2) | collective-permute-done | bytes 65568 | tf_op jit(solution)/shard_map/ppermute | solution.py:316
  22.6 5.5 %collective-permute-done.1.refs_2_ = bf16[32,1024]{1,0:T(8,128)(2,1)S(1)} collective-permute-done((bf16[32,1024]{1,0:T(8,128)(2,1)}, bf16[32,1024]{1,0:T(8,128)(2,1)S(1)}, u32[]{:S(2)}, u32[]{:S(2)}) %collective-permute-start.1) | collective-permute-done | bytes 65568 | tf_op jit(solution)/shard_map/ppermute | solution.py:316
  28.1 0.8 copy-done.1
  28.9 1.5 %collective-permute-start.3 = (bf16[4,32,1024]{2,1,0:T(8,128)(2,1)S(1)}, bf16[4,32,1024]{2,1,0:T(8,128)(2,1)S(1)}, u32[]{:S(2)}, u32[]{:S(2)}) collective-permute-start(bf16[4,32,1024]{2,1,0:T(8,128)(2,1)S(1)} %shard_map.160.a_ref), channel_id=1, source_target_pairs={{0,2},{2,0},{4,6},{6,4},{8,10},{10,8},{12,14},{14,12},{1,3},{3,1},... | collective-permute-start | bytes 786440 | tf_op jit(solution)/shard_map/ppermute | solution.py:311
  30.5 0.9 select_reduce_fusion
  31.3 0.1 eq.53
  31.4 0.0 collective-permute-start.4
  31.4 5.4 %collective-permute-done.3.x_ref = bf16[4,32,1024]{2,1,0:T(8,128)(2,1)S(1)} collective-permute-done((bf16[4,32,1024]{2,1,0:T(8,128)(2,1)S(1)}, bf16[4,32,1024]{2,1,0:T(8,128)(2,1)S(1)}, u32[]{:S(2)}, u32[]{:S(2)}) %collective-permute-start.3) | collective-permute-done | bytes 262176 | tf_op jit(solution)/shard_map/ppermute | solution.py:311
  36.9 0.0 all-to-all-done.dep_ref.up_ref
  36.9 0.1 collective-permute-start.5
  37.0 0.1 convert_element_type.19.own_ref
  37.1 0.1 eq.51
  37.2 0.1 pad_add_fusion.at_ref
  37.2 1.4 %shard_map.159.d_ref = bf16[48,16384]{1,0:T(8,128)(2,1)S(1)} custom-call(bf16[16,16,512]{2,1,0:T(8,128)(2,1)S(1)} %all-to-all-done.dep_ref.up_ref, bf16[48,16384]{1,0:T(8,128)(2,1)} %bitcast.29), custom_call_target="tpu_custom_call" | custom-call | tf_op jit(solution)/shard_map/pallas_call | solution.py:135
  38.7 0.0 collective-permute-done.4.c_ref
  38.7 1.7 %shard_map.162 = (bf16[16,16,128]{2,1,0:T(8,128)(2,1)}, bf16[32,32]{1,0:T(8,128)(2,1)S(1)}) custom-call(s32[2]{0:T(128)S(1)} %pad_add_fusion.at_ref, bf16[48,16384]{1,0:T(8,128)(2,1)S(1)} %shard_map.159.d_ref, bf16[4,32,1024]{2,1,0:T(8,128)(2,1)S(1)} %shard_map.160.a_ref, bf16[4,32,1024]{2,1,0:T(8,128)(2,1)S(1)} %shard_map.161.b_ref, ...), custom_call_target="tpu_custom_call" | custom-call | tf_op jit(solution)/shard_map/pallas_call | solution.py:353
  40.4 4.0 %all-to-all-start.1 = ((bf16[16,16,128]{2,1,0:T(8,128)(2,1)}), bf16[16,16,128]{2,1,0:T(8,128)(2,1)S(1)}, u32[]{:S(2)}, u32[]{:S(2)}) async-start(bf16[16,16,128]{2,1,0:T(8,128)(2,1)} %get-tuple-element.19.refs_0_), calls=%async_computation.1 | async-start | bytes 131072 | tf_op jit(solution)/shard_map/all_to_all | solution.py:319
  44.5 0.1 compare_convert_fusion.mask_ref
  45.2 10.6 %shard_map.163 = (f32[32,512]{1,0:T(8,128)S(1)}, f32[32,1024]{1,0:T(8,128)S(1)}) custom-call(s32[2]{0:T(128)S(1)} %pad_add_fusion.at_ref, bf16[16384,512]{1,0:T(8,128)(2,1)} %w_ref.3, bf16[1024,1024]{1,0:T(8,128)(2,1)} %kw_ref.1, bf16[16,512]{1,0:T(8,128)(2,1)} %bitcast.33, bf16[16,512]{1,0:T(8,128)(2,1)} %bitcast.34, ...), custom_call_target="tpu_custom_call" | custom-call | tf_op jit(solution)/shard_map/pallas_call | solution.py:364
  55.8 0.9 shard_map.164
  56.7 6.0 %all-to-all-start.2 = ((f32[16,2,1536]{2,1,0:T(2,128)}), f32[16,2,1536]{2,1,0:T(2,128)S(1)}, u32[]{:S(2)}, u32[]{:S(2)}) async-start(f32[16,2,1536]{2,1,0:T(2,128)} %shard_map.164), calls=%async_computation.2 | async-start | bytes 393216 | tf_op jit(solution)/shard_map/all_to_all | solution.py:319
  62.7 0.1 fusion
  62.8 0.1 pad_maximum_fusion
  62.9 8.8 %all-to-all-done.2.recv_ref = f32[16,2,1536]{2,1,0:T(2,128)S(1)} async-done(((f32[16,2,1536]{2,1,0:T(2,128)}), f32[16,2,1536]{2,1,0:T(2,128)S(1)}, u32[]{:S(2)}, u32[]{:S(2)}) %all-to-all-start.2) | async-done | bytes 196640 | tf_op jit(solution)/shard_map/all_to_all | solution.py:319
  71.7 2.8 %shard_map.165 = (bf16[128,128]{1,0:T(8,128)(2,1)S(1)}, f32[2,1024]{1,0:T(2,128)S(1)}) custom-call(s32[1]{0:T(128)} %copy.18.len_ref, f32[16,2,1536]{2,1,0:T(2,128)S(1)} %all-to-all-done.2.recv_ref, f32[32,128]{1,0:T(8,128)S(1)} %bitcast.27, f32[32,128]{1,0:T(8,128)S(1)} %bitcast.28, bf16[512,512]{1,0:T(8,128)(2,1)} %bitcast.30, bf16[512,512]{1,0:T(8,128)(2,1)} %bitcast.31), custom_call_target="tpu_custom_call" | custom-call | tf_op jit(solution)/shard_map/pallas_call | solution.py:407
  74.5 0.9 collective-permute-start.8
  75.4 1.9 %collective-permute-start.6 = (bf16[128,128]{1,0:T(8,128)(2,1)S(1)}, bf16[128,128]{1,0:T(8,128)(2,1)S(1)}, u32[]{:S(2)}, u32[]{:S(2)}) collective-permute-start(bf16[128,128]{1,0:T(8,128)(2,1)S(1)} %get-tuple-element.22.dep_ref.refs_0_), channel_id=1, source_target_pairs={{0,4},{2,6},{4,8},{6,10},{8,12},{10,14},{12,0},{14,2},{1,5},{3,7},... | collective-permute-start | bytes 98312 | tf_op jit(solution)/shard_map/ppermute | solution.py:316
  77.3 4.0 %shard_map.166.refs_4_.w_ref = bf16[8,512,1024]{2,1,0:T(8,128)(2,1)S(1)} custom-call(s32[2]{0:T(128)S(1)} %pad_add_fusion.at_ref, bf16[512,16384]{1,0:T(8,128)(2,1)} %w_ref.5, bf16[128,128]{1,0:T(8,128)(2,1)S(1)} %get-tuple-element.22.dep_ref.refs_0_), custom_call_target="tpu_custom_call" | custom-call | tf_op jit(solution)/shard_map/pallas_call | solution.py:427
  81.4 0.9 collective-permute-start.9
  82.4 4.0 %shard_map.168.dep_ref.w_ref = bf16[8,512,1024]{2,1,0:T(8,128)(2,1)S(1)} custom-call(s32[2]{0:T(128)S(1)} %pad_add_fusion.at_ref, bf16[512,16384]{1,0:T(8,128)(2,1)} %w_ref.5, bf16[4,128,128]{2,1,0:T(8,128)(2,1)S(1)} %shard_map.167.dep_ref.a_ref), custom_call_target="tpu_custom_call" | custom-call | tf_op jit(solution)/shard_map/pallas_call | solution.py:427
  86.4 0.0 copy-start.4
  86.4 0.0 copy-start
  86.4 0.0 collective-permute-done.9.x_ref
  86.5 0.6 collective-permute-start.11
  87.0 1.0 collective-permute-done.11.d_ref
  88.0 1.5 %shard_map.170 = (bf16[32,512]{1,0:T(8,128)(2,1)S(1)}, bf16[16,32]{1,0:T(8,128)(2,1)S(1)}) custom-call(s32[2]{0:T(128)S(1)} %pad_add_fusion.at_ref, bf16[16,8192]{1,0:T(8,128)(2,1)S(1)} %bitcast.26, f32[1,32]{1,0:T(1,128)S(1)} %convert_element_type.19.own_ref, bf16[4,128,128]{2,1,0:T(8,128)(2,1)S(1)} %shard_map.167.dep_ref.a_ref, ...), custom_call_target="tpu_custom_call" | custom-call | tf_op jit(solution)/shard_map/pallas_call | solution.py:443
  89.5 0.0 copy-done
  89.5 2.3 %shard_map.172 = f32[8,32,1024]{2,1,0:T(8,128)S(1)} custom-call(s32[2]{0:T(128)S(1)} %pad_add_fusion.at_ref, bf16[32,512]{1,0:T(8,128)(2,1)S(1)} %get-tuple-element.23.x_ref, bf16[8,512,1024]{2,1,0:T(8,128)(2,1)S(1)} %shard_map.166.refs_4_.w_ref, bf16[16,32]{1,0:T(8,128)(2,1)S(1)} %get-tuple-element.24.rank_ref, bf16[16,16384]{1,0:T(8,128)(2,1)S(1)} %bitcast.18), custom_call_target="tpu_custom_call" | custom-call | tf_op jit(solution)/shard_map/pallas_call | solution.py:458
  91.8 0.4 collective-permute-start.12
  92.2 2.3 %shard_map.171.a_ref = f32[8,32,1024]{2,1,0:T(8,128)S(1)} custom-call(s32[2]{0:T(128)S(1)} %pad_add_fusion.at_ref, bf16[32,512]{1,0:T(8,128)(2,1)S(1)} %get-tuple-element.23.x_ref, bf16[8,512,1024]{2,1,0:T(8,128)(2,1)S(1)} %shard_map.168.dep_ref.w_ref, bf16[16,32]{1,0:T(8,128)(2,1)S(1)} %get-tuple-element.24.rank_ref, bf16[16,16384]{1,0:T(8,128)(2,1)S(1)} %bitcast.19), custom_call_target="tpu_custom_call" | custom-call | tf_op jit(solution)/shard_map/pallas_call | solution.py:458
  94.4 0.0 collective-permute-done.12.b_ref
  94.5 0.2 shard_map.173
  94.6 1.2 %collective-permute-start.13 = (bf16[32,1024]{1,0:T(8,128)(2,1)S(1)}, bf16[32,1024]{1,0:T(8,128)(2,1)S(1)}, u32[]{:S(2)}, u32[]{:S(2)}) collective-permute-start(bf16[32,1024]{1,0:T(8,128)(2,1)S(1)} %get-tuple-element.26), channel_id=1, source_target_pairs={{0,2},{2,4},{4,6},{6,8},{8,10},{10,12},{12,14},{14,0},{1,3},{3,5},... | collective-permute-start | bytes 196616 | tf_op jit(solution)/shard_map/ppermute | solution.py:316
  95.9 1.6 %collective-permute-start.14 = (bf16[32,1024]{1,0:T(8,128)(2,1)S(1)}, bf16[32,1024]{1,0:T(8,128)(2,1)S(1)}, u32[]{:S(2)}, u32[]{:S(2)}) collective-permute-start(bf16[32,1024]{1,0:T(8,128)(2,1)S(1)} %get-tuple-element.27), channel_id=1, source_target_pairs={{0,4},{2,6},{4,8},{6,10},{8,12},{10,14},{12,0},{14,2},{1,5},{3,7},... | collective-permute-start | bytes 196616 | tf_op jit(solution)/shard_map/ppermute | solution.py:316
  97.5 1.7 %collective-permute-start.15 = (bf16[32,1024]{1,0:T(8,128)(2,1)S(1)}, bf16[32,1024]{1,0:T(8,128)(2,1)S(1)}, u32[]{:S(2)}, u32[]{:S(2)}) collective-permute-start(bf16[32,1024]{1,0:T(8,128)(2,1)S(1)} %get-tuple-element.28), channel_id=1, source_target_pairs={{0,6},{2,8},{4,10},{6,12},{8,14},{10,0},{12,2},{14,4},{1,7},{3,9},... | collective-permute-start | bytes 196616 | tf_op jit(solution)/shard_map/ppermute | solution.py:316
  99.1 2.6 %collective-permute-start.16 = (bf16[32,1024]{1,0:T(8,128)(2,1)S(1)}, bf16[32,1024]{1,0:T(8,128)(2,1)S(1)}, u32[]{:S(2)}, u32[]{:S(2)}) collective-permute-start(bf16[32,1024]{1,0:T(8,128)(2,1)S(1)} %get-tuple-element.29), channel_id=1, source_target_pairs={{0,8},{2,10},{4,12},{6,14},{8,0},{10,2},{12,4},{14,6},{1,9},{3,11}... | collective-permute-start | bytes 196616 | tf_op jit(solution)/shard_map/ppermute | solution.py:316
  101.7 0.5 collective-permute-start.17
  102.2 2.6 %collective-permute-start.18 = (bf16[32,1024]{1,0:T(8,128)(2,1)S(1)}, bf16[32,1024]{1,0:T(8,128)(2,1)S(1)}, u32[]{:S(2)}, u32[]{:S(2)}) collective-permute-start(bf16[32,1024]{1,0:T(8,128)(2,1)S(1)} %get-tuple-element.31), channel_id=1, source_target_pairs={{0,12},{2,14},{4,0},{6,2},{8,4},{10,6},{12,8},{14,10},{1,13},{3,15... | collective-permute-start | bytes 196616 | tf_op jit(solution)/shard_map/ppermute | solution.py:316
  104.8 1.6 %collective-permute-start.19 = (bf16[32,1024]{1,0:T(8,128)(2,1)S(1)}, bf16[32,1024]{1,0:T(8,128)(2,1)S(1)}, u32[]{:S(2)}, u32[]{:S(2)}) collective-permute-start(bf16[32,1024]{1,0:T(8,128)(2,1)S(1)} %get-tuple-element.32), channel_id=1, source_target_pairs={{0,14},{2,0},{4,2},{6,4},{8,6},{10,8},{12,10},{14,12},{1,15},{3,1}... | collective-permute-start | bytes 196616 | tf_op jit(solution)/shard_map/ppermute | solution.py:316
  106.5 0.6 convert_bitcast_fusion
  107.0 0.5 collective-permute-done.15.refs_3_
  107.6 0.4 collective-permute-done.16.refs_4_
  107.9 1.6 %collective-permute-done.17.refs_5_ = bf16[32,1024]{1,0:T(8,128)(2,1)S(1)} collective-permute-done((bf16[32,1024]{1,0:T(8,128)(2,1)S(1)}, bf16[32,1024]{1,0:T(8,128)(2,1)S(1)}, u32[]{:S(2)}, u32[]{:S(2)}) %collective-permute-start.17) | collective-permute-done | bytes 65568 | tf_op jit(solution)/shard_map/ppermute | solution.py:316
  109.5 0.0 collective-permute-done.18.refs_6_
  109.6 0.0 collective-permute-done.19.refs_7_
  109.6 0.7 shard_map.174
  (26 shorter events, 0.1 us)
Async XLA Ops:
  0.6 44.6 %copy-start.2 = (bf16[2,16,1024]{2,1,0:T(8,128)(2,1)S(1)}, bf16[2,16,1024]{2,1,0:T(8,128)(2,1)}, u32[]{:S(2)}) copy-start(bf16[2,16,1024]{2,1,0:T(8,128)(2,1)} %param.15) | copy-start | bytes 196612
  0.6 7.6 %collective-permute-start = (bf16[32,1024]{1,0:T(8,128)(2,1)}, bf16[32,1024]{1,0:T(8,128)(2,1)S(1)}, u32[]{:S(2)}, u32[]{:S(2)}) collective-permute-start(bf16[32,1024]{1,0:T(8,128)(2,1)} %bitcast.20), channel_id=1, source_target_pairs={{0,4},{2,6},{4,8},{6,10},{8,12},{10,14},{12,0},{14,2},{1,5},{3,7},... | collective-permute-start | bytes 196616 | tf_op jit(solution)/shard_map/ppermute | solution.py:316
  8.2 1.0 copy-start.3
  9.9 27.0 %all-to-all-start = ((bf16[16,16,512]{2,1,0:T(8,128)(2,1)}), bf16[16,16,512]{2,1,0:T(8,128)(2,1)S(1)}, u32[]{:S(2)}, u32[]{:S(2)}) async-start(bf16[16,16,512]{2,1,0:T(8,128)(2,1)} %shard_map.158), calls=%async_computation | async-start | bytes 524288 | tf_op jit(solution)/shard_map/all_to_all | solution.py:319
  14.2 8.4 %collective-permute-start.2 = (bf16[32,1024]{1,0:T(8,128)(2,1)}, bf16[32,1024]{1,0:T(8,128)(2,1)S(1)}, u32[]{:S(2)}, u32[]{:S(2)}) collective-permute-start(bf16[32,1024]{1,0:T(8,128)(2,1)} %bitcast.21), channel_id=1, source_target_pairs={{0,12},{2,14},{4,0},{6,2},{8,4},{10,6},{12,8},{14,10},{1,13},{3,15... | collective-permute-start | bytes 196616 | tf_op jit(solution)/shard_map/ppermute | solution.py:316
  18.0 10.1 %collective-permute-start.1 = (bf16[32,1024]{1,0:T(8,128)(2,1)}, bf16[32,1024]{1,0:T(8,128)(2,1)S(1)}, u32[]{:S(2)}, u32[]{:S(2)}) collective-permute-start(bf16[32,1024]{1,0:T(8,128)(2,1)} %bitcast.22), channel_id=1, source_target_pairs={{0,8},{2,10},{4,12},{6,14},{8,0},{10,2},{12,4},{14,6},{1,9},{3,11}... | collective-permute-start | bytes 196616 | tf_op jit(solution)/shard_map/ppermute | solution.py:316
  28.1 0.8 copy-start.1
  28.9 7.9 %collective-permute-start.3 = (bf16[4,32,1024]{2,1,0:T(8,128)(2,1)S(1)}, bf16[4,32,1024]{2,1,0:T(8,128)(2,1)S(1)}, u32[]{:S(2)}, u32[]{:S(2)}) collective-permute-start(bf16[4,32,1024]{2,1,0:T(8,128)(2,1)S(1)} %shard_map.160.a_ref), channel_id=1, source_target_pairs={{0,2},{2,0},{4,6},{6,4},{8,10},{10,8},{12,14},{14,12},{1,3},{3,1},... | collective-permute-start | bytes 786440 | tf_op jit(solution)/shard_map/ppermute | solution.py:311
  31.4 7.2 %collective-permute-start.4 = (bf16[4,32,1024]{2,1,0:T(8,128)(2,1)S(1)}, bf16[4,32,1024]{2,1,0:T(8,128)(2,1)S(1)}, u32[]{:S(2)}, u32[]{:S(2)}) collective-permute-start(bf16[4,32,1024]{2,1,0:T(8,128)(2,1)S(1)} %shard_map.160.a_ref), channel_id=1, source_target_pairs={{0,1},{1,0},{2,3},{3,2},{4,5},{5,4},{6,7},{7,6},{8,9},{9,8},{10,11... | collective-permute-start | bytes 786440 | tf_op jit(solution)/shard_map/ppermute | solution.py:308
  36.9 1.8 %collective-permute-start.5 = (bf16[4,32,1024]{2,1,0:T(8,128)(2,1)S(1)}, bf16[4,32,1024]{2,1,0:T(8,128)(2,1)S(1)}, u32[]{:S(2)}, u32[]{:S(2)}) collective-permute-start(bf16[4,32,1024]{2,1,0:T(8,128)(2,1)S(1)} %shard_map.161.b_ref), channel_id=1, source_target_pairs={{0,1},{1,0},{2,3},{3,2},{4,5},{5,4},{6,7},{7,6},{8,9},{9,8},{10,11... | collective-permute-start | bytes 786440 | tf_op jit(solution)/shard_map/ppermute | solution.py:308
  40.4 15.4 %all-to-all-start.1 = ((bf16[16,16,128]{2,1,0:T(8,128)(2,1)}), bf16[16,16,128]{2,1,0:T(8,128)(2,1)S(1)}, u32[]{:S(2)}, u32[]{:S(2)}) async-start(bf16[16,16,128]{2,1,0:T(8,128)(2,1)} %get-tuple-element.19.refs_0_), calls=%async_computation.1 | async-start | bytes 131072 | tf_op jit(solution)/shard_map/all_to_all | solution.py:319
  56.7 15.0 %all-to-all-start.2 = ((f32[16,2,1536]{2,1,0:T(2,128)}), f32[16,2,1536]{2,1,0:T(2,128)S(1)}, u32[]{:S(2)}, u32[]{:S(2)}) async-start(f32[16,2,1536]{2,1,0:T(2,128)} %shard_map.164), calls=%async_computation.2 | async-start | bytes 393216 | tf_op jit(solution)/shard_map/all_to_all | solution.py:319
  74.5 6.8 %collective-permute-start.8 = (bf16[128,128]{1,0:T(8,128)(2,1)S(1)}, bf16[128,128]{1,0:T(8,128)(2,1)S(1)}, u32[]{:S(2)}, u32[]{:S(2)}) collective-permute-start(bf16[128,128]{1,0:T(8,128)(2,1)S(1)} %get-tuple-element.22.dep_ref.refs_0_), channel_id=1, source_target_pairs={{0,12},{2,14},{4,0},{6,2},{8,4},{10,6},{12,8},{14,10},{1,13},{3,15... | collective-permute-start | bytes 98312 | tf_op jit(solution)/shard_map/ppermute | solution.py:316
  75.4 6.0 %collective-permute-start.7 = (bf16[128,128]{1,0:T(8,128)(2,1)S(1)}, bf16[128,128]{1,0:T(8,128)(2,1)S(1)}, u32[]{:S(2)}, u32[]{:S(2)}) collective-permute-start(bf16[128,128]{1,0:T(8,128)(2,1)S(1)} %get-tuple-element.22.dep_ref.refs_0_), channel_id=1, source_target_pairs={{0,8},{2,10},{4,12},{6,14},{8,0},{10,2},{12,4},{14,6},{1,9},{3,11}... | collective-permute-start | bytes 98312 | tf_op jit(solution)/shard_map/ppermute | solution.py:316
  75.4 6.0 %collective-permute-start.6 = (bf16[128,128]{1,0:T(8,128)(2,1)S(1)}, bf16[128,128]{1,0:T(8,128)(2,1)S(1)}, u32[]{:S(2)}, u32[]{:S(2)}) collective-permute-start(bf16[128,128]{1,0:T(8,128)(2,1)S(1)} %get-tuple-element.22.dep_ref.refs_0_), channel_id=1, source_target_pairs={{0,4},{2,6},{4,8},{6,10},{8,12},{10,14},{12,0},{14,2},{1,5},{3,7},... | collective-permute-start | bytes 98312 | tf_op jit(solution)/shard_map/ppermute | solution.py:316
  81.4 5.0 %collective-permute-start.9 = (bf16[4,128,128]{2,1,0:T(8,128)(2,1)S(1)}, bf16[4,128,128]{2,1,0:T(8,128)(2,1)S(1)}, u32[]{:S(2)}, u32[]{:S(2)}) collective-permute-start(bf16[4,128,128]{2,1,0:T(8,128)(2,1)S(1)} %shard_map.167.dep_ref.a_ref), channel_id=1, source_target_pairs={{0,2},{2,0},{4,6},{6,4},{8,10},{10,8},{12,14},{14,12},{1,3},{3,1},... | collective-permute-start | bytes 393224 | tf_op jit(solution)/shard_map/ppermute | solution.py:311
  82.4 4.7 %collective-permute-start.10 = (bf16[4,128,128]{2,1,0:T(8,128)(2,1)S(1)}, bf16[4,128,128]{2,1,0:T(8,128)(2,1)S(1)}, u32[]{:S(2)}, u32[]{:S(2)}) collective-permute-start(bf16[4,128,128]{2,1,0:T(8,128)(2,1)S(1)} %shard_map.167.dep_ref.a_ref), channel_id=1, source_target_pairs={{0,1},{1,0},{2,3},{3,2},{4,5},{5,4},{6,7},{7,6},{8,9},{9,8},{10,11... | collective-permute-start | bytes 393224 | tf_op jit(solution)/shard_map/ppermute | solution.py:308
  86.4 1.6 %copy-start.4 = (bf16[1,16,8192]{2,1,0:T(8,128)(2,1)S(1)}, bf16[1,16,8192]{2,1,0:T(8,128)(2,1)}, u32[]{:S(2)}) copy-start(bf16[1,16,8192]{2,1,0:T(8,128)(2,1)} %param.28) | copy-start | bytes 786436
  86.4 3.1 %copy-start = (bf16[1,16,16384]{2,1,0:T(8,128)(2,1)S(1)}, bf16[1,16,16384]{2,1,0:T(8,128)(2,1)}, u32[]{:S(2)}) copy-start(bf16[1,16,16384]{2,1,0:T(8,128)(2,1)} %param.29) | copy-start | bytes 1572868
  86.5 1.6 %collective-permute-start.11 = (bf16[4,128,128]{2,1,0:T(8,128)(2,1)S(1)}, bf16[4,128,128]{2,1,0:T(8,128)(2,1)S(1)}, u32[]{:S(2)}, u32[]{:S(2)}) collective-permute-start(bf16[4,128,128]{2,1,0:T(8,128)(2,1)S(1)} %shard_map.169.b_ref), channel_id=1, source_target_pairs={{0,1},{1,0},{2,3},{3,2},{4,5},{5,4},{6,7},{7,6},{8,9},{9,8},{10,11... | collective-permute-start | bytes 393224 | tf_op jit(solution)/shard_map/ppermute | solution.py:308
  91.8 2.7 %collective-permute-start.12 = (f32[8,32,1024]{2,1,0:T(8,128)S(1)}, f32[8,32,1024]{2,1,0:T(8,128)S(1)}, u32[]{:S(2)}, u32[]{:S(2)}) collective-permute-start(f32[8,32,1024]{2,1,0:T(8,128)S(1)} %shard_map.172), channel_id=1, source_target_pairs={{0,1},{1,0},{2,3},{3,2},{4,5},{5,4},{6,7},{7,6},{8,9},{9,8},{10,11... | collective-permute-start | bytes 3145736 | tf_op jit(solution)/shard_map/ppermute | solution.py:308
  94.6 7.6 %collective-permute-start.13 = (bf16[32,1024]{1,0:T(8,128)(2,1)S(1)}, bf16[32,1024]{1,0:T(8,128)(2,1)S(1)}, u32[]{:S(2)}, u32[]{:S(2)}) collective-permute-start(bf16[32,1024]{1,0:T(8,128)(2,1)S(1)} %get-tuple-element.26), channel_id=1, source_target_pairs={{0,2},{2,4},{4,6},{6,8},{8,10},{10,12},{12,14},{14,0},{1,3},{3,5},... | collective-permute-start | bytes 196616 | tf_op jit(solution)/shard_map/ppermute | solution.py:316
  95.9 9.0 %collective-permute-start.14 = (bf16[32,1024]{1,0:T(8,128)(2,1)S(1)}, bf16[32,1024]{1,0:T(8,128)(2,1)S(1)}, u32[]{:S(2)}, u32[]{:S(2)}) collective-permute-start(bf16[32,1024]{1,0:T(8,128)(2,1)S(1)} %get-tuple-element.27), channel_id=1, source_target_pairs={{0,4},{2,6},{4,8},{6,10},{8,12},{10,14},{12,0},{14,2},{1,5},{3,7},... | collective-permute-start | bytes 196616 | tf_op jit(solution)/shard_map/ppermute | solution.py:316
  97.5 10.1 %collective-permute-start.15 = (bf16[32,1024]{1,0:T(8,128)(2,1)S(1)}, bf16[32,1024]{1,0:T(8,128)(2,1)S(1)}, u32[]{:S(2)}, u32[]{:S(2)}) collective-permute-start(bf16[32,1024]{1,0:T(8,128)(2,1)S(1)} %get-tuple-element.28), channel_id=1, source_target_pairs={{0,6},{2,8},{4,10},{6,12},{8,14},{10,0},{12,2},{14,4},{1,7},{3,9},... | collective-permute-start | bytes 196616 | tf_op jit(solution)/shard_map/ppermute | solution.py:316
  99.1 8.8 %collective-permute-start.16 = (bf16[32,1024]{1,0:T(8,128)(2,1)S(1)}, bf16[32,1024]{1,0:T(8,128)(2,1)S(1)}, u32[]{:S(2)}, u32[]{:S(2)}) collective-permute-start(bf16[32,1024]{1,0:T(8,128)(2,1)S(1)} %get-tuple-element.29), channel_id=1, source_target_pairs={{0,8},{2,10},{4,12},{6,14},{8,0},{10,2},{12,4},{14,6},{1,9},{3,11}... | collective-permute-start | bytes 196616 | tf_op jit(solution)/shard_map/ppermute | solution.py:316
  101.7 7.8 %collective-permute-start.17 = (bf16[32,1024]{1,0:T(8,128)(2,1)S(1)}, bf16[32,1024]{1,0:T(8,128)(2,1)S(1)}, u32[]{:S(2)}, u32[]{:S(2)}) collective-permute-start(bf16[32,1024]{1,0:T(8,128)(2,1)S(1)} %get-tuple-element.30), channel_id=1, source_target_pairs={{0,10},{2,12},{4,14},{6,0},{8,2},{10,4},{12,6},{14,8},{1,11},{3,13... | collective-permute-start | bytes 196616 | tf_op jit(solution)/shard_map/ppermute | solution.py:316
  102.2 7.4 %collective-permute-start.18 = (bf16[32,1024]{1,0:T(8,128)(2,1)S(1)}, bf16[32,1024]{1,0:T(8,128)(2,1)S(1)}, u32[]{:S(2)}, u32[]{:S(2)}) collective-permute-start(bf16[32,1024]{1,0:T(8,128)(2,1)S(1)} %get-tuple-element.31), channel_id=1, source_target_pairs={{0,12},{2,14},{4,0},{6,2},{8,4},{10,6},{12,8},{14,10},{1,13},{3,15... | collective-permute-start | bytes 196616 | tf_op jit(solution)/shard_map/ppermute | solution.py:316
  104.8 4.7 %collective-permute-start.19 = (bf16[32,1024]{1,0:T(8,128)(2,1)S(1)}, bf16[32,1024]{1,0:T(8,128)(2,1)S(1)}, u32[]{:S(2)}, u32[]{:S(2)}) collective-permute-start(bf16[32,1024]{1,0:T(8,128)(2,1)S(1)} %get-tuple-element.32), channel_id=1, source_target_pairs={{0,14},{2,0},{4,2},{6,4},{8,6},{10,8},{12,10},{14,12},{1,15},{3,1}... | collective-permute-start | bytes 196616 | tf_op jit(solution)/shard_map/ppermute | solution.py:316
